TPU v7x, 32 devices: a whole 2x2x4 slice. The times are simulated.
32 devices in a mesh: groups: 2 (over x), lines: 16 (over z, y, core).
Axes of the slice: x: 2, y: 2, z: 4, core: 2. Of those that a mesh axis runs over, the one named last changes fastest.
Arguments:
- raw_echo: bfloat16 [8, 2, 2048, 512], P('groups', None, 'lines'), parts along dimension 0, may hold values from -6 to 6
- range_filter: bfloat16 [2, 512, 512], replicated, may hold values from -0.1875 to 0.1875
- azimuth_phase: float32 [512, 2048], P('lines'), may hold values from -3.140625 to 3.140625
- pair_offset: int32 [4], replicated, may hold values from 1 to 3
Outputs:
- filtered: float32 [8, 2, 128, 1024], P('groups', None, None, 'lines'), parts along dimension 0
There are 2 independent parts, one for each index of `groups`. A program takes and returns all parts, laid end to end along the dimension named above; an argument that names none is the same for every part. Nothing has to cross between parts.
Inputs may be any that keep to these rules, and one draw needn't show every extreme that they name: Date d is paired with date (d + pair_offset[d]) mod 4.
All inputs are finite; a program needn't handle non-finite values.
Results may differ from a plain program's by a relative error of at most 0.0095.
Values may be sent and summed in bfloat16 or wider, within the bound.
No kernel may reach another device: no remote copies, remote signals or barrier semaphores. Data moves between devices by JAX's collectives and lax.ppermute only.
A program may use at most 192 MiB of HBM per device.

v0:
```python
import math

import jax
import jax.numpy as jnp
import numpy as np
from jax import lax
from jax.experimental import pallas as pl
from jax.experimental.pallas import tpu as pltpu
from jax.sharding import PartitionSpec as P

ML_RG = 4
ML_AZ = 2
PATCH = 32
HALF = PATCH // 2
BOX_FLOOR = 0.25
LEVEL_FLOOR = 1e-06
SUB = 8
LANES = 128
VMEM_BYTES = 48 * 1024 * 1024


def real_block(table):
    return np.block([[table.real, table.imag], [-table.imag, table.real]])


def wave(rows, cols, period, direction):
    product = np.asarray(rows)[:, None] * np.asarray(cols)[None, :] % period
    return np.exp(direction * 2j * math.pi / period * product)


def as_bf16(table):
    return jnp.asarray(np.asarray(table, np.float32), jnp.bfloat16)


def line_order(line_len):
    return np.arange(line_len).reshape(line_len // ML_AZ, ML_AZ).T.reshape(-1)


def small_dft(parts, direction):
    count = len(parts)
    if count == 1:
        return parts
    even = small_dft(parts[0::2], direction)
    odd = small_dft(parts[1::2], direction)
    low, high = [], []
    for k in range(count // 2):
        (er, ei), (vr, vi) = even[k], odd[k]
        if k == 0:
            tr, ti = vr, vi
        elif 4 * k == count:
            if direction < 0:
                tr, ti = vi, -vr
            else:
                tr, ti = -vi, vr
        elif 8 * k == count:
            s = math.sqrt(0.5)
            if direction < 0:
                tr, ti = (vr + vi) * s, (vi - vr) * s
            else:
                tr, ti = (vr - vi) * s, (vi + vr) * s
        elif 8 * k == 3 * count:
            s = math.sqrt(0.5)
            if direction < 0:
                tr, ti = (vi - vr) * s, -(vr + vi) * s
            else:
                tr, ti = -(vr + vi) * s, (vr - vi) * s
        else:
            c = math.cos(2 * math.pi * k / count)
            s = direction * math.sin(2 * math.pi * k / count)
            tr, ti = vr * c - vi * s, vr * s + vi * c
        low.append((er + tr, ei + ti))
        high.append((er - tr, ei - ti))
    return low + high


def compress_kernel(shape, raw_ref, filter_ref, out_ref, wide_ref):
    dates, targets, tiles, gates, lines = shape
    looks_rows = gates // ML_RG
    raw = [raw_ref[:, part].reshape(dates * lines, raw_ref.shape[3]) for part in (0, 1)]
    weight = [filter_ref[part] for part in (0, 1)]

    def product(w, x):
        return lax.dot_general(
            w, x, (((1,), (1,)), ((), ())), preferred_element_type=jnp.float32
        )

    real = product(weight[0], raw[0]) - product(weight[1], raw[1])
    imag = product(weight[1], raw[0]) + product(weight[0], raw[1])
    for date in range(dates):
        wide_ref[date, 0] = real[:, date * lines : (date + 1) * lines]
        wide_ref[date, 1] = imag[:, date * lines : (date + 1) * lines]
    for target in range(targets):
        for date in range(dates):
            for tile in range(tiles):
                rows = []
                for part in (0, 1):
                    first, count = tile * SUB, min(looks_rows, SUB)
                    for at in range(first, first + SUB, count):
                        gate = target * gates + at // looks_rows + ML_RG * (at % looks_rows)
                        rows.append(wide_ref[date, part, pl.ds(gate, count, stride=ML_RG), :])
                out_ref[target, date, tile] = jnp.concatenate(rows, axis=0).astype(jnp.bfloat16)


def compress(raw_echo, range_filter, targets):
    dates, _, lines, gates_in = raw_echo.shape
    gates_out = range_filter.shape[1]
    gates = gates_out // targets
    tiles = gates // SUB
    step = 2 if dates % 2 == 0 else 1
    shape = (step, targets, tiles, gates, lines)
    return pl.pallas_call(
        lambda *refs: compress_kernel(shape, *refs),
        grid=(dates // step,),
        out_shape=jax.ShapeDtypeStruct((targets, dates, tiles, 2 * SUB, lines), jnp.bfloat16),
        in_specs=[
            pl.BlockSpec((step, 2, lines, gates_in), lambda i: (i, 0, 0, 0)),
            pl.BlockSpec(range_filter.shape, lambda i: (0, 0, 0)),
        ],
        out_specs=pl.BlockSpec((targets, step, tiles, 2 * SUB, lines), lambda i: (0, i, 0, 0, 0)),
        scratch_shapes=[pltpu.VMEM((step, 2, gates_out, lines), jnp.float32)],
        compiler_params=pltpu.CompilerParams(vmem_limit_bytes=VMEM_BYTES),
        name="compress",
    )(raw_echo, range_filter)


def focus_kernel(
    shape, offset_ref, data_ref, phase_ref, turn_ref, fwd_ref, back_ref, out_ref, image_ref, look_ref
):
    dates, blocks, tiles, gates, lines = shape
    looks_rows = gates // ML_RG
    look_lines = lines // ML_AZ
    for date in range(dates):
        for tile in range(tiles):
            parts = []
            for a in range(blocks):
                both = data_ref[a, date, tile].astype(jnp.float32)
                parts.append((both[:SUB], both[SUB:]))
            parts = small_dft(parts, -1)
            turned = []
            for a, (re, im) in enumerate(parts):
                tr, ti = turn_ref[0, a : a + 1], turn_ref[1, a : a + 1]
                turned.append((re * tr - im * ti, re * ti + im * tr))
            rows = jnp.concatenate(
                [jnp.concatenate([re, im], axis=1) for re, im in turned], axis=0
            ).astype(jnp.bfloat16)
            spectrum = jnp.dot(rows, fwd_ref[...], preferred_element_type=jnp.float32)
            re, im = spectrum[:, :lines], spectrum[:, lines:]
            pr, pi = phase_ref[0, tile], phase_ref[1, tile]
            rows = jnp.concatenate([re * pr - im * pi, re * pi + im * pr], axis=1).astype(
                jnp.bfloat16
            )
            back = jnp.dot(rows, back_ref[...], preferred_element_type=jnp.float32)
            parts = []
            for a in range(blocks):
                re = back[a * SUB : (a + 1) * SUB, :lines]
                im = back[a * SUB : (a + 1) * SUB, lines:]
                tr, ti = turn_ref[2, a : a + 1], turn_ref[3, a : a + 1]
                parts.append((re * tr - im * ti, re * ti + im * tr))
            parts = small_dft(parts, 1)
            for a, (re, im) in enumerate(parts):
                image_ref[date, tile, a, 0] = re
                image_ref[date, tile, a, 1] = im

    lane = lax.broadcasted_iota(jnp.int32, (SUB, lines), 1)
    first = lane < look_lines
    scale = 1.0 / (ML_RG * ML_AZ)
    for date in range(dates):
        partner = lax.rem(date + offset_ref[date], dates)
        for a in range(blocks):
            sums = {}
            for tile in range(tiles):
                cr, ci = image_ref[date, tile, a, 0], image_ref[date, tile, a, 1]
                pr, pi = image_ref[partner, tile, a, 0], image_ref[partner, tile, a, 1]
                re, im = cr * pr + ci * pi, ci * pr - cr * pi
                at = tile * SUB % looks_rows
                if at in sums:
                    re, im = re + sums[at][0], im + sums[at][1]
                sums[at] = (re, im)
            for at, (re, im) in sums.items():
                step = SUB
                while step > looks_rows:
                    step //= 2
                    re = re + pltpu.roll(re, step, 0)
                    im = im + pltpu.roll(im, step, 0)
                re = re + pltpu.roll(re, look_lines, 1)
                im = im + pltpu.roll(im, look_lines, 1)
                count = min(SUB, looks_rows)
                row = date * looks_rows + at
                look_ref[a, row : row + count, :] = (jnp.where(first, re, im) * scale)[:count]

    small = lax.broadcasted_iota(jnp.int32, (looks_rows, lines), 1) % look_lines
    from_high, from_low = small < HALF, small >= look_lines - HALF
    zero = jnp.zeros((looks_rows, lines), jnp.float32)

    def rim(a, date):
        rows = slice(date * looks_rows, (date + 1) * looks_rows)
        high = look_ref[a + 1, rows, :] if a + 1 < blocks else zero
        low = look_ref[a - 1, rows, :] if a > 0 else zero
        return jnp.where(from_high, high, low)

    for a in range(blocks):
        for date in range(0, dates, 2):
            own = rim(a, date)
            other = pltpu.roll(rim(a, date + 1), look_lines // 2, 1)
            row = (dates + date // 2) * looks_rows
            look_ref[a, row : row + looks_rows, :] = jnp.where(from_high | from_low, own, other)
    out_ref[...] = look_ref[...].astype(jnp.bfloat16)


def focus(columns, azimuth_phase, pair_offset):
    blocks, dates, tiles, _, lines = columns.shape
    gates, total = azimuth_phase.shape
    looks_rows = gates // ML_RG
    phase = azimuth_phase.reshape(looks_rows, ML_RG, lines, blocks).transpose(3, 1, 0, 2)
    phase = phase.reshape(blocks, tiles, SUB, lines).transpose(1, 0, 2, 3)
    phase = phase.reshape(tiles, blocks * SUB, lines)
    phase = jnp.stack([jnp.cos(phase), jnp.sin(phase)])
    order = line_order(lines)
    ahead = wave(np.arange(blocks), np.arange(lines), total, -1)
    behind = wave(np.arange(blocks), order, total, 1)
    turn = np.stack([ahead.real, ahead.imag, behind.real, behind.imag]).astype(np.float32)
    fwd = as_bf16(real_block(wave(np.arange(lines), np.arange(lines), lines, -1)))
    back = as_bf16(real_block(wave(np.arange(lines), order, lines, 1) / total))
    slots = dates + dates // 2
    shape = (dates, blocks, tiles, gates, lines)
    whole = pl.BlockSpec(memory_space=pltpu.VMEM)
    return pl.pallas_call(
        lambda *refs: focus_kernel(shape, *refs),
        out_shape=jax.ShapeDtypeStruct((blocks, slots * looks_rows, lines), jnp.bfloat16),
        in_specs=[pl.BlockSpec(memory_space=pltpu.SMEM)] + [whole] * 5,
        out_specs=whole,
        scratch_shapes=[
            pltpu.VMEM((dates, tiles, blocks, 2, SUB, lines), jnp.float32),
            pltpu.VMEM((blocks, slots * looks_rows, lines), jnp.float32),
        ],
        compiler_params=pltpu.CompilerParams(vmem_limit_bytes=VMEM_BYTES),
        name="focus",
    )(pair_offset, columns, phase, jnp.asarray(turn), fwd, back)


def tri_window(offset):
    inside = (offset >= 0) & (offset < PATCH)
    return np.where(inside, 1.0 - np.abs(offset - (PATCH - 1) / 2.0) / HALF, 0.0)


def patch_tables(cells, starts):
    offset = np.asarray(cells)[:, None] - np.asarray(starts)[None, :]
    inside = ((offset >= 0) & (offset < PATCH)).astype(np.float64)
    angle = 2.0 * math.pi / PATCH * (offset[:, :, None] * np.arange(PATCH) % PATCH)
    ahead = np.exp(-1j * angle) * inside[:, :, None]
    behind = np.exp(1j * angle) * tri_window(offset)[:, :, None] / PATCH
    flat = (len(cells), len(starts) * PATCH)
    return ahead.reshape(flat), behind.reshape(flat).T


def goldstein_tables(dates, gate_looks, line_looks):
    per = LANES // PATCH
    starts = np.arange(-HALF, line_looks, HALF)
    cells = np.arange(-HALF, line_looks + HALF)
    ahead, behind = patch_tables(cells, starts)
    main = slice(HALF, HALF + line_looks)
    behind = behind[:, main]
    split = per * PATCH

    def lanes_of(table, shift):
        block = np.zeros((2, line_looks, table.shape[1]), complex)
        block[0], block[1] = table[main], 1j * table[main]
        rim = np.zeros((2, line_looks, table.shape[1]), complex)
        for part, turn in enumerate((1.0, 1j)):
            rim[part, :HALF] = turn * table[HALF + line_looks :]
            rim[part, line_looks - HALF :] = turn * table[:HALF]
        flat = (2 * line_looks, table.shape[1])
        return block.reshape(flat), np.roll(rim.reshape(flat), shift, axis=0)

    def out_parts(table):
        return np.concatenate([table.real, table.imag], axis=1)

    near = [
        out_parts(np.concatenate(lanes_of(ahead[:, :split], parity * (line_looks // 2))))
        for parity in (0, 1)
    ]
    rest = ahead.shape[1] - split
    far_block = np.zeros((dates, 2 * line_looks, dates, rest), complex)
    far_rim = np.zeros((dates // 2, 2 * line_looks, dates, rest), complex)
    for date in range(dates):
        block, rim = lanes_of(ahead[:, split:], date % 2 * (line_looks // 2))
        far_block[date, :, date] = block
        far_rim[date // 2, :, date] = rim
    far = np.concatenate([far_block, far_rim]).reshape(-1, dates * rest)
    gate_starts = np.arange(-HALF, gate_looks, HALF)
    gate_ahead, gate_behind = patch_tables(np.arange(gate_looks), gate_starts)
    ahead_rows = real_block(gate_ahead).T
    behind_rows = real_block(gate_behind).T

    lines_back = []
    for date in range(dates):
        far_back = np.zeros((dates, rest, line_looks), complex)
        far_back[date] = behind[split:]
        lines_back.append(
            np.concatenate(
                [real_block(behind[:split]), real_block(far_back.reshape(-1, line_looks))]
            ).T
        )
    gap = (np.arange(PATCH)[:, None] - np.arange(PATCH)[None, :]) % PATCH
    ring = ((gap == 0) | (gap == 1) | (gap == PATCH - 1)).astype(np.float64)
    box = np.concatenate(
        [np.kron(np.eye(per), ring), np.kron(np.eye(per), np.ones((PATCH, PATCH)))], axis=1
    )
    tables = (np.stack(near), out_parts(far), ahead_rows, box, behind_rows, np.stack(lines_back))
    return [as_bf16(table) for table in tables]


def goldstein_kernel(
    shape, data_ref, near_ref, far_ref, ahead_ref, box_ref, behind_ref, back_ref, out_ref,
    half_ref, spec_ref, weighted_ref,
):
    dates, blocks, looks_rows, line_looks = shape
    slots = dates + dates // 2
    gate_looks = blocks * looks_rows
    cols = dates + 1
    dot = lambda a, b: jnp.dot(a, b, preferred_element_type=jnp.float32)
    if len(data_ref.shape) == 3 and data_ref.shape[0] == slots:
        held = [data_ref[slot] for slot in range(slots)]
    else:
        data = data_ref[...].astype(jnp.float32)
        held = [
            data[:, slot * looks_rows : (slot + 1) * looks_rows]
            .reshape(gate_looks, LANES)
            .astype(jnp.bfloat16)
            for slot in range(slots)
        ]
    for parity in (0, 1):
        rows = jnp.concatenate(
            [
                jnp.concatenate([held[date], held[dates + date // 2]], axis=1)
                for date in range(parity, dates, 2)
            ],
            axis=0,
        )
        both = dot(rows, near_ref[parity]).astype(jnp.bfloat16)
        for index, date in enumerate(range(parity, dates, 2)):
            mine = both[index * gate_looks : (index + 1) * gate_looks]
            half_ref[:gate_looks, date * LANES : (date + 1) * LANES] = mine[:, :LANES]
            half_ref[gate_looks:, date * LANES : (date + 1) * LANES] = mine[:, LANES:]
    both = dot(jnp.concatenate(held, axis=1), far_ref[...]).astype(jnp.bfloat16)
    half_ref[:gate_looks, dates * LANES :] = both[:, :LANES]
    half_ref[gate_looks:, dates * LANES :] = both[:, LANES:]

    spec_ref[...] = dot(ahead_ref[...], half_ref[...])
    bins = ahead_ref.shape[0] // 2
    for col in range(cols):
        lanes = slice(col * LANES, (col + 1) * LANES)
        re, im = spec_ref[:bins, lanes], spec_ref[bins:, lanes]
        power = (re * re + im * im).astype(jnp.bfloat16)
        sums = dot(power, box_ref[...])
        for start in range(0, bins, PATCH):
            rows = slice(start, start + PATCH)
            line = sums[rows, :LANES]
            total = jnp.sum(sums[rows, LANES:], axis=0, keepdims=True)
            smooth = line + pltpu.roll(line, 1, 0) + pltpu.roll(line, PATCH - 1, 0)
            level = total * (1.0 / (PATCH * PATCH)) + LEVEL_FLOOR
            weight = jnp.sqrt(smooth * (1.0 / (9.0 * level)) + BOX_FLOOR)
            weighted_ref[rows, lanes] = (re[rows] * weight).astype(jnp.bfloat16)
            weighted_ref[start + bins : start + bins + PATCH, lanes] = (im[rows] * weight).astype(
                jnp.bfloat16
            )
    inverse = dot(behind_ref[...], weighted_ref[...]).astype(jnp.bfloat16)
    far = [inverse[:gate_looks, dates * LANES :], inverse[gate_looks:, dates * LANES :]]
    for date in range(dates):
        lanes = slice(date * LANES, (date + 1) * LANES)
        rows = jnp.concatenate([inverse[:gate_looks, lanes], inverse[gate_looks:, lanes]] + far, axis=1)
        result = lax.dot_general(
            back_ref[date], rows, (((1,), (1,)), ((), ())), preferred_element_type=jnp.float32
        )
        out_ref[date, 0] = result[:line_looks]
        out_ref[date, 1] = result[line_looks:]


def goldstein(looks, dates, line_looks):
    blocks, rows, _ = looks.shape
    slots = dates + dates // 2
    looks_rows = rows // slots
    gate_looks = blocks * looks_rows
    if looks_rows % SUB:
        looks = looks.reshape(blocks, slots, looks_rows, LANES).transpose(1, 0, 2, 3)
        looks = looks.reshape(slots, gate_looks, LANES)
    tables = goldstein_tables(dates, gate_looks, line_looks)
    bins = tables[2].shape[0] // 2
    width = (dates + 1) * LANES
    shape = (dates, blocks, looks_rows, line_looks)
    whole = pl.BlockSpec(memory_space=pltpu.VMEM)
    filtered = pl.pallas_call(
        lambda *refs: goldstein_kernel(shape, *refs),
        out_shape=jax.ShapeDtypeStruct((dates, 2, line_looks, gate_looks), jnp.float32),
        in_specs=[whole] * 7,
        out_specs=whole,
        scratch_shapes=[
            pltpu.VMEM((2 * gate_looks, width), jnp.bfloat16),
            pltpu.VMEM((2 * bins, width), jnp.float32),
            pltpu.VMEM((2 * bins, width), jnp.bfloat16),
        ],
        compiler_params=pltpu.CompilerParams(vmem_limit_bytes=VMEM_BYTES),
        name="goldstein",
    )(looks, *tables)
    return filtered.swapaxes(2, 3)


def body(raw_echo, range_filter, azimuth_phase, pair_offset):
    dates, _, lines, _ = raw_echo.shape
    devices = lax.axis_size("lines")
    sent = compress(raw_echo, range_filter, devices)
    columns = lax.all_to_all(sent, "lines", split_axis=0, concat_axis=0, tiled=True)
    sent = focus(columns, azimuth_phase, pair_offset)
    looks = lax.all_to_all(sent, "lines", split_axis=0, concat_axis=0, tiled=True)
    return goldstein(looks, dates, lines // ML_AZ)


def solution(mesh):
    placed = (P("groups", None, "lines", None), P(), P("lines", None), P())
    return jax.shard_map(
        body,
        mesh=mesh,
        in_specs=placed,
        out_specs=P("groups", None, None, "lines"),
        check_vma=False,
    )
```

profile of v0, /device:TPU:0, one launch (start us, length us, event | category | flops | bytes accessed | tf_op | source)
XLA Modules:
  0.0 57.3 jit_solution(3459764680980021754)
XLA Ops:
  0.0 1.2 %copy-done = bf16[4,2,128,512]{3,2,1,0:T(8,128)(2,1)S(1)} copy-done((bf16[4,2,128,512]{3,2,1,0:T(8,128)(2,1)S(1)}, bf16[4,2,128,512]{3,2,1,0:T(8,128)(2,1)}, u32[]{:S(2)}) %copy-start) | copy-done | bytes 1048600
  1.2 1.2 %copy-done.1 = bf16[2,512,512]{2,1,0:T(8,128)(2,1)S(1)} copy-done((bf16[2,512,512]{2,1,0:T(8,128)(2,1)S(1)}, bf16[2,512,512]{2,1,0:T(8,128)(2,1)}, u32[]{:S(2)}) %copy-start.1) | copy-done | bytes 1048600
  2.5 2.4 %compress.1 = bf16[16,4,4,16,128]{4,3,2,1,0:T(8,128)(2,1)} custom-call(bf16[4,2,128,512]{3,2,1,0:T(8,128)(2,1)S(1)} %copy-done, bf16[2,512,512]{2,1,0:T(8,128)(2,1)S(1)} %copy-done.1), custom_call_target="tpu_custom_call" | custom-call | tf_op jit(solution)/shard_map/compress/pallas_call | solution.py:111
  4.9 7.4 %all-to-all-start = ((bf16[16,4,4,16,128]{4,3,2,1,0:T(8,128)(2,1)}), bf16[16,4,4,16,128]{4,3,2,1,0:T(8,128)(2,1)S(1)}, u32[]{:S(2)}, u32[]{:S(2)}) async-start(bf16[16,4,4,16,128]{4,3,2,1,0:T(8,128)(2,1)} %compress.1), calls=%async_computation | async-start | bytes 2097152 | tf_op jit(solution)/shard_map/all_to_all | solution.py:412
  12.2 0.0 copy-done.12
  12.3 1.6 %fusion = (f32[32,2048]{1,0:T(8,128)}, f32[32,2048]{1,0:T(8,128)S(1)}) fusion(f32[32,2048]{1,0:T(8,128)S(1)} %copy-done.12), kind=kLoop, calls=%fused_computation.1 | loop fusion | bytes 786432 | tf_op jit(solution)/shard_map/cos | solution.py:217
  13.9 1.7 %cos.20 = f32[8,4,128,16]{3,2,1,0:T(8,128)S(1)} reshape(f32[32,2048]{1,0:T(8,128)} %get-tuple-element.5) | data formatting | bytes 524288 | tf_op jit(solution)/shard_map/cos | solution.py:217
  15.5 1.3 %copy.16 = f32[4,16,8,128]{3,2,1,0:T(8,128)} copy(f32[4,16,8,128]{1,3,0,2:T(8,128)S(1)} %bitcast.5) | data formatting | bytes 524288 | tf_op jit(solution)/shard_map/cos | solution.py:217
  16.8 0.7 %sin.20 = f32[8,4,128,16]{3,2,1,0:T(8,128)S(1)} reshape(f32[32,2048]{1,0:T(8,128)S(1)} %get-tuple-element.6) | data formatting | bytes 524288 | tf_op jit(solution)/shard_map/sin | solution.py:217
  17.6 0.0 copy-start.7
  17.6 0.0 copy-start.10
  17.6 0.0 copy-start.11
  17.6 1.3 %copy.17 = f32[4,16,8,128]{3,2,1,0:T(8,128)} copy(f32[4,16,8,128]{1,3,0,2:T(8,128)S(1)} %bitcast.6) | data formatting | bytes 524288 | tf_op jit(solution)/shard_map/sin | solution.py:217
  18.9 0.0 copy-start.6
  18.9 1.2 %pad_maximum_fusion.refs_2_ = f32[2,4,128,128]{3,2,1,0:T(8,128)S(1)} fusion(f32[1,4,128,128]{3,2,1,0:T(8,128)} %bitcast.8, f32[1,4,128,128]{3,2,1,0:T(8,128)} %bitcast.7), kind=kLoop, calls=%fused_computation | loop fusion | flops 131072 | bytes 1048576 | tf_op jit(solution)/shard_map/stack | solution.py:217
  20.1 15.1 %all-to-all-done.refs_1_ = bf16[16,4,4,16,128]{4,3,2,1,0:T(8,128)(2,1)S(1)} async-done(((bf16[16,4,4,16,128]{4,3,2,1,0:T(8,128)(2,1)}), bf16[16,4,4,16,128]{4,3,2,1,0:T(8,128)(2,1)S(1)}, u32[]{:S(2)}, u32[]{:S(2)}) %all-to-all-start) | async-done | bytes 1048608 | tf_op jit(solution)/shard_map/all_to_all | solution.py:412
  35.2 0.0 copy-done.7
  35.2 0.0 copy-done.10
  35.2 0.0 copy-start.8
  35.2 0.9 %copy-done.8 = bf16[256,256]{1,0:T(8,128)(2,1)S(1)} copy-done((bf16[256,256]{1,0:T(8,128)(2,1)S(1)}, bf16[256,256]{1,0:T(8,128)(2,1)}, u32[]{:S(2)}) %copy-start.8) | copy-done | bytes 131096
  36.1 2.9 %focus.1 = bf16[16,48,128]{2,1,0:T(8,128)(2,1)S(1)} custom-call(s32[4]{0:T(128)S(1)} %copy-done.11, bf16[16,4,4,16,128]{4,3,2,1,0:T(8,128)(2,1)S(1)} %all-to-all-done.refs_1_, f32[2,4,128,128]{3,2,1,0:T(8,128)S(1)} %pad_maximum_fusion.refs_2_, f32[4,16,128]{2,1,0:T(8,128)S(1)} %copy-done.10, bf16[256,256]{1,0:T(8,128)(2,1)S(1)} %copy-done.7, ...), custom_call_target="tpu_custom_call" | custom-call | tf_op jit(solution)/shard_map/focus/pallas_call | solution.py:227
  39.0 15.7 %all_to_all.10.refs_0_ = bf16[16,48,128]{2,1,0:T(8,128)(2,1)S(1)} all-to-all(bf16[16,48,128]{2,1,0:T(8,128)(2,1)S(1)} %focus.1), channel_id=1, replica_groups=mesh['groups'=2,'lines'=16] {'lines'}, dimensions={0} | all-to-all | bytes 393216 | tf_op jit(solution)/shard_map/all_to_all | solution.py:414
  54.7 0.0 copy-done.3
  54.7 2.6 %goldstein.1 = f32[4,2,64,128]{3,2,1,0:T(8,128)} custom-call(bf16[16,48,128]{2,1,0:T(8,128)(2,1)S(1)} %all_to_all.10.refs_0_, bf16[2,256,256]{2,1,0:T(8,128)(2,1)S(1)} %copy-done.6, bf16[768,256]{1,0:T(8,128)(2,1)S(1)} %copy-done.3, bf16[576,256]{1,0:T(8,128)(2,1)S(1)} %copy-done.5, bf16[128,256]{1,0:T(8,128)(2,1)S(1)} %copy-done.9, ...), custom_call_target="tpu_custom_call" | custom-call | tf_op jit(solution)/shard_map/goldstein/pallas_call | solution.py:392
  (14 shorter events, 0.0 us)
Async XLA Ops:
  0.0 1.2 %copy-start = (bf16[4,2,128,512]{3,2,1,0:T(8,128)(2,1)S(1)}, bf16[4,2,128,512]{3,2,1,0:T(8,128)(2,1)}, u32[]{:S(2)}) copy-start(bf16[4,2,128,512]{3,2,1,0:T(8,128)(2,1)} %refs_0_.2) | copy-start | bytes 3145732
  1.2 1.2 %copy-start.1 = (bf16[2,512,512]{2,1,0:T(8,128)(2,1)S(1)}, bf16[2,512,512]{2,1,0:T(8,128)(2,1)}, u32[]{:S(2)}) copy-start(bf16[2,512,512]{2,1,0:T(8,128)(2,1)} %refs_1_.2) | copy-start | bytes 3145732
  2.5 9.8 %copy-start.12 = (f32[32,2048]{1,0:T(8,128)S(1)}, f32[32,2048]{1,0:T(8,128)}, u32[]{:S(2)}) copy-start(f32[32,2048]{1,0:T(8,128)} %param.15) | copy-start | bytes 786436
  4.9 30.3 %all-to-all-start = ((bf16[16,4,4,16,128]{4,3,2,1,0:T(8,128)(2,1)}), bf16[16,4,4,16,128]{4,3,2,1,0:T(8,128)(2,1)S(1)}, u32[]{:S(2)}, u32[]{:S(2)}) async-start(bf16[16,4,4,16,128]{4,3,2,1,0:T(8,128)(2,1)} %compress.1), calls=%async_computation | async-start | bytes 2097152 | tf_op jit(solution)/shard_map/all_to_all | solution.py:412
  17.6 17.6 %copy-start.7 = (bf16[256,256]{1,0:T(8,128)(2,1)S(1)}, bf16[256,256]{1,0:T(8,128)(2,1)}, u32[]{:S(2)}) copy-start(bf16[256,256]{1,0:T(8,128)(2,1)} %constant.18.clone.refs_4_) | copy-start | bytes 393220
  17.6 17.6 %copy-start.10 = (f32[4,16,128]{2,1,0:T(8,128)S(1)}, f32[4,16,128]{2,1,0:T(8,128)}, u32[]{:S(2)}) copy-start(f32[4,16,128]{2,1,0:T(8,128)} %constant.20.clone.refs_3_) | copy-start | bytes 98308
  17.6 17.6 %copy-start.11 = (s32[4]{0:T(128)S(1)}, s32[4]{0:T(128)}, u32[]{:S(2)}) copy-start(s32[4]{0:T(128)} %refs_0_.3) | copy-start | bytes 52
  18.9 35.8 %copy-start.2 = (bf16[4,128,512]{2,1,0:T(8,128)(2,1)S(1)}, bf16[4,128,512]{2,1,0:T(8,128)(2,1)}, u32[]{:S(2)}) copy-start(bf16[4,128,512]{2,1,0:T(8,128)(2,1)} %constant.26.clone.refs_6_) | copy-start | bytes 1572868
  18.9 35.8 %copy-start.3 = (bf16[768,256]{1,0:T(8,128)(2,1)S(1)}, bf16[768,256]{1,0:T(8,128)(2,1)}, u32[]{:S(2)}) copy-start(bf16[768,256]{1,0:T(8,128)(2,1)} %constant.22.clone.refs_2_) | copy-start | bytes 1179652
  18.9 35.8 %copy-start.4 = (bf16[256,576]{1,0:T(8,128)(2,1)S(1)}, bf16[256,576]{1,0:T(8,128)(2,1)}, u32[]{:S(2)}) copy-start(bf16[256,576]{1,0:T(8,128)(2,1)} %constant.25.clone.refs_5_) | copy-start | bytes 884740
  18.9 35.8 %copy-start.5 = (bf16[576,256]{1,0:T(8,128)(2,1)S(1)}, bf16[576,256]{1,0:T(8,128)(2,1)}, u32[]{:S(2)}) copy-start(bf16[576,256]{1,0:T(8,128)(2,1)} %constant.23.clone.refs_3_) | copy-start | bytes 884740
  18.9 35.8 %copy-start.6 = (bf16[2,256,256]{2,1,0:T(8,128)(2,1)S(1)}, bf16[2,256,256]{2,1,0:T(8,128)(2,1)}, u32[]{:S(2)}) copy-start(bf16[2,256,256]{2,1,0:T(8,128)(2,1)} %constant.21.clone.refs_1_) | copy-start | bytes 786436
  35.2 0.9 %copy-start.8 = (bf16[256,256]{1,0:T(8,128)(2,1)S(1)}, bf16[256,256]{1,0:T(8,128)(2,1)}, u32[]{:S(2)}) copy-start(bf16[256,256]{1,0:T(8,128)(2,1)} %constant.19.clone.refs_5_) | copy-start | bytes 393220
  36.1 18.6 %copy-start.9 = (bf16[128,256]{1,0:T(8,128)(2,1)S(1)}, bf16[128,256]{1,0:T(8,128)(2,1)}, u32[]{:S(2)}) copy-start(bf16[128,256]{1,0:T(8,128)(2,1)} %constant.24.clone.refs_4_) | copy-start | bytes 196612
where the time goes:
time: 57.7 us; the launch traced here: 57.3 us
  blocking collectives  15.7 us (27%)
  waiting for transfers between devices  15.1 us (26%)
  local copies, waits for them, and re-layouts  9.96 us (17%)
  Pallas kernels  7.89 us (14%)
  starting transfers between devices  7.38 us (13%)
  other arithmetic  1.19 us (2%)
    all_to_all x1, blocking collectives, body(): lax.all_to_all(sent, 'lines', split_axis=0, concat_axis=0, tiled=True)  15.7 us
    all_to_all x1, waiting for transfers between devices, body(): lax.all_to_all(sent, 'lines', split_axis=0, concat_axis=0, tiled=True)  15.1 us
    all_to_all x1, starting transfers between devices, body(): lax.all_to_all(sent, 'lines', split_axis=0, concat_axis=0, tiled=True)  7.38 us
    cos x3, local copies, waits for them, and re-layouts, focus(): phase = jnp.stack([jnp.cos(phase), jnp.sin(phase)])  4.57 us
    unnamed x26, local copies, waits for them, and re-layouts  3.4 us
    pallas_call x1, Pallas kernels, focus(): pl.pallas_call(lambda *refs: focus_kernel(shape, *refs), out_shape=jax.Sh...  2.88 us
    pallas_call x1, Pallas kernels, goldstein(): pl.pallas_call(lambda *refs: goldstein_kernel(shape, *refs), out_shape=ja...  2.6 us
    pallas_call x1, Pallas kernels, compress(): pl.pallas_call(lambda *refs: compress_kernel(shape, *refs), grid=(dates /...  2.41 us
  transfers between devices with their start and end apart: 1, of which 1 were waited for; matrix products, arithmetic and copies ran while one was open for 14% of the time, Pallas kernels for 0%

commit v1 on v0

--- a/solution.py
+++ b/solution.py
@@ -73,60 +73,88 @@
     return low + high
 
 
-def compress_kernel(shape, raw_ref, filter_ref, out_ref, wide_ref):
-    dates, targets, tiles, gates, lines = shape
+def compress_kernel(
+    shape, raw_hbm, filter_hbm, out_ref, raw_ref, filter_ref, wide_ref, raw_sems, filter_sem
+):
+    chunk, dates, step, targets, tiles, gates, lines = shape
     looks_rows = gates // ML_RG
-    raw = [raw_ref[:, part].reshape(dates * lines, raw_ref.shape[3]) for part in (0, 1)]
-    weight = [filter_ref[part] for part in (0, 1)]
+    gates_in = raw_ref.shape[3]
+    copies = [
+        pltpu.make_async_copy(
+            raw_hbm.at[pl.ds(first, step)], raw_ref.at[pl.ds(first, step)], raw_sems.at[first // step]
+        )
+        for first in range(0, dates, step)
+    ]
+    filter_copy = pltpu.make_async_copy(filter_hbm.at[:, :, chunk], filter_ref, filter_sem)
+    filter_copy.start()
+    for copy in copies:
+        copy.start()
+    filter_copy.wait()
+    weight = [filter_ref[part].reshape(targets * gates, gates_in) for part in (0, 1)]
 
     def product(w, x):
         return lax.dot_general(
             w, x, (((1,), (1,)), ((), ())), preferred_element_type=jnp.float32
         )
 
-    real = product(weight[0], raw[0]) - product(weight[1], raw[1])
-    imag = product(weight[1], raw[0]) + product(weight[0], raw[1])
-    for date in range(dates):
-        wide_ref[date, 0] = real[:, date * lines : (date + 1) * lines]
-        wide_ref[date, 1] = imag[:, date * lines : (date + 1) * lines]
-    for target in range(targets):
-        for date in range(dates):
-            for tile in range(tiles):
-                rows = []
-                for part in (0, 1):
-                    first, count = tile * SUB, min(looks_rows, SUB)
-                    for at in range(first, first + SUB, count):
-                        gate = target * gates + at // looks_rows + ML_RG * (at % looks_rows)
-                        rows.append(wide_ref[date, part, pl.ds(gate, count, stride=ML_RG), :])
-                out_ref[target, date, tile] = jnp.concatenate(rows, axis=0).astype(jnp.bfloat16)
-
-
-def compress(raw_echo, range_filter, targets):
+    for first in range(0, dates, step):
+        copies[first // step].wait()
+        raw = [
+            raw_ref[first : first + step, part].reshape(step * lines, gates_in) for part in (0, 1)
+        ]
+        real = product(weight[0], raw[0]) - product(weight[1], raw[1])
+        imag = product(weight[1], raw[0]) + product(weight[0], raw[1])
+        for at in range(step):
+            wide_ref[first + at, 0] = real[:, at * lines : (at + 1) * lines]
+            wide_ref[first + at, 1] = imag[:, at * lines : (at + 1) * lines]
+        for target in range(targets):
+            for date in range(first, first + step):
+                for tile in range(tiles):
+                    rows = []
+                    for part in (0, 1):
+                        begin, count = tile * SUB, min(looks_rows, SUB)
+                        for at in range(begin, begin + SUB, count):
+                            gate = target * gates + at // looks_rows + ML_RG * (at % looks_rows)
+                            rows.append(wide_ref[date, part, pl.ds(gate, count, stride=ML_RG), :])
+                    out_ref[target, date, tile] = jnp.concatenate(rows, axis=0).astype(
+                        jnp.bfloat16
+                    )
+
+
+def compress(raw_echo, filter_chunks, chunk):
     dates, _, lines, gates_in = raw_echo.shape
-    gates_out = range_filter.shape[1]
-    gates = gates_out // targets
+    _, targets, _, gates, _ = filter_chunks.shape
     tiles = gates // SUB
     step = 2 if dates % 2 == 0 else 1
-    shape = (step, targets, tiles, gates, lines)
+    shape = (chunk, dates, step, targets, tiles, gates, lines)
+    hbm = pl.BlockSpec(memory_space=pltpu.HBM)
     return pl.pallas_call(
         lambda *refs: compress_kernel(shape, *refs),
-        grid=(dates // step,),
         out_shape=jax.ShapeDtypeStruct((targets, dates, tiles, 2 * SUB, lines), jnp.bfloat16),
-        in_specs=[
-            pl.BlockSpec((step, 2, lines, gates_in), lambda i: (i, 0, 0, 0)),
-            pl.BlockSpec(range_filter.shape, lambda i: (0, 0, 0)),
+        in_specs=[hbm, hbm],
+        out_specs=pl.BlockSpec(memory_space=pltpu.VMEM),
+        scratch_shapes=[
+            pltpu.VMEM(raw_echo.shape, jnp.bfloat16),
+            pltpu.VMEM((2, targets, gates, gates_in), jnp.bfloat16),
+            pltpu.VMEM((dates, 2, targets * gates, lines), jnp.float32),
+            pltpu.SemaphoreType.DMA((dates // step,)),
+            pltpu.SemaphoreType.DMA,
         ],
-        out_specs=pl.BlockSpec((targets, step, tiles, 2 * SUB, lines), lambda i: (0, i, 0, 0, 0)),
-        scratch_shapes=[pltpu.VMEM((step, 2, gates_out, lines), jnp.float32)],
         compiler_params=pltpu.CompilerParams(vmem_limit_bytes=VMEM_BYTES),
+        cost_estimate=pl.CostEstimate(
+            flops=8 * dates * lines * targets * gates * gates_in,
+            bytes_accessed=4 * (raw_echo.size + targets * gates * gates_in),
+            transcendentals=0,
+        ),
         name="compress",
-    )(raw_echo, range_filter)
+    )(raw_echo, filter_chunks)
 
 
 def focus_kernel(
-    shape, offset_ref, data_ref, phase_ref, turn_ref, fwd_ref, back_ref, out_ref, image_ref, look_ref
+    shape, offset_ref, data_ref, cos_ref, sin_ref, turn_ref, fwd_ref, back_ref, out_ref, image_ref,
+    look_ref,
 ):
-    dates, blocks, tiles, gates, lines = shape
+    chunk, dates, blocks, tiles, gates, lines = shape
     looks_rows = gates // ML_RG
     look_lines = lines // ML_AZ
     for date in range(dates):
@@ -145,7 +173,7 @@
             ).astype(jnp.bfloat16)
             spectrum = jnp.dot(rows, fwd_ref[...], preferred_element_type=jnp.float32)
             re, im = spectrum[:, :lines], spectrum[:, lines:]
-            pr, pi = phase_ref[0, tile], phase_ref[1, tile]
+            pr, pi = cos_ref[chunk, tile], sin_ref[chunk, tile]
             rows = jnp.concatenate([re * pr - im * pi, re * pi + im * pr], axis=1).astype(
                 jnp.bfloat16
             )
@@ -177,16 +205,16 @@
                     re, im = re + sums[at][0], im + sums[at][1]
                 sums[at] = (re, im)
             for at, (re, im) in sums.items():
+                look = jnp.where(first, re, im) + pltpu.roll(
+                    jnp.where(first, im, re), look_lines, 1
+                )
                 step = SUB
                 while step > looks_rows:
                     step //= 2
-                    re = re + pltpu.roll(re, step, 0)
-                    im = im + pltpu.roll(im, step, 0)
-                re = re + pltpu.roll(re, look_lines, 1)
-                im = im + pltpu.roll(im, look_lines, 1)
+                    look = look + pltpu.roll(look, step, 0)
                 count = min(SUB, looks_rows)
                 row = date * looks_rows + at
-                look_ref[a, row : row + count, :] = (jnp.where(first, re, im) * scale)[:count]
+                look_ref[a, row : row + count, :] = (look * scale)[:count]
 
     small = lax.broadcasted_iota(jnp.int32, (looks_rows, lines), 1) % look_lines
     from_high, from_low = small < HALF, small >= look_lines - HALF
@@ -207,35 +235,53 @@
     out_ref[...] = look_ref[...].astype(jnp.bfloat16)
 
 
-def focus(columns, azimuth_phase, pair_offset):
-    blocks, dates, tiles, _, lines = columns.shape
+def phase_tables(azimuth_phase, chunks, blocks):
     gates, total = azimuth_phase.shape
-    looks_rows = gates // ML_RG
-    phase = azimuth_phase.reshape(looks_rows, ML_RG, lines, blocks).transpose(3, 1, 0, 2)
-    phase = phase.reshape(blocks, tiles, SUB, lines).transpose(1, 0, 2, 3)
-    phase = phase.reshape(tiles, blocks * SUB, lines)
-    phase = jnp.stack([jnp.cos(phase), jnp.sin(phase)])
+    looks_rows = gates // chunks // ML_RG
+    lines = total // blocks
+    tiles = gates // chunks // SUB
+    phase = azimuth_phase.reshape(chunks, looks_rows, ML_RG, lines, blocks)
+    phase = phase.transpose(0, 2, 1, 4, 3).reshape(chunks, tiles, SUB, blocks, lines)
+    phase = phase.transpose(0, 1, 3, 2, 4).reshape(chunks, tiles, blocks * SUB, lines)
+    phase = lax.optimization_barrier(phase)
+    return jnp.cos(phase), jnp.sin(phase)
+
+
+def focus_tables(blocks, lines):
+    total = blocks * lines
     order = line_order(lines)
     ahead = wave(np.arange(blocks), np.arange(lines), total, -1)
     behind = wave(np.arange(blocks), order, total, 1)
     turn = np.stack([ahead.real, ahead.imag, behind.real, behind.imag]).astype(np.float32)
     fwd = as_bf16(real_block(wave(np.arange(lines), np.arange(lines), lines, -1)))
     back = as_bf16(real_block(wave(np.arange(lines), order, lines, 1) / total))
+    return jnp.asarray(turn), fwd, back
+
+
+def focus(columns, pair_offset, phases, tables, chunk):
+    blocks, dates, tiles, _, lines = columns.shape
+    gates = tiles * SUB
+    looks_rows = gates // ML_RG
     slots = dates + dates // 2
-    shape = (dates, blocks, tiles, gates, lines)
+    shape = (chunk, dates, blocks, tiles, gates, lines)
     whole = pl.BlockSpec(memory_space=pltpu.VMEM)
     return pl.pallas_call(
         lambda *refs: focus_kernel(shape, *refs),
         out_shape=jax.ShapeDtypeStruct((blocks, slots * looks_rows, lines), jnp.bfloat16),
-        in_specs=[pl.BlockSpec(memory_space=pltpu.SMEM)] + [whole] * 5,
+        in_specs=[pl.BlockSpec(memory_space=pltpu.SMEM)] + [whole] * 6,
         out_specs=whole,
         scratch_shapes=[
             pltpu.VMEM((dates, tiles, blocks, 2, SUB, lines), jnp.float32),
             pltpu.VMEM((blocks, slots * looks_rows, lines), jnp.float32),
         ],
         compiler_params=pltpu.CompilerParams(vmem_limit_bytes=VMEM_BYTES),
+        cost_estimate=pl.CostEstimate(
+            flops=16 * dates * gates * blocks * lines * lines,
+            bytes_accessed=4 * columns.size,
+            transcendentals=0,
+        ),
         name="focus",
-    )(pair_offset, columns, phase, jnp.asarray(turn), fwd, back)
+    )(pair_offset, columns, *phases, *tables)
 
 
 def tri_window(offset):
@@ -253,7 +299,7 @@
     return ahead.reshape(flat), behind.reshape(flat).T
 
 
-def goldstein_tables(dates, gate_looks, line_looks):
+def goldstein_tables(dates, gate_order, line_looks):
     per = LANES // PATCH
     starts = np.arange(-HALF, line_looks, HALF)
     cells = np.arange(-HALF, line_looks + HALF)
@@ -287,9 +333,9 @@
         far_block[date, :, date] = block
         far_rim[date // 2, :, date] = rim
     far = np.concatenate([far_block, far_rim]).reshape(-1, dates * rest)
-    gate_starts = np.arange(-HALF, gate_looks, HALF)
-    gate_ahead, gate_behind = patch_tables(np.arange(gate_looks), gate_starts)
-    ahead_rows = real_block(gate_ahead).T
+    gate_starts = np.arange(-HALF, len(gate_order), HALF)
+    gate_ahead, gate_behind = patch_tables(np.arange(len(gate_order)), gate_starts)
+    ahead_rows = real_block(gate_ahead[gate_order]).T
     behind_rows = real_block(gate_behind).T
 
     lines_back = []
@@ -310,25 +356,38 @@
     return [as_bf16(table) for table in tables]
 
 
-def goldstein_kernel(
-    shape, data_ref, near_ref, far_ref, ahead_ref, box_ref, behind_ref, back_ref, out_ref,
-    half_ref, spec_ref, weighted_ref,
-):
-    dates, blocks, looks_rows, line_looks = shape
+def slot_rows(data_ref, slots, looks_rows):
+    blocks = data_ref.shape[0]
+    data = data_ref[...].astype(jnp.float32)
+    if looks_rows % SUB == 0:
+        return [
+            data[:, slot * looks_rows : (slot + 1) * looks_rows].reshape(-1, LANES)
+            for slot in range(slots)
+        ]
+    top = lax.broadcasted_iota(jnp.int32, (SUB, LANES), 0) < looks_rows
+    held = [[] for _ in range(slots)]
+    for block in range(0, blocks, 2):
+        for slot in range(0, slots, 2):
+            rows = slice(slot * looks_rows, (slot + 2) * looks_rows)
+            one, two = data[block, rows], data[block + 1, rows]
+            held[slot].append(jnp.where(top, one, pltpu.roll(two, looks_rows, 0)))
+            held[slot + 1].append(jnp.where(top, pltpu.roll(one, looks_rows, 0), two))
+    return [jnp.concatenate(rows, axis=0) for rows in held]
+
+
+def goldstein_kernel(shape, *refs):
+    dates, chunks, looks_rows, gate_looks, line_looks = shape
+    data_refs, refs = refs[:chunks], refs[chunks:]
+    near_ref, far_ref, ahead_ref, box_ref, behind_ref, back_ref, out_ref = refs[:7]
+    half_ref, spec_ref, weighted_ref = refs[7:]
     slots = dates + dates // 2
-    gate_looks = blocks * looks_rows
     cols = dates + 1
     dot = lambda a, b: jnp.dot(a, b, preferred_element_type=jnp.float32)
-    if len(data_ref.shape) == 3 and data_ref.shape[0] == slots:
-        held = [data_ref[slot] for slot in range(slots)]
+    if data_refs[0].shape[0] == slots:
+        held = [data_refs[0][slot] for slot in range(slots)]
     else:
-        data = data_ref[...].astype(jnp.float32)
-        held = [
-            data[:, slot * looks_rows : (slot + 1) * looks_rows]
-            .reshape(gate_looks, LANES)
-            .astype(jnp.bfloat16)
-            for slot in range(slots)
-        ]
+        held = zip(*[slot_rows(ref, slots, looks_rows) for ref in data_refs])
+        held = [jnp.concatenate(rows, axis=0).astype(jnp.bfloat16) for rows in held]
     for parity in (0, 1):
         rows = jnp.concatenate(
             [
@@ -377,22 +436,29 @@
 
 
 def goldstein(looks, dates, line_looks):
-    blocks, rows, _ = looks.shape
+    chunks = len(looks)
+    blocks, rows, _ = looks[0].shape
     slots = dates + dates // 2
     looks_rows = rows // slots
-    gate_looks = blocks * looks_rows
-    if looks_rows % SUB:
-        looks = looks.reshape(blocks, slots, looks_rows, LANES).transpose(1, 0, 2, 3)
-        looks = looks.reshape(slots, gate_looks, LANES)
-    tables = goldstein_tables(dates, gate_looks, line_looks)
+    gate_looks = chunks * blocks * looks_rows
+    order = np.arange(gate_looks).reshape(blocks, chunks, looks_rows).swapaxes(0, 1).reshape(-1)
+    if looks_rows % SUB and 2 * looks_rows != SUB:
+        looks = [
+            each.reshape(blocks, slots, looks_rows, LANES)
+            .swapaxes(0, 1)
+            .reshape(slots, blocks * looks_rows, LANES)
+            for each in looks
+        ]
+        looks = [jnp.concatenate(looks, axis=1)]
+    tables = goldstein_tables(dates, order, line_looks)
     bins = tables[2].shape[0] // 2
     width = (dates + 1) * LANES
-    shape = (dates, blocks, looks_rows, line_looks)
+    shape = (dates, len(looks), looks_rows, gate_looks, line_looks)
     whole = pl.BlockSpec(memory_space=pltpu.VMEM)
     filtered = pl.pallas_call(
         lambda *refs: goldstein_kernel(shape, *refs),
         out_shape=jax.ShapeDtypeStruct((dates, 2, line_looks, gate_looks), jnp.float32),
-        in_specs=[whole] * 7,
+        in_specs=[whole] * (len(looks) + len(tables)),
         out_specs=whole,
         scratch_shapes=[
             pltpu.VMEM((2 * gate_looks, width), jnp.bfloat16),
@@ -401,17 +467,27 @@
         ],
         compiler_params=pltpu.CompilerParams(vmem_limit_bytes=VMEM_BYTES),
         name="goldstein",
-    )(looks, *tables)
+    )(*looks, *tables)
     return filtered.swapaxes(2, 3)
 
 
 def body(raw_echo, range_filter, azimuth_phase, pair_offset):
-    dates, _, lines, _ = raw_echo.shape
+    dates, _, lines, gates_in = raw_echo.shape
     devices = lax.axis_size("lines")
-    sent = compress(raw_echo, range_filter, devices)
-    columns = lax.all_to_all(sent, "lines", split_axis=0, concat_axis=0, tiled=True)
-    sent = focus(columns, azimuth_phase, pair_offset)
-    looks = lax.all_to_all(sent, "lines", split_axis=0, concat_axis=0, tiled=True)
+    gates = azimuth_phase.shape[0]
+    chunks = 2 if gates % (4 * SUB) == 0 else 1
+    filter_chunks = range_filter.reshape(2, devices, chunks, gates // chunks, gates_in)
+    phases = phase_tables(azimuth_phase, chunks, devices)
+    tables = focus_tables(devices, lines)
+
+    def exchange(blocks):
+        return lax.all_to_all(blocks, "lines", split_axis=0, concat_axis=0, tiled=True)
+
+    columns = [exchange(compress(raw_echo, filter_chunks, chunk)) for chunk in range(chunks)]
+    looks = [
+        exchange(focus(columns[chunk], pair_offset, phases, tables, chunk))
+        for chunk in range(chunks)
+    ]
     return goldstein(looks, dates, lines // ML_AZ)
 
 

time: 57.7 us -> 71.6 us (1.24)
  waiting for transfers between devices: 15.1 us -> 25 us
  starting transfers between devices: 7.38 us -> 15.6 us
  blocking collectives: 15.7 us -> 9.98 us
  Pallas kernels: 7.89 us -> 10.8 us
  other arithmetic: 1.19 us -> 0 us
    all_to_all x1 -> x3, waiting for transfers between devices: 15.1 us -> 25 us  [exchange(): lax.all_to_all(blocks, 'lines', split_axis=0, concat_axis=0, tiled=True)]
    all_to_all x1 -> x3, starting transfers between devices: 7.38 us -> 15.6 us  [exchange(): lax.all_to_all(blocks, 'lines', split_axis=0, concat_axis=0, tiled=True)]
    all_to_all x1, blocking collectives: 15.7 us -> 9.98 us  [exchange(): lax.all_to_all(blocks, 'lines', split_axis=0, concat_axis=0, tiled=True)]
    cos x3 -> x0, local copies, waits for them, and re-layouts: 4.57 us -> none  [focus(): phase = jnp.stack([jnp.cos(phase), jnp.sin(phase)])]
    transpose x0 -> x2, local copies, waits for them, and re-layouts: none -> 2.31 us  [the longest x1 1.28 us: phase_tables(): phase.transpose(0, 2, 1, 4, 3).reshape(chunks, tiles, SUB, blocks, lines)]
    pallas_call x1 -> x2, Pallas kernels: 2.41 us -> 4.08 us  [compress(): pl.pallas_call(lambda *refs: compress_kernel(shape, *refs), out_shape=jax...]
    reshape x0 -> x1, local copies, waits for them, and re-layouts: none -> 1.66 us  [phase_tables(): phase = azimuth_phase.reshape(chunks, looks_rows, ML_RG, lines, blocks)]
    pallas_call x1 -> x2, Pallas kernels: 2.88 us -> 4.13 us  [focus(): pl.pallas_call(lambda *refs: focus_kernel(shape, *refs), out_shape=jax.Sh...]
  transfers between devices with their start and end apart: 1 -> 3, of which waited for: 1 -> 3; matrix products, arithmetic and copies ran while one was open for 14% -> 7% of each run, Pallas kernels for 0% -> 9%
where the time goes in v1:
time: 71.6 us; the launch traced here: 71 us
  waiting for transfers between devices  25 us (35%)
  starting transfers between devices  15.6 us (22%)
  Pallas kernels  10.8 us (15%)
  blocking collectives  9.98 us (14%)
  local copies, waits for them, and re-layouts  9.36 us (13%)
    all_to_all x3, waiting for transfers between devices, exchange(): lax.all_to_all(blocks, 'lines', split_axis=0, concat_axis=0, tiled=True)  25 us
    all_to_all x3, starting transfers between devices, exchange(): lax.all_to_all(blocks, 'lines', split_axis=0, concat_axis=0, tiled=True)  15.6 us
    all_to_all x1, blocking collectives, exchange(): lax.all_to_all(blocks, 'lines', split_axis=0, concat_axis=0, tiled=True)  9.98 us
    unnamed x28, local copies, waits for them, and re-layouts  4.42 us
    pallas_call x2, Pallas kernels, focus(): pl.pallas_call(lambda *refs: focus_kernel(shape, *refs), out_shape=jax.Sh...  4.13 us
    pallas_call x2, Pallas kernels, compress(): pl.pallas_call(lambda *refs: compress_kernel(shape, *refs), out_shape=jax...  4.08 us
    pallas_call x1, Pallas kernels, goldstein(): pl.pallas_call(lambda *refs: goldstein_kernel(shape, *refs), out_shape=ja...  2.63 us
    reshape x1, local copies, waits for them, and re-layouts, phase_tables(): phase = azimuth_phase.reshape(chunks, looks_rows, ML_RG, lines, blocks)  1.66 us
  transfers between devices with their start and end apart: 3, of which 3 were waited for; matrix products, arithmetic and copies ran while one was open for 7% of the time, Pallas kernels for 9%

profile of v1, /device:TPU:0, one launch (start us, length us, event | category | flops | bytes accessed | tf_op | source)
XLA Modules:
  0.0 71.0 jit_solution(6415934679823871770)
XLA Ops:
  0.0 1.2 %copy-done = bf16[4,2,128,512]{3,2,1,0:T(8,128)(2,1)S(1)} copy-done((bf16[4,2,128,512]{3,2,1,0:T(8,128)(2,1)S(1)}, bf16[4,2,128,512]{3,2,1,0:T(8,128)(2,1)}, u32[]{:S(2)}) %copy-start) | copy-done | bytes 1048600
  1.2 1.2 %copy-done.2 = bf16[2,512,512]{2,1,0:T(8,128)(2,1)S(1)} copy-done((bf16[2,512,512]{2,1,0:T(8,128)(2,1)S(1)}, bf16[2,512,512]{2,1,0:T(8,128)(2,1)}, u32[]{:S(2)}) %copy-start.2) | copy-done | bytes 1048600
  2.5 2.0 %compress.3 = bf16[16,4,2,16,128]{4,3,2,1,0:T(8,128)(2,1)} custom-call(bf16[4,2,128,512]{3,2,1,0:T(8,128)(2,1)S(1)} %copy-done, bf16[2,16,2,16,512]{4,3,2,1,0:T(8,128)(2,1)S(1)} %bitcast.9), custom_call_target="tpu_custom_call" | custom-call | flops 536870912 | bytes 2621440 | tf_op jit(solution)/shard_map/compress/pallas_call | solution.py:131
  4.5 7.4 %all-to-all-start.2 = ((bf16[16,4,2,16,128]{4,3,2,1,0:T(8,128)(2,1)}), bf16[16,4,2,16,128]{4,3,2,1,0:T(8,128)(2,1)S(1)}, u32[]{:S(2)}, u32[]{:S(2)}) async-start(bf16[16,4,2,16,128]{4,3,2,1,0:T(8,128)(2,1)} %compress.3), calls=%async_computation.2 | async-start | bytes 1048576 | tf_op jit(solution)/shard_map/all_to_all | solution.py:484
  11.9 2.0 %compress.2 = bf16[16,4,2,16,128]{4,3,2,1,0:T(8,128)(2,1)} custom-call(bf16[4,2,128,512]{3,2,1,0:T(8,128)(2,1)S(1)} %copy-done.1, bf16[2,16,2,16,512]{4,3,2,1,0:T(8,128)(2,1)S(1)} %bitcast.10), custom_call_target="tpu_custom_call" | custom-call | flops 536870912 | bytes 2621440 | tf_op jit(solution)/shard_map/compress/pallas_call | solution.py:131
  14.0 12.4 %all-to-all-done.2.refs_1_ = bf16[16,4,2,16,128]{4,3,2,1,0:T(8,128)(2,1)S(1)} async-done(((bf16[16,4,2,16,128]{4,3,2,1,0:T(8,128)(2,1)}), bf16[16,4,2,16,128]{4,3,2,1,0:T(8,128)(2,1)S(1)}, u32[]{:S(2)}, u32[]{:S(2)}) %all-to-all-start.2) | async-done | bytes 524320 | tf_op jit(solution)/shard_map/all_to_all | solution.py:484
  26.4 4.1 %all-to-all-start = ((bf16[16,4,2,16,128]{4,3,2,1,0:T(8,128)(2,1)}), bf16[16,4,2,16,128]{4,3,2,1,0:T(8,128)(2,1)S(1)}, u32[]{:S(2)}, u32[]{:S(2)}) async-start(bf16[16,4,2,16,128]{4,3,2,1,0:T(8,128)(2,1)} %compress.2), calls=%async_computation | async-start | bytes 1048576 | tf_op jit(solution)/shard_map/all_to_all | solution.py:484
  30.5 1.7 %reshape.13 = f32[2,4,4,128,16]{4,3,2,1,0:T(8,128)S(1)} reshape(f32[32,2048]{1,0:T(8,128)} %param.15) | data formatting | bytes 524288 | tf_op jit(solution)/shard_map/reshape | solution.py:243
  32.2 0.0 copy-start.5
  32.2 0.0 copy-start.6
  32.2 0.0 copy-start.11
  32.2 1.3 %copy.14 = f32[2,4,4,16,128]{4,3,2,1,0:T(8,128)} copy(f32[2,4,4,16,128]{3,4,1,2,0:T(8,128)S(1)} %bitcast.11) | data formatting | bytes 524288 | tf_op jit(solution)/shard_map/transpose | solution.py:244
  33.5 1.0 %copy.17 = f32[2,2,16,8,128]{4,3,2,1,0:T(8,128)S(1)} copy(f32[2,2,16,8,128]{4,2,3,1,0:T(8,128)} %bitcast.13) | data formatting | bytes 524288 | tf_op jit(solution)/shard_map/transpose | solution.py:245
  34.5 0.0 copy-start.4
  34.6 1.0 %fusion = (f32[2,2,128,128]{3,2,1,0:T(8,128)S(1)}, f32[2,2,128,128]{3,2,1,0:T(8,128)S(1)}) fusion(f32[2,2,128,128]{3,2,1,0:T(8,128)S(1)} %bitcast.12), kind=kLoop, calls=%fused_computation.1 | loop fusion | bytes 786432 | tf_op jit(solution)/shard_map/sin | solution.py:247
  35.6 2.4 %focus.3 = bf16[16,24,128]{2,1,0:T(8,128)(2,1)} custom-call(s32[4]{0:T(128)S(1)} %copy-done.13, bf16[16,4,2,16,128]{4,3,2,1,0:T(8,128)(2,1)S(1)} %all-to-all-done.2.refs_1_, f32[2,2,128,128]{3,2,1,0:T(8,128)S(1)} %get-tuple-element.6.refs_2_, f32[2,2,128,128]{3,2,1,0:T(8,128)S(1)} %get-tuple-element.5.refs_3_, f32[4,16,128]{2,1,0:T(8,128)S(1)} %copy-done.11, ...), custom_call_target="tpu_custom_call" | custom-call | flops 268435456 | bytes 1048576 | tf_op jit(solution)/shard_map/focus/pallas_call | solution.py:268
  38.0 7.0 %all-to-all-done.refs_1_ = bf16[16,4,2,16,128]{4,3,2,1,0:T(8,128)(2,1)S(1)} async-done(((bf16[16,4,2,16,128]{4,3,2,1,0:T(8,128)(2,1)}), bf16[16,4,2,16,128]{4,3,2,1,0:T(8,128)(2,1)S(1)}, u32[]{:S(2)}, u32[]{:S(2)}) %all-to-all-start) | async-done | bytes 524320 | tf_op jit(solution)/shard_map/all_to_all | solution.py:484
  45.0 4.1 %all-to-all-start.3 = ((bf16[16,24,128]{2,1,0:T(8,128)(2,1)}), bf16[16,24,128]{2,1,0:T(8,128)(2,1)S(1)}, u32[]{:S(2)}, u32[]{:S(2)}) async-start(bf16[16,24,128]{2,1,0:T(8,128)(2,1)} %focus.3), calls=%async_computation.3 | async-start | bytes 196608 | tf_op jit(solution)/shard_map/all_to_all | solution.py:484
  49.1 1.7 %focus.2 = bf16[16,24,128]{2,1,0:T(8,128)(2,1)S(1)} custom-call(s32[4]{0:T(128)S(1)} %copy-done.13, bf16[16,4,2,16,128]{4,3,2,1,0:T(8,128)(2,1)S(1)} %all-to-all-done.refs_1_, f32[2,2,128,128]{3,2,1,0:T(8,128)S(1)} %get-tuple-element.6.refs_2_, f32[2,2,128,128]{3,2,1,0:T(8,128)S(1)} %get-tuple-element.5.refs_3_, f32[4,16,128]{2,1,0:T(8,128)S(1)} %copy-done.11, ...), custom_call_target="tpu_custom_call" | custom-call | flops 268435456 | bytes 1048576 | tf_op jit(solution)/shard_map/focus/pallas_call | solution.py:268
  50.8 5.7 %all-to-all-done.3.refs_1_ = bf16[16,24,128]{2,1,0:T(8,128)(2,1)S(1)} async-done(((bf16[16,24,128]{2,1,0:T(8,128)(2,1)}), bf16[16,24,128]{2,1,0:T(8,128)(2,1)S(1)}, u32[]{:S(2)}, u32[]{:S(2)}) %all-to-all-start.3) | async-done | bytes 98336 | tf_op jit(solution)/shard_map/all_to_all | solution.py:484
  56.5 10.0 %all_to_all.20.refs_0_ = bf16[16,24,128]{2,1,0:T(8,128)(2,1)S(1)} all-to-all(bf16[16,24,128]{2,1,0:T(8,128)(2,1)S(1)} %focus.2), channel_id=1, replica_groups=mesh['groups'=2,'lines'=16] {'lines'}, dimensions={0} | all-to-all | bytes 196608 | tf_op jit(solution)/shard_map/all_to_all | solution.py:484
  66.5 1.0 %copy-done.9 = bf16[576,256]{1,0:T(8,128)(2,1)S(1)} copy-done((bf16[576,256]{1,0:T(8,128)(2,1)S(1)}, bf16[576,256]{1,0:T(8,128)(2,1)}, u32[]{:S(2)}) %copy-start.9) | copy-done | bytes 294936
  67.4 0.9 %copy-done.10 = bf16[2,256,256]{2,1,0:T(8,128)(2,1)S(1)} copy-done((bf16[2,256,256]{2,1,0:T(8,128)(2,1)S(1)}, bf16[2,256,256]{2,1,0:T(8,128)(2,1)}, u32[]{:S(2)}) %copy-start.10) | copy-done | bytes 262168
  68.4 2.6 %goldstein.1 = f32[4,2,64,128]{3,2,1,0:T(8,128)} custom-call(bf16[16,24,128]{2,1,0:T(8,128)(2,1)S(1)} %all_to_all.20.refs_0_, bf16[16,24,128]{2,1,0:T(8,128)(2,1)S(1)} %all-to-all-done.3.refs_1_, bf16[2,256,256]{2,1,0:T(8,128)(2,1)S(1)} %copy-done.10, bf16[768,256]{1,0:T(8,128)(2,1)S(1)} %copy-done.7, bf16[576,256]{1,0:T(8,128)(2,1)S(1)} %copy-done.9, ...), custom_call_target="tpu_custom_call" | custom-call | tf_op jit(solution)/shard_map/goldstein/pallas_call | solution.py:458
  (20 shorter events, 0.1 us)
Async XLA Ops:
  0.0 1.2 %copy-start = (bf16[4,2,128,512]{3,2,1,0:T(8,128)(2,1)S(1)}, bf16[4,2,128,512]{3,2,1,0:T(8,128)(2,1)}, u32[]{:S(2)}) copy-start(bf16[4,2,128,512]{3,2,1,0:T(8,128)(2,1)} %refs_0_.6) | copy-start | bytes 3145732
  1.2 1.2 %copy-start.2 = (bf16[2,512,512]{2,1,0:T(8,128)(2,1)S(1)}, bf16[2,512,512]{2,1,0:T(8,128)(2,1)}, u32[]{:S(2)}) copy-start(bf16[2,512,512]{2,1,0:T(8,128)(2,1)} %param.14) | copy-start | bytes 3145732
  2.5 9.5 %copy-start.1 = (bf16[4,2,128,512]{3,2,1,0:T(8,128)(2,1)S(1)}, bf16[4,2,128,512]{3,2,1,0:T(8,128)(2,1)}, u32[]{:S(2)}) copy-start(bf16[4,2,128,512]{3,2,1,0:T(8,128)(2,1)} %refs_0_.6) | copy-start | bytes 3145732
  2.5 9.5 %copy-start.3 = (bf16[2,512,512]{2,1,0:T(8,128)(2,1)S(1)}, bf16[2,512,512]{2,1,0:T(8,128)(2,1)}, u32[]{:S(2)}) copy-start(bf16[2,512,512]{2,1,0:T(8,128)(2,1)} %param.14) | copy-start | bytes 3145732
  4.5 21.9 %all-to-all-start.2 = ((bf16[16,4,2,16,128]{4,3,2,1,0:T(8,128)(2,1)}), bf16[16,4,2,16,128]{4,3,2,1,0:T(8,128)(2,1)S(1)}, u32[]{:S(2)}, u32[]{:S(2)}) async-start(bf16[16,4,2,16,128]{4,3,2,1,0:T(8,128)(2,1)} %compress.3), calls=%async_computation.2 | async-start | bytes 1048576 | tf_op jit(solution)/shard_map/all_to_all | solution.py:484
  26.4 18.6 %all-to-all-start = ((bf16[16,4,2,16,128]{4,3,2,1,0:T(8,128)(2,1)}), bf16[16,4,2,16,128]{4,3,2,1,0:T(8,128)(2,1)S(1)}, u32[]{:S(2)}, u32[]{:S(2)}) async-start(bf16[16,4,2,16,128]{4,3,2,1,0:T(8,128)(2,1)} %compress.2), calls=%async_computation | async-start | bytes 1048576 | tf_op jit(solution)/shard_map/all_to_all | solution.py:484
  32.2 3.4 %copy-start.5 = (bf16[256,256]{1,0:T(8,128)(2,1)S(1)}, bf16[256,256]{1,0:T(8,128)(2,1)}, u32[]{:S(2)}) copy-start(bf16[256,256]{1,0:T(8,128)(2,1)} %constant.18.clone.refs_5_) | copy-start | bytes 393220
  32.2 3.4 %copy-start.6 = (bf16[256,256]{1,0:T(8,128)(2,1)S(1)}, bf16[256,256]{1,0:T(8,128)(2,1)}, u32[]{:S(2)}) copy-start(bf16[256,256]{1,0:T(8,128)(2,1)} %constant.19.clone.refs_6_) | copy-start | bytes 393220
  32.2 3.4 %copy-start.11 = (f32[4,16,128]{2,1,0:T(8,128)S(1)}, f32[4,16,128]{2,1,0:T(8,128)}, u32[]{:S(2)}) copy-start(f32[4,16,128]{2,1,0:T(8,128)} %constant.20.clone.refs_4_) | copy-start | bytes 98308
  32.2 3.4 %copy-start.13 = (s32[4]{0:T(128)S(1)}, s32[4]{0:T(128)}, u32[]{:S(2)}) copy-start(s32[4]{0:T(128)} %refs_0_.7) | copy-start | bytes 52
  34.5 31.9 %copy-start.4 = (bf16[4,128,512]{2,1,0:T(8,128)(2,1)S(1)}, bf16[4,128,512]{2,1,0:T(8,128)(2,1)}, u32[]{:S(2)}) copy-start(bf16[4,128,512]{2,1,0:T(8,128)(2,1)} %constant.26.clone.refs_7_) | copy-start | bytes 1572868
  34.5 31.9 %copy-start.7 = (bf16[768,256]{1,0:T(8,128)(2,1)S(1)}, bf16[768,256]{1,0:T(8,128)(2,1)}, u32[]{:S(2)}) copy-start(bf16[768,256]{1,0:T(8,128)(2,1)} %constant.22.clone.refs_3_) | copy-start | bytes 1179652
  34.5 31.9 %copy-start.8 = (bf16[256,576]{1,0:T(8,128)(2,1)S(1)}, bf16[256,576]{1,0:T(8,128)(2,1)}, u32[]{:S(2)}) copy-start(bf16[256,576]{1,0:T(8,128)(2,1)} %constant.25.clone.refs_6_) | copy-start | bytes 884740
  34.6 31.9 %copy-start.12 = (bf16[128,256]{1,0:T(8,128)(2,1)S(1)}, bf16[128,256]{1,0:T(8,128)(2,1)}, u32[]{:S(2)}) copy-start(bf16[128,256]{1,0:T(8,128)(2,1)} %constant.24.clone.refs_5_) | copy-start | bytes 196612
  45.0 11.5 %all-to-all-start.3 = ((bf16[16,24,128]{2,1,0:T(8,128)(2,1)}), bf16[16,24,128]{2,1,0:T(8,128)(2,1)S(1)}, u32[]{:S(2)}, u32[]{:S(2)}) async-start(bf16[16,24,128]{2,1,0:T(8,128)(2,1)} %focus.3), calls=%async_computation.3 | async-start | bytes 196608 | tf_op jit(solution)/shard_map/all_to_all | solution.py:484
  66.5 1.0 %copy-start.9 = (bf16[576,256]{1,0:T(8,128)(2,1)S(1)}, bf16[576,256]{1,0:T(8,128)(2,1)}, u32[]{:S(2)}) copy-start(bf16[576,256]{1,0:T(8,128)(2,1)} %constant.23.clone.refs_4_) | copy-start | bytes 884740
  67.4 0.9 %copy-start.10 = (bf16[2,256,256]{2,1,0:T(8,128)(2,1)S(1)}, bf16[2,256,256]{2,1,0:T(8,128)(2,1)}, u32[]{:S(2)}) copy-start(bf16[2,256,256]{2,1,0:T(8,128)(2,1)} %constant.21.clone.refs_2_) | copy-start | bytes 786436

commit v2 on v1

--- a/solution.py
+++ b/solution.py
@@ -16,7 +16,7 @@
 LEVEL_FLOOR = 1e-06
 SUB = 8
 LANES = 128
-VMEM_BYTES = 48 * 1024 * 1024
+VMEM_BYTES = 32 * 1024 * 1024
 
 
 def real_block(table):
@@ -73,24 +73,30 @@
     return low + high
 
 
-def compress_kernel(
-    shape, raw_hbm, filter_hbm, out_ref, raw_ref, filter_ref, wide_ref, raw_sems, filter_sem
-):
-    chunk, dates, step, targets, tiles, gates, lines = shape
-    looks_rows = gates // ML_RG
+def compress_kernel(shape, raw_hbm, filter_hbm, *refs):
+    region, dates, step, devices, gates, lines = shape
+    count = devices // 2
+    tiles, looks_rows = gates // SUB, gates // ML_RG
+    out_refs, refs = refs[:-5], refs[-5:]
+    raw_ref, filter_ref, wide_ref, raw_sems, filter_sem = refs
     gates_in = raw_ref.shape[3]
+    me = lax.axis_index("lines")
+    half = me // count if region == 0 else 1 - me // count
     copies = [
         pltpu.make_async_copy(
             raw_hbm.at[pl.ds(first, step)], raw_ref.at[pl.ds(first, step)], raw_sems.at[first // step]
         )
         for first in range(0, dates, step)
     ]
-    filter_copy = pltpu.make_async_copy(filter_hbm.at[:, :, chunk], filter_ref, filter_sem)
+    filter_copy = pltpu.make_async_copy(
+        filter_hbm.at[:, pl.ds(pl.multiple_of(half * count * gates, count * gates), count * gates)],
+        filter_ref,
+        filter_sem,
+    )
     filter_copy.start()
     for copy in copies:
         copy.start()
     filter_copy.wait()
-    weight = [filter_ref[part].reshape(targets * gates, gates_in) for part in (0, 1)]
 
     def product(w, x):
         return lax.dot_general(
@@ -102,59 +108,71 @@
         raw = [
             raw_ref[first : first + step, part].reshape(step * lines, gates_in) for part in (0, 1)
         ]
-        real = product(weight[0], raw[0]) - product(weight[1], raw[1])
-        imag = product(weight[1], raw[0]) + product(weight[0], raw[1])
+        real = product(filter_ref[0], raw[0]) - product(filter_ref[1], raw[1])
+        imag = product(filter_ref[1], raw[0]) + product(filter_ref[0], raw[1])
         for at in range(step):
             wide_ref[first + at, 0] = real[:, at * lines : (at + 1) * lines]
             wide_ref[first + at, 1] = imag[:, at * lines : (at + 1) * lines]
-        for target in range(targets):
+        for index in range(count):
+            base = pl.multiple_of((me % count ^ index) * gates, gates)
             for date in range(first, first + step):
                 for tile in range(tiles):
                     rows = []
                     for part in (0, 1):
-                        begin, count = tile * SUB, min(looks_rows, SUB)
-                        for at in range(begin, begin + SUB, count):
-                            gate = target * gates + at // looks_rows + ML_RG * (at % looks_rows)
-                            rows.append(wide_ref[date, part, pl.ds(gate, count, stride=ML_RG), :])
-                    out_ref[target, date, tile] = jnp.concatenate(rows, axis=0).astype(
-                        jnp.bfloat16
-                    )
-
-
-def compress(raw_echo, filter_chunks, chunk):
+                        begin, run = tile * SUB, min(looks_rows, SUB)
+                        for at in range(begin, begin + SUB, run):
+                            gate = base + at // looks_rows + ML_RG * (at % looks_rows)
+                            rows.append(wide_ref[date, part, pl.ds(gate, run, stride=ML_RG), :])
+                    tile_rows = jnp.concatenate(rows, axis=0).astype(jnp.bfloat16)
+                    if len(out_refs) == 1:
+                        out_refs[0][index, date, tile] = tile_rows
+                    else:
+                        out_refs[index][date, tile] = tile_rows
+
+
+def compress(raw_echo, range_filter, devices, region, after=None):
     dates, _, lines, gates_in = raw_echo.shape
-    _, targets, _, gates, _ = filter_chunks.shape
+    gates = range_filter.shape[1] // devices
+    count = devices // 2
     tiles = gates // SUB
     step = 2 if dates % 2 == 0 else 1
-    shape = (chunk, dates, step, targets, tiles, gates, lines)
+    shape = (region, dates, step, devices, gates, lines)
     hbm = pl.BlockSpec(memory_space=pltpu.HBM)
+    block = (dates, tiles, 2 * SUB, lines)
+    operands = [pltpu.with_memory_space_constraint(x, pltpu.HBM) for x in (raw_echo, range_filter)]
+    extra = [] if after is None else [after]
+
+    def kernel(raw_hbm, filter_hbm, *refs):
+        compress_kernel(shape, raw_hbm, filter_hbm, *refs[len(extra) :])
+
     return pl.pallas_call(
-        lambda *refs: compress_kernel(shape, *refs),
-        out_shape=jax.ShapeDtypeStruct((targets, dates, tiles, 2 * SUB, lines), jnp.bfloat16),
-        in_specs=[hbm, hbm],
-        out_specs=pl.BlockSpec(memory_space=pltpu.VMEM),
+        kernel,
+        out_shape=[jax.ShapeDtypeStruct(block, jnp.bfloat16)] * count,
+        in_specs=[hbm, hbm] + [pl.BlockSpec(memory_space=pl.ANY)] * len(extra),
+        out_specs=[pl.BlockSpec(memory_space=pltpu.VMEM)] * count,
         scratch_shapes=[
             pltpu.VMEM(raw_echo.shape, jnp.bfloat16),
-            pltpu.VMEM((2, targets, gates, gates_in), jnp.bfloat16),
-            pltpu.VMEM((dates, 2, targets * gates, lines), jnp.float32),
+            pltpu.VMEM((2, count * gates, gates_in), jnp.bfloat16),
+            pltpu.VMEM((dates, 2, count * gates, lines), jnp.float32),
             pltpu.SemaphoreType.DMA((dates // step,)),
             pltpu.SemaphoreType.DMA,
         ],
         compiler_params=pltpu.CompilerParams(vmem_limit_bytes=VMEM_BYTES),
         cost_estimate=pl.CostEstimate(
-            flops=8 * dates * lines * targets * gates * gates_in,
-            bytes_accessed=4 * (raw_echo.size + targets * gates * gates_in),
+            flops=8 * dates * lines * count * gates * gates_in,
+            bytes_accessed=4 * (raw_echo.size + count * gates * gates_in),
             transcendentals=0,
         ),
         name="compress",
-    )(raw_echo, filter_chunks)
-
-
-def focus_kernel(
-    shape, offset_ref, data_ref, cos_ref, sin_ref, turn_ref, fwd_ref, back_ref, out_ref, image_ref,
-    look_ref,
-):
-    chunk, dates, blocks, tiles, gates, lines = shape
+    )(*operands, *extra)
+
+
+def focus_kernel(shape, offset_ref, cos_ref, sin_ref, turn_ref, fwd_ref, back_ref, *refs):
+    dates, blocks, tiles, gates, lines = shape
+    block_refs, (out_ref, data_ref, image_ref, look_ref) = refs[:blocks], refs[blocks:]
+    me = lax.axis_index("lines")
+    for index, block_ref in enumerate(block_refs):
+        data_ref[me ^ index] = block_ref[...]
     looks_rows = gates // ML_RG
     look_lines = lines // ML_AZ
     for date in range(dates):
@@ -173,7 +191,7 @@
             ).astype(jnp.bfloat16)
             spectrum = jnp.dot(rows, fwd_ref[...], preferred_element_type=jnp.float32)
             re, im = spectrum[:, :lines], spectrum[:, lines:]
-            pr, pi = cos_ref[chunk, tile], sin_ref[chunk, tile]
+            pr, pi = cos_ref[tile], sin_ref[tile]
             rows = jnp.concatenate([re * pr - im * pi, re * pi + im * pr], axis=1).astype(
                 jnp.bfloat16
             )
@@ -235,14 +253,14 @@
     out_ref[...] = look_ref[...].astype(jnp.bfloat16)
 
 
-def phase_tables(azimuth_phase, chunks, blocks):
+def phase_tables(azimuth_phase, blocks):
     gates, total = azimuth_phase.shape
-    looks_rows = gates // chunks // ML_RG
+    looks_rows = gates // ML_RG
     lines = total // blocks
-    tiles = gates // chunks // SUB
-    phase = azimuth_phase.reshape(chunks, looks_rows, ML_RG, lines, blocks)
-    phase = phase.transpose(0, 2, 1, 4, 3).reshape(chunks, tiles, SUB, blocks, lines)
-    phase = phase.transpose(0, 1, 3, 2, 4).reshape(chunks, tiles, blocks * SUB, lines)
+    tiles = gates // SUB
+    phase = azimuth_phase.reshape(looks_rows, ML_RG, lines, blocks)
+    phase = phase.transpose(1, 0, 3, 2).reshape(tiles, SUB, blocks, lines)
+    phase = phase.transpose(0, 2, 1, 3).reshape(tiles, blocks * SUB, lines)
     phase = lax.optimization_barrier(phase)
     return jnp.cos(phase), jnp.sin(phase)
 
@@ -258,30 +276,32 @@
     return jnp.asarray(turn), fwd, back
 
 
-def focus(columns, pair_offset, phases, tables, chunk):
-    blocks, dates, tiles, _, lines = columns.shape
+def focus(columns, pair_offset, phases, tables):
+    blocks = len(columns)
+    dates, tiles, _, lines = columns[0].shape
     gates = tiles * SUB
     looks_rows = gates // ML_RG
     slots = dates + dates // 2
-    shape = (chunk, dates, blocks, tiles, gates, lines)
+    shape = (dates, blocks, tiles, gates, lines)
     whole = pl.BlockSpec(memory_space=pltpu.VMEM)
     return pl.pallas_call(
         lambda *refs: focus_kernel(shape, *refs),
         out_shape=jax.ShapeDtypeStruct((blocks, slots * looks_rows, lines), jnp.bfloat16),
-        in_specs=[pl.BlockSpec(memory_space=pltpu.SMEM)] + [whole] * 6,
+        in_specs=[pl.BlockSpec(memory_space=pltpu.SMEM)] + [whole] * (5 + blocks),
         out_specs=whole,
         scratch_shapes=[
+            pltpu.VMEM((blocks, dates, tiles, 2 * SUB, lines), jnp.bfloat16),
             pltpu.VMEM((dates, tiles, blocks, 2, SUB, lines), jnp.float32),
             pltpu.VMEM((blocks, slots * looks_rows, lines), jnp.float32),
         ],
         compiler_params=pltpu.CompilerParams(vmem_limit_bytes=VMEM_BYTES),
         cost_estimate=pl.CostEstimate(
             flops=16 * dates * gates * blocks * lines * lines,
-            bytes_accessed=4 * columns.size,
+            bytes_accessed=4 * blocks * columns[0].size,
             transcendentals=0,
         ),
         name="focus",
-    )(pair_offset, columns, *phases, *tables)
+    )(pair_offset, *phases, *tables, *columns)
 
 
 def tri_window(offset):
@@ -472,23 +492,21 @@
 
 
 def body(raw_echo, range_filter, azimuth_phase, pair_offset):
-    dates, _, lines, gates_in = raw_echo.shape
+    dates, _, lines, _ = raw_echo.shape
     devices = lax.axis_size("lines")
-    gates = azimuth_phase.shape[0]
-    chunks = 2 if gates % (4 * SUB) == 0 else 1
-    filter_chunks = range_filter.reshape(2, devices, chunks, gates // chunks, gates_in)
-    phases = phase_tables(azimuth_phase, chunks, devices)
+    phases = phase_tables(azimuth_phase, devices)
     tables = focus_tables(devices, lines)
-
-    def exchange(blocks):
-        return lax.all_to_all(blocks, "lines", split_axis=0, concat_axis=0, tiled=True)
-
-    columns = [exchange(compress(raw_echo, filter_chunks, chunk)) for chunk in range(chunks)]
-    looks = [
-        exchange(focus(columns[chunk], pair_offset, phases, tables, chunk))
-        for chunk in range(chunks)
-    ]
-    return goldstein(looks, dates, lines // ML_AZ)
+    far = compress(raw_echo, range_filter, devices, 1)
+    near = compress(raw_echo, range_filter, devices, 0, far[0])
+    columns = []
+    for index, block in enumerate(near + far):
+        if index:
+            pairs = [(i, i ^ index) for i in range(devices)]
+            block = lax.ppermute(block, "lines", pairs)
+        columns.append(block)
+    sent = focus(columns, pair_offset, phases, tables)
+    looks = lax.all_to_all(sent, "lines", split_axis=0, concat_axis=0, tiled=True)
+    return goldstein([looks], dates, lines // ML_AZ)
 
 
 def solution(mesh):

time: 71.6 us -> 58.8 us (0.82)
  waiting for transfers between devices: 25 us -> 5.28 us
  starting transfers between devices: 15.6 us -> 22.7 us
  blocking collectives: 9.98 us -> 14.9 us
  local copies, waits for them, and re-layouts: 9.36 us -> 5.28 us
    all_to_all x3 -> x0, waiting for transfers between devices: 25 us -> none  [exchange(): lax.all_to_all(blocks, 'lines', split_axis=0, concat_axis=0, tiled=True)]
    ppermute x0 -> x15, starting transfers between devices: none -> 22.7 us  [body(): block = lax.ppermute(block, 'lines', pairs)]
    all_to_all x3 -> x0, starting transfers between devices: 15.6 us -> none  [exchange(): lax.all_to_all(blocks, 'lines', split_axis=0, concat_axis=0, tiled=True)]
    ppermute x0 -> x15, waiting for transfers between devices: none -> 5.28 us  [body(): block = lax.ppermute(block, 'lines', pairs)]
    all_to_all x1, blocking collectives: 9.98 us -> 14.9 us  [body(): lax.all_to_all(sent, 'lines', split_axis=0, concat_axis=0, tiled=True)]
    unnamed x28 -> x22, local copies, waits for them, and re-layouts: 4.42 us -> 0.06 us
    transpose x2 -> x0, local copies, waits for them, and re-layouts: 2.31 us -> none  [the longest x1 1.28 us: phase_tables(): phase.transpose(0, 2, 1, 4, 3).reshape(chunks, tiles, SUB, blocks, lines)]
    another operation x0 -> x1, local copies, waits for them, and re-layouts: none -> 2.21 us  [phase_tables(): phase = phase.transpose(0, 2, 1, 3).reshape(tiles, blocks * SUB, lines)]
  transfers between devices with their start and end apart: 3 -> 15, of which waited for: 3 -> 2; matrix products, arithmetic and copies ran while one was open for 7% -> 9% of each run, Pallas kernels for 9% -> 0%
where the time goes in v2:
time: 58.8 us; the launch traced here: 58.5 us
  starting transfers between devices  22.7 us (39%)
  blocking collectives  14.9 us (25%)
  Pallas kernels  10.2 us (17%)
  local copies, waits for them, and re-layouts  5.28 us (9%)
  waiting for transfers between devices  5.28 us (9%)
    ppermute x15, starting transfers between devices, body(): block = lax.ppermute(block, 'lines', pairs)  22.7 us
    all_to_all x1, blocking collectives, body(): lax.all_to_all(sent, 'lines', split_axis=0, concat_axis=0, tiled=True)  14.9 us
    ppermute x15, waiting for transfers between devices, body(): block = lax.ppermute(block, 'lines', pairs)  5.28 us
    pallas_call x2, Pallas kernels, compress(): pl.pallas_call(kernel, out_shape=[jax.ShapeDtypeStruct(block, jnp.bfloat1...  4.82 us
    pallas_call x1, Pallas kernels, focus(): pl.pallas_call(lambda *refs: focus_kernel(shape, *refs), out_shape=jax.Sh...  2.74 us
    pallas_call x1, Pallas kernels, goldstein(): pl.pallas_call(lambda *refs: goldstein_kernel(shape, *refs), out_shape=ja...  2.6 us
    another operation x1, local copies, waits for them, and re-layouts, phase_tables(): phase = phase.transpose(0, 2, 1, 3).reshape(tiles, blocks * SUB, lines)  2.21 us
    reshape x1, local copies, waits for them, and re-layouts, phase_tables(): phase = azimuth_phase.reshape(looks_rows, ML_RG, lines, blocks)  2.06 us
  transfers between devices with their start and end apart: 15, of which 2 were waited for; matrix products, arithmetic and copies ran while one was open for 9% of the time, Pallas kernels for 0%

profile of v2, /device:TPU:0, one launch (start us, length us, event | category | flops | bytes accessed | tf_op | source)
XLA Modules:
  0.0 58.5 jit_solution(17744314232402257600)
XLA Ops:
  0.0 2.4 %compress.2 = (bf16[4,4,16,128]{3,2,1,0:T(8,128)(2,1)S(1)}, bf16[4,4,16,128]{3,2,1,0:T(8,128)(2,1)S(1)}, bf16[4,4,16,128]{3,2,1,0:T(8,128)(2,1)S(1)}, bf16[4,4,1...) custom-call(bf16[4,2,128,512]{3,2,1,0:T(8,128)(2,1)} %raw_hbm.3, ...), custom_call_target="tpu_custom_call" | custom-call | flops 536870912 | bytes 2621440 | tf_op jit(solution)/shard_map/compress/pallas_call | solution.py:148
  2.4 2.4 %compress.3 = (bf16[4,4,16,128]{3,2,1,0:T(8,128)(2,1)S(1)}, bf16[4,4,16,128]{3,2,1,0:T(8,128)(2,1)S(1)}, bf16[4,4,16,128]{3,2,1,0:T(8,128)(2,1)S(1)}, bf16[4,4,1...) custom-call(bf16[4,2,128,512]{3,2,1,0:T(8,128)(2,1)} %raw_hbm.3, ...), custom_call_target="tpu_custom_call" | custom-call | flops 536870912 | bytes 2621440 | tf_op jit(solution)/shard_map/compress/pallas_call | solution.py:148
  4.8 0.5 collective-permute-start
  5.4 2.6 %collective-permute-start.1 = (bf16[4,4,16,128]{3,2,1,0:T(8,128)(2,1)S(1)}, bf16[4,4,16,128]{3,2,1,0:T(8,128)(2,1)S(1)}, u32[]{:S(2)}, u32[]{:S(2)}) collective-permute-start(bf16[4,4,16,128]{3,2,1,0:T(8,128)(2,1)S(1)} %get-tuple-element.24), channel_id=1, source_target_pairs={{0,2},{1,3},{2,0},{3,1},{4,6},{5,7},{6,4},{7,5},{8,10},{9,11},{10,... | collective-permute-start | bytes 196616 | tf_op jit(solution)/shard_map/ppermute | solution.py:505
  7.9 0.1 collective-permute-start.2
  8.0 1.8 %collective-permute-start.3 = (bf16[4,4,16,128]{3,2,1,0:T(8,128)(2,1)S(1)}, bf16[4,4,16,128]{3,2,1,0:T(8,128)(2,1)S(1)}, u32[]{:S(2)}, u32[]{:S(2)}) collective-permute-start(bf16[4,4,16,128]{3,2,1,0:T(8,128)(2,1)S(1)} %get-tuple-element.26), channel_id=1, source_target_pairs={{0,4},{1,5},{2,6},{3,7},{4,0},{5,1},{6,2},{7,3},{8,12},{9,13},{10,... | collective-permute-start | bytes 196616 | tf_op jit(solution)/shard_map/ppermute | solution.py:505
  9.8 2.6 %collective-permute-start.5 = (bf16[4,4,16,128]{3,2,1,0:T(8,128)(2,1)S(1)}, bf16[4,4,16,128]{3,2,1,0:T(8,128)(2,1)S(1)}, u32[]{:S(2)}, u32[]{:S(2)}) collective-permute-start(bf16[4,4,16,128]{3,2,1,0:T(8,128)(2,1)S(1)} %get-tuple-element.28), channel_id=1, source_target_pairs={{0,6},{1,7},{2,4},{3,5},{4,2},{5,3},{6,0},{7,1},{8,14},{9,15},{10,... | collective-permute-start | bytes 196616 | tf_op jit(solution)/shard_map/ppermute | solution.py:505
  12.5 0.2 collective-permute-start.6
  12.7 2.6 %collective-permute-start.7 = (bf16[4,4,16,128]{3,2,1,0:T(8,128)(2,1)S(1)}, bf16[4,4,16,128]{3,2,1,0:T(8,128)(2,1)S(1)}, u32[]{:S(2)}, u32[]{:S(2)}) collective-permute-start(bf16[4,4,16,128]{3,2,1,0:T(8,128)(2,1)S(1)} %get-tuple-element.21.refs_0_), channel_id=1, source_target_pairs={{0,8},{1,9},{2,10},{3,11},{4,12},{5,13},{6,14},{7,15},{8,0},{9,1},... | collective-permute-start | bytes 196616 | tf_op jit(solution)/shard_map/ppermute | solution.py:505
  15.3 1.0 %collective-permute-start.8 = (bf16[4,4,16,128]{3,2,1,0:T(8,128)(2,1)S(1)}, bf16[4,4,16,128]{3,2,1,0:T(8,128)(2,1)S(1)}, u32[]{:S(2)}, u32[]{:S(2)}) collective-permute-start(bf16[4,4,16,128]{3,2,1,0:T(8,128)(2,1)S(1)} %get-tuple-element.30), channel_id=1, source_target_pairs={{0,9},{1,8},{2,11},{3,10},{4,13},{5,12},{6,15},{7,14},{8,1},{9,0},... | collective-permute-start | bytes 196616 | tf_op jit(solution)/shard_map/ppermute | solution.py:505
  16.3 2.5 %collective-permute-start.9 = (bf16[4,4,16,128]{3,2,1,0:T(8,128)(2,1)S(1)}, bf16[4,4,16,128]{3,2,1,0:T(8,128)(2,1)S(1)}, u32[]{:S(2)}, u32[]{:S(2)}) collective-permute-start(bf16[4,4,16,128]{3,2,1,0:T(8,128)(2,1)S(1)} %get-tuple-element.31), channel_id=1, source_target_pairs={{0,10},{1,11},{2,8},{3,9},{4,14},{5,15},{6,12},{7,13},{8,2},{9,3},... | collective-permute-start | bytes 196616 | tf_op jit(solution)/shard_map/ppermute | solution.py:505
  18.8 2.1 %reshape.6 = f32[8,4,128,16]{3,2,1,0:T(8,128)} reshape(f32[32,2048]{1,0:T(8,128)S(1)} %copy-done.10) | data formatting | bytes 524288 | tf_op jit(solution)/shard_map/reshape | solution.py:261
  20.9 2.2 %copy.15 = f32[4,16,8,128]{3,2,1,0:T(8,128)S(1)} copy(f32[4,16,8,128]{1,3,0,2:T(8,128)} %bitcast.3) | data formatting | bytes 524288 | tf_op jit(solution)/shard_map/transpose;transpose | solution.py:263
  23.2 0.8 %collective-permute-start.10 = (bf16[4,4,16,128]{3,2,1,0:T(8,128)(2,1)S(1)}, bf16[4,4,16,128]{3,2,1,0:T(8,128)(2,1)S(1)}, u32[]{:S(2)}, u32[]{:S(2)}) collective-permute-start(bf16[4,4,16,128]{3,2,1,0:T(8,128)(2,1)S(1)} %get-tuple-element.32), channel_id=1, source_target_pairs={{0,11},{1,10},{2,9},{3,8},{4,15},{5,14},{6,13},{7,12},{8,3},{9,2},... | collective-permute-start | bytes 196616 | tf_op jit(solution)/shard_map/ppermute | solution.py:505
  24.0 2.9 %collective-permute-start.11 = (bf16[4,4,16,128]{3,2,1,0:T(8,128)(2,1)S(1)}, bf16[4,4,16,128]{3,2,1,0:T(8,128)(2,1)S(1)}, u32[]{:S(2)}, u32[]{:S(2)}) collective-permute-start(bf16[4,4,16,128]{3,2,1,0:T(8,128)(2,1)S(1)} %get-tuple-element.33), channel_id=1, source_target_pairs={{0,12},{1,13},{2,14},{3,15},{4,8},{5,9},{6,10},{7,11},{8,4},{9,5},... | collective-permute-start | bytes 196616 | tf_op jit(solution)/shard_map/ppermute | solution.py:505
  26.9 0.9 %collective-permute-start.12 = (bf16[4,4,16,128]{3,2,1,0:T(8,128)(2,1)S(1)}, bf16[4,4,16,128]{3,2,1,0:T(8,128)(2,1)S(1)}, u32[]{:S(2)}, u32[]{:S(2)}) collective-permute-start(bf16[4,4,16,128]{3,2,1,0:T(8,128)(2,1)S(1)} %get-tuple-element.34), channel_id=1, source_target_pairs={{0,13},{1,12},{2,15},{3,14},{4,9},{5,8},{6,11},{7,10},{8,5},{9,4},... | collective-permute-start | bytes 196616 | tf_op jit(solution)/shard_map/ppermute | solution.py:505
  27.8 3.5 %collective-permute-start.13 = (bf16[4,4,16,128]{3,2,1,0:T(8,128)(2,1)S(1)}, bf16[4,4,16,128]{3,2,1,0:T(8,128)(2,1)S(1)}, u32[]{:S(2)}, u32[]{:S(2)}) collective-permute-start(bf16[4,4,16,128]{3,2,1,0:T(8,128)(2,1)S(1)} %get-tuple-element.35), channel_id=1, source_target_pairs={{0,14},{1,15},{2,12},{3,13},{4,10},{5,11},{6,8},{7,9},{8,6},{9,7},... | collective-permute-start | bytes 196616 | tf_op jit(solution)/shard_map/ppermute | solution.py:505
  31.3 0.6 %collective-permute-start.14 = (bf16[4,4,16,128]{3,2,1,0:T(8,128)(2,1)S(1)}, bf16[4,4,16,128]{3,2,1,0:T(8,128)(2,1)S(1)}, u32[]{:S(2)}, u32[]{:S(2)}) collective-permute-start(bf16[4,4,16,128]{3,2,1,0:T(8,128)(2,1)S(1)} %get-tuple-element.36), channel_id=1, source_target_pairs={{0,15},{1,14},{2,13},{3,12},{4,11},{5,10},{6,9},{7,8},{8,7},{9,6},... | collective-permute-start | bytes 196616 | tf_op jit(solution)/shard_map/ppermute | solution.py:505
  32.0 0.9 %fusion = (f32[4,128,128]{2,1,0:T(8,128)S(1)}, f32[4,128,128]{2,1,0:T(8,128)S(1)}) fusion(f32[4,128,128]{2,1,0:T(8,128)S(1)} %bitcast.4), kind=kLoop, calls=%fused_computation | loop fusion | bytes 786432 | tf_op jit(solution)/shard_map/sin | solution.py:265
  33.0 2.6 %collective-permute-done.13.refs_20_ = bf16[4,4,16,128]{3,2,1,0:T(8,128)(2,1)S(1)} collective-permute-done((bf16[4,4,16,128]{3,2,1,0:T(8,128)(2,1)S(1)}, bf16[4,4,16,128]{3,2,1,0:T(8,128)(2,1)S(1)}, u32[]{:S(2)}, u32[]{:S(2)}) %collective-permute-start.13) | collective-permute-done | bytes 65568 | tf_op jit(solution)/shard_map/ppermute | solution.py:505
  35.6 2.6 %collective-permute-done.14.refs_21_ = bf16[4,4,16,128]{3,2,1,0:T(8,128)(2,1)S(1)} collective-permute-done((bf16[4,4,16,128]{3,2,1,0:T(8,128)(2,1)S(1)}, bf16[4,4,16,128]{3,2,1,0:T(8,128)(2,1)S(1)}, u32[]{:S(2)}, u32[]{:S(2)}) %collective-permute-start.14) | collective-permute-done | bytes 65568 | tf_op jit(solution)/shard_map/ppermute | solution.py:505
  38.2 2.7 %focus.1 = bf16[16,48,128]{2,1,0:T(8,128)(2,1)S(1)} custom-call(s32[4]{0:T(128)S(1)} %copy-done.9, f32[4,128,128]{2,1,0:T(8,128)S(1)} %get-tuple-element.38.refs_1_, f32[4,128,128]{2,1,0:T(8,128)S(1)} %get-tuple-element.37.refs_2_, f32[4,16,128]{2,1,0:T(8,128)S(1)} %copy-done.8, bf16[256,256]{1,0:T(8,128)(2,1)S(1)} %copy-done.5, ...), custom_call_target="tpu_custom_call" | custom-call | flops 536870912 | bytes 2097152 | tf_op jit(solution)/shard_map/focus/pallas_call | solution.py:287
  41.0 14.9 %all_to_all.5.refs_0_ = bf16[16,48,128]{2,1,0:T(8,128)(2,1)S(1)} all-to-all(bf16[16,48,128]{2,1,0:T(8,128)(2,1)S(1)} %focus.1), channel_id=1, replica_groups=mesh['groups'=2,'lines'=16] {'lines'}, dimensions={0} | all-to-all | bytes 393216 | tf_op jit(solution)/shard_map/all_to_all | solution.py:508
  55.9 2.6 %goldstein.1 = f32[4,2,64,128]{3,2,1,0:T(8,128)} custom-call(bf16[16,48,128]{2,1,0:T(8,128)(2,1)S(1)} %all_to_all.5.refs_0_, bf16[2,256,256]{2,1,0:T(8,128)(2,1)S(1)} %copy-done.4, bf16[768,256]{1,0:T(8,128)(2,1)S(1)} %copy-done.1, bf16[576,256]{1,0:T(8,128)(2,1)S(1)} %copy-done.3, bf16[128,256]{1,0:T(8,128)(2,1)S(1)} %copy-done.7, ...), custom_call_target="tpu_custom_call" | custom-call | tf_op jit(solution)/shard_map/goldstein/pallas_call | solution.py:478
  (36 shorter events, 0.1 us)
Async XLA Ops:
  0.0 18.8 %copy-start.10 = (f32[32,2048]{1,0:T(8,128)S(1)}, f32[32,2048]{1,0:T(8,128)}, u32[]{:S(2)}) copy-start(f32[32,2048]{1,0:T(8,128)} %param.15) | copy-start | bytes 786436
  4.8 5.0 %collective-permute-start = (bf16[4,4,16,128]{3,2,1,0:T(8,128)(2,1)S(1)}, bf16[4,4,16,128]{3,2,1,0:T(8,128)(2,1)S(1)}, u32[]{:S(2)}, u32[]{:S(2)}) collective-permute-start(bf16[4,4,16,128]{3,2,1,0:T(8,128)(2,1)S(1)} %get-tuple-element.23), channel_id=1, source_target_pairs={{0,1},{1,0},{2,3},{3,2},{4,5},{5,4},{6,7},{7,6},{8,9},{9,8},{10,11... | collective-permute-start | bytes 196616 | tf_op jit(solution)/shard_map/ppermute | solution.py:505
  5.4 7.1 %collective-permute-start.1 = (bf16[4,4,16,128]{3,2,1,0:T(8,128)(2,1)S(1)}, bf16[4,4,16,128]{3,2,1,0:T(8,128)(2,1)S(1)}, u32[]{:S(2)}, u32[]{:S(2)}) collective-permute-start(bf16[4,4,16,128]{3,2,1,0:T(8,128)(2,1)S(1)} %get-tuple-element.24), channel_id=1, source_target_pairs={{0,2},{1,3},{2,0},{3,1},{4,6},{5,7},{6,4},{7,5},{8,10},{9,11},{10,... | collective-permute-start | bytes 196616 | tf_op jit(solution)/shard_map/ppermute | solution.py:505
  7.9 4.7 %collective-permute-start.2 = (bf16[4,4,16,128]{3,2,1,0:T(8,128)(2,1)S(1)}, bf16[4,4,16,128]{3,2,1,0:T(8,128)(2,1)S(1)}, u32[]{:S(2)}, u32[]{:S(2)}) collective-permute-start(bf16[4,4,16,128]{3,2,1,0:T(8,128)(2,1)S(1)} %get-tuple-element.25), channel_id=1, source_target_pairs={{0,3},{1,2},{2,1},{3,0},{4,7},{5,6},{6,5},{7,4},{8,11},{9,10},{10,... | collective-permute-start | bytes 196616 | tf_op jit(solution)/shard_map/ppermute | solution.py:505
  8.0 7.3 %collective-permute-start.3 = (bf16[4,4,16,128]{3,2,1,0:T(8,128)(2,1)S(1)}, bf16[4,4,16,128]{3,2,1,0:T(8,128)(2,1)S(1)}, u32[]{:S(2)}, u32[]{:S(2)}) collective-permute-start(bf16[4,4,16,128]{3,2,1,0:T(8,128)(2,1)S(1)} %get-tuple-element.26), channel_id=1, source_target_pairs={{0,4},{1,5},{2,6},{3,7},{4,0},{5,1},{6,2},{7,3},{8,12},{9,13},{10,... | collective-permute-start | bytes 196616 | tf_op jit(solution)/shard_map/ppermute | solution.py:505
  9.8 6.4 %collective-permute-start.4 = (bf16[4,4,16,128]{3,2,1,0:T(8,128)(2,1)S(1)}, bf16[4,4,16,128]{3,2,1,0:T(8,128)(2,1)S(1)}, u32[]{:S(2)}, u32[]{:S(2)}) collective-permute-start(bf16[4,4,16,128]{3,2,1,0:T(8,128)(2,1)S(1)} %get-tuple-element.27), channel_id=1, source_target_pairs={{0,5},{1,4},{2,7},{3,6},{4,1},{5,0},{6,3},{7,2},{8,13},{9,12},{10,... | collective-permute-start | bytes 196616 | tf_op jit(solution)/shard_map/ppermute | solution.py:505
  9.8 13.3 %collective-permute-start.5 = (bf16[4,4,16,128]{3,2,1,0:T(8,128)(2,1)S(1)}, bf16[4,4,16,128]{3,2,1,0:T(8,128)(2,1)S(1)}, u32[]{:S(2)}, u32[]{:S(2)}) collective-permute-start(bf16[4,4,16,128]{3,2,1,0:T(8,128)(2,1)S(1)} %get-tuple-element.28), channel_id=1, source_target_pairs={{0,6},{1,7},{2,4},{3,5},{4,2},{5,3},{6,0},{7,1},{8,14},{9,15},{10,... | collective-permute-start | bytes 196616 | tf_op jit(solution)/shard_map/ppermute | solution.py:505
  12.5 11.5 %collective-permute-start.6 = (bf16[4,4,16,128]{3,2,1,0:T(8,128)(2,1)S(1)}, bf16[4,4,16,128]{3,2,1,0:T(8,128)(2,1)S(1)}, u32[]{:S(2)}, u32[]{:S(2)}) collective-permute-start(bf16[4,4,16,128]{3,2,1,0:T(8,128)(2,1)S(1)} %get-tuple-element.29), channel_id=1, source_target_pairs={{0,7},{1,6},{2,5},{3,4},{4,3},{5,2},{6,1},{7,0},{8,15},{9,14},{10,... | collective-permute-start | bytes 196616 | tf_op jit(solution)/shard_map/ppermute | solution.py:505
  12.7 14.2 %collective-permute-start.7 = (bf16[4,4,16,128]{3,2,1,0:T(8,128)(2,1)S(1)}, bf16[4,4,16,128]{3,2,1,0:T(8,128)(2,1)S(1)}, u32[]{:S(2)}, u32[]{:S(2)}) collective-permute-start(bf16[4,4,16,128]{3,2,1,0:T(8,128)(2,1)S(1)} %get-tuple-element.21.refs_0_), channel_id=1, source_target_pairs={{0,8},{1,9},{2,10},{3,11},{4,12},{5,13},{6,14},{7,15},{8,0},{9,1},... | collective-permute-start | bytes 196616 | tf_op jit(solution)/shard_map/ppermute | solution.py:505
  15.3 12.6 %collective-permute-start.8 = (bf16[4,4,16,128]{3,2,1,0:T(8,128)(2,1)S(1)}, bf16[4,4,16,128]{3,2,1,0:T(8,128)(2,1)S(1)}, u32[]{:S(2)}, u32[]{:S(2)}) collective-permute-start(bf16[4,4,16,128]{3,2,1,0:T(8,128)(2,1)S(1)} %get-tuple-element.30), channel_id=1, source_target_pairs={{0,9},{1,8},{2,11},{3,10},{4,13},{5,12},{6,15},{7,14},{8,1},{9,0},... | collective-permute-start | bytes 196616 | tf_op jit(solution)/shard_map/ppermute | solution.py:505
  16.3 15.1 %collective-permute-start.9 = (bf16[4,4,16,128]{3,2,1,0:T(8,128)(2,1)S(1)}, bf16[4,4,16,128]{3,2,1,0:T(8,128)(2,1)S(1)}, u32[]{:S(2)}, u32[]{:S(2)}) collective-permute-start(bf16[4,4,16,128]{3,2,1,0:T(8,128)(2,1)S(1)} %get-tuple-element.31), channel_id=1, source_target_pairs={{0,10},{1,11},{2,8},{3,9},{4,14},{5,15},{6,12},{7,13},{8,2},{9,3},... | collective-permute-start | bytes 196616 | tf_op jit(solution)/shard_map/ppermute | solution.py:505
  20.9 17.3 %copy-start.8 = (f32[4,16,128]{2,1,0:T(8,128)S(1)}, f32[4,16,128]{2,1,0:T(8,128)}, u32[]{:S(2)}) copy-start(f32[4,16,128]{2,1,0:T(8,128)} %constant.20.clone.refs_3_) | copy-start | bytes 98308
  20.9 17.3 %copy-start.9 = (s32[4]{0:T(128)S(1)}, s32[4]{0:T(128)}, u32[]{:S(2)}) copy-start(s32[4]{0:T(128)} %refs_0_.1) | copy-start | bytes 52
  23.1 32.8 %copy-start = (bf16[4,128,512]{2,1,0:T(8,128)(2,1)S(1)}, bf16[4,128,512]{2,1,0:T(8,128)(2,1)}, u32[]{:S(2)}) copy-start(bf16[4,128,512]{2,1,0:T(8,128)(2,1)} %constant.26.clone.refs_6_) | copy-start | bytes 1572868
  23.1 32.8 %copy-start.1 = (bf16[768,256]{1,0:T(8,128)(2,1)S(1)}, bf16[768,256]{1,0:T(8,128)(2,1)}, u32[]{:S(2)}) copy-start(bf16[768,256]{1,0:T(8,128)(2,1)} %constant.22.clone.refs_2_) | copy-start | bytes 1179652
  23.1 32.8 %copy-start.2 = (bf16[256,576]{1,0:T(8,128)(2,1)S(1)}, bf16[256,576]{1,0:T(8,128)(2,1)}, u32[]{:S(2)}) copy-start(bf16[256,576]{1,0:T(8,128)(2,1)} %constant.25.clone.refs_5_) | copy-start | bytes 884740
  23.1 32.8 %copy-start.3 = (bf16[576,256]{1,0:T(8,128)(2,1)S(1)}, bf16[576,256]{1,0:T(8,128)(2,1)}, u32[]{:S(2)}) copy-start(bf16[576,256]{1,0:T(8,128)(2,1)} %constant.23.clone.refs_3_) | copy-start | bytes 884740
  23.1 32.8 %copy-start.4 = (bf16[2,256,256]{2,1,0:T(8,128)(2,1)S(1)}, bf16[2,256,256]{2,1,0:T(8,128)(2,1)}, u32[]{:S(2)}) copy-start(bf16[2,256,256]{2,1,0:T(8,128)(2,1)} %constant.21.clone.refs_1_) | copy-start | bytes 786436
  23.1 32.8 %copy-start.7 = (bf16[128,256]{1,0:T(8,128)(2,1)S(1)}, bf16[128,256]{1,0:T(8,128)(2,1)}, u32[]{:S(2)}) copy-start(bf16[128,256]{1,0:T(8,128)(2,1)} %constant.24.clone.refs_4_) | copy-start | bytes 196612
  23.2 9.8 %collective-permute-start.10 = (bf16[4,4,16,128]{3,2,1,0:T(8,128)(2,1)S(1)}, bf16[4,4,16,128]{3,2,1,0:T(8,128)(2,1)S(1)}, u32[]{:S(2)}, u32[]{:S(2)}) collective-permute-start(bf16[4,4,16,128]{3,2,1,0:T(8,128)(2,1)S(1)} %get-tuple-element.32), channel_id=1, source_target_pairs={{0,11},{1,10},{2,9},{3,8},{4,15},{5,14},{6,13},{7,12},{8,3},{9,2},... | collective-permute-start | bytes 196616 | tf_op jit(solution)/shard_map/ppermute | solution.py:505
  24.0 9.0 %collective-permute-start.11 = (bf16[4,4,16,128]{3,2,1,0:T(8,128)(2,1)S(1)}, bf16[4,4,16,128]{3,2,1,0:T(8,128)(2,1)S(1)}, u32[]{:S(2)}, u32[]{:S(2)}) collective-permute-start(bf16[4,4,16,128]{3,2,1,0:T(8,128)(2,1)S(1)} %get-tuple-element.33), channel_id=1, source_target_pairs={{0,12},{1,13},{2,14},{3,15},{4,8},{5,9},{6,10},{7,11},{8,4},{9,5},... | collective-permute-start | bytes 196616 | tf_op jit(solution)/shard_map/ppermute | solution.py:505
  26.9 6.1 %collective-permute-start.12 = (bf16[4,4,16,128]{3,2,1,0:T(8,128)(2,1)S(1)}, bf16[4,4,16,128]{3,2,1,0:T(8,128)(2,1)S(1)}, u32[]{:S(2)}, u32[]{:S(2)}) collective-permute-start(bf16[4,4,16,128]{3,2,1,0:T(8,128)(2,1)S(1)} %get-tuple-element.34), channel_id=1, source_target_pairs={{0,13},{1,12},{2,15},{3,14},{4,9},{5,8},{6,11},{7,10},{8,5},{9,4},... | collective-permute-start | bytes 196616 | tf_op jit(solution)/shard_map/ppermute | solution.py:505
  27.8 7.7 %collective-permute-start.13 = (bf16[4,4,16,128]{3,2,1,0:T(8,128)(2,1)S(1)}, bf16[4,4,16,128]{3,2,1,0:T(8,128)(2,1)S(1)}, u32[]{:S(2)}, u32[]{:S(2)}) collective-permute-start(bf16[4,4,16,128]{3,2,1,0:T(8,128)(2,1)S(1)} %get-tuple-element.35), channel_id=1, source_target_pairs={{0,14},{1,15},{2,12},{3,13},{4,10},{5,11},{6,8},{7,9},{8,6},{9,7},... | collective-permute-start | bytes 196616 | tf_op jit(solution)/shard_map/ppermute | solution.py:505
  31.3 6.8 %collective-permute-start.14 = (bf16[4,4,16,128]{3,2,1,0:T(8,128)(2,1)S(1)}, bf16[4,4,16,128]{3,2,1,0:T(8,128)(2,1)S(1)}, u32[]{:S(2)}, u32[]{:S(2)}) collective-permute-start(bf16[4,4,16,128]{3,2,1,0:T(8,128)(2,1)S(1)} %get-tuple-element.36), channel_id=1, source_target_pairs={{0,15},{1,14},{2,13},{3,12},{4,11},{5,10},{6,9},{7,8},{8,7},{9,6},... | collective-permute-start | bytes 196616 | tf_op jit(solution)/shard_map/ppermute | solution.py:505
  (2 other events, 34.7 us)

commit v3 on v2

--- a/solution.py
+++ b/solution.py
@@ -169,7 +169,8 @@
 
 def focus_kernel(shape, offset_ref, cos_ref, sin_ref, turn_ref, fwd_ref, back_ref, *refs):
     dates, blocks, tiles, gates, lines = shape
-    block_refs, (out_ref, data_ref, image_ref, look_ref) = refs[:blocks], refs[blocks:]
+    block_refs, out_refs, refs = refs[:blocks], refs[blocks : 2 * blocks], refs[2 * blocks :]
+    data_ref, image_ref, look_ref = refs
     me = lax.axis_index("lines")
     for index, block_ref in enumerate(block_refs):
         data_ref[me ^ index] = block_ref[...]
@@ -250,7 +251,8 @@
             other = pltpu.roll(rim(a, date + 1), look_lines // 2, 1)
             row = (dates + date // 2) * looks_rows
             look_ref[a, row : row + looks_rows, :] = jnp.where(from_high | from_low, own, other)
-    out_ref[...] = look_ref[...].astype(jnp.bfloat16)
+    for index, out_ref in enumerate(out_refs):
+        out_ref[...] = look_ref[me ^ index].astype(jnp.bfloat16)
 
 
 def phase_tables(azimuth_phase, blocks):
@@ -286,9 +288,9 @@
     whole = pl.BlockSpec(memory_space=pltpu.VMEM)
     return pl.pallas_call(
         lambda *refs: focus_kernel(shape, *refs),
-        out_shape=jax.ShapeDtypeStruct((blocks, slots * looks_rows, lines), jnp.bfloat16),
+        out_shape=[jax.ShapeDtypeStruct((slots * looks_rows, lines), jnp.bfloat16)] * blocks,
         in_specs=[pl.BlockSpec(memory_space=pltpu.SMEM)] + [whole] * (5 + blocks),
-        out_specs=whole,
+        out_specs=[whole] * blocks,
         scratch_shapes=[
             pltpu.VMEM((blocks, dates, tiles, 2 * SUB, lines), jnp.bfloat16),
             pltpu.VMEM((dates, tiles, blocks, 2, SUB, lines), jnp.float32),
@@ -319,7 +321,7 @@
     return ahead.reshape(flat), behind.reshape(flat).T
 
 
-def goldstein_tables(dates, gate_order, line_looks):
+def goldstein_tables(dates, gate_looks, line_looks):
     per = LANES // PATCH
     starts = np.arange(-HALF, line_looks, HALF)
     cells = np.arange(-HALF, line_looks + HALF)
@@ -353,9 +355,9 @@
         far_block[date, :, date] = block
         far_rim[date // 2, :, date] = rim
     far = np.concatenate([far_block, far_rim]).reshape(-1, dates * rest)
-    gate_starts = np.arange(-HALF, len(gate_order), HALF)
-    gate_ahead, gate_behind = patch_tables(np.arange(len(gate_order)), gate_starts)
-    ahead_rows = real_block(gate_ahead[gate_order]).T
+    gate_starts = np.arange(-HALF, gate_looks, HALF)
+    gate_ahead, gate_behind = patch_tables(np.arange(gate_looks), gate_starts)
+    ahead_rows = real_block(gate_ahead).T
     behind_rows = real_block(gate_behind).T
 
     lines_back = []
@@ -376,38 +378,22 @@
     return [as_bf16(table) for table in tables]
 
 
-def slot_rows(data_ref, slots, looks_rows):
-    blocks = data_ref.shape[0]
-    data = data_ref[...].astype(jnp.float32)
-    if looks_rows % SUB == 0:
-        return [
-            data[:, slot * looks_rows : (slot + 1) * looks_rows].reshape(-1, LANES)
-            for slot in range(slots)
-        ]
-    top = lax.broadcasted_iota(jnp.int32, (SUB, LANES), 0) < looks_rows
-    held = [[] for _ in range(slots)]
-    for block in range(0, blocks, 2):
-        for slot in range(0, slots, 2):
-            rows = slice(slot * looks_rows, (slot + 2) * looks_rows)
-            one, two = data[block, rows], data[block + 1, rows]
-            held[slot].append(jnp.where(top, one, pltpu.roll(two, looks_rows, 0)))
-            held[slot + 1].append(jnp.where(top, pltpu.roll(one, looks_rows, 0), two))
-    return [jnp.concatenate(rows, axis=0) for rows in held]
-
-
 def goldstein_kernel(shape, *refs):
-    dates, chunks, looks_rows, gate_looks, line_looks = shape
-    data_refs, refs = refs[:chunks], refs[chunks:]
+    dates, blocks, looks_rows, line_looks = shape
+    block_refs, refs = refs[:blocks], refs[blocks:]
     near_ref, far_ref, ahead_ref, box_ref, behind_ref, back_ref, out_ref = refs[:7]
-    half_ref, spec_ref, weighted_ref = refs[7:]
+    data_ref, half_ref, spec_ref, weighted_ref = refs[7:]
     slots = dates + dates // 2
+    gate_looks = blocks * looks_rows
     cols = dates + 1
     dot = lambda a, b: jnp.dot(a, b, preferred_element_type=jnp.float32)
-    if data_refs[0].shape[0] == slots:
-        held = [data_refs[0][slot] for slot in range(slots)]
-    else:
-        held = zip(*[slot_rows(ref, slots, looks_rows) for ref in data_refs])
-        held = [jnp.concatenate(rows, axis=0).astype(jnp.bfloat16) for rows in held]
+    me = lax.axis_index("lines")
+    for index, block_ref in enumerate(block_refs):
+        block = block_ref[...].astype(jnp.float32)
+        rows = pl.ds(pl.multiple_of((me ^ index) * looks_rows, looks_rows), looks_rows)
+        for slot in range(slots):
+            data_ref[slot, rows, :] = block[slot * looks_rows : (slot + 1) * looks_rows]
+    held = [data_ref[slot].astype(jnp.bfloat16) for slot in range(slots)]
     for parity in (0, 1):
         rows = jnp.concatenate(
             [
@@ -456,24 +442,14 @@
 
 
 def goldstein(looks, dates, line_looks):
-    chunks = len(looks)
-    blocks, rows, _ = looks[0].shape
+    blocks = len(looks)
     slots = dates + dates // 2
-    looks_rows = rows // slots
-    gate_looks = chunks * blocks * looks_rows
-    order = np.arange(gate_looks).reshape(blocks, chunks, looks_rows).swapaxes(0, 1).reshape(-1)
-    if looks_rows % SUB and 2 * looks_rows != SUB:
-        looks = [
-            each.reshape(blocks, slots, looks_rows, LANES)
-            .swapaxes(0, 1)
-            .reshape(slots, blocks * looks_rows, LANES)
-            for each in looks
-        ]
-        looks = [jnp.concatenate(looks, axis=1)]
-    tables = goldstein_tables(dates, order, line_looks)
+    looks_rows = looks[0].shape[0] // slots
+    gate_looks = blocks * looks_rows
+    tables = goldstein_tables(dates, gate_looks, line_looks)
     bins = tables[2].shape[0] // 2
     width = (dates + 1) * LANES
-    shape = (dates, len(looks), looks_rows, gate_looks, line_looks)
+    shape = (dates, blocks, looks_rows, line_looks)
     whole = pl.BlockSpec(memory_space=pltpu.VMEM)
     filtered = pl.pallas_call(
         lambda *refs: goldstein_kernel(shape, *refs),
@@ -481,6 +457,7 @@
         in_specs=[whole] * (len(looks) + len(tables)),
         out_specs=whole,
         scratch_shapes=[
+            pltpu.VMEM((slots, gate_looks, LANES), jnp.float32),
             pltpu.VMEM((2 * gate_looks, width), jnp.bfloat16),
             pltpu.VMEM((2 * bins, width), jnp.float32),
             pltpu.VMEM((2 * bins, width), jnp.bfloat16),
@@ -491,22 +468,26 @@
     return filtered.swapaxes(2, 3)
 
 
+def exchange(blocks, devices, first):
+    held = []
+    for index, block in enumerate(blocks, first):
+        if index:
+            block = lax.ppermute(block, "lines", [(i, i ^ index) for i in range(devices)])
+        held.append(block)
+    return held
+
+
 def body(raw_echo, range_filter, azimuth_phase, pair_offset):
     dates, _, lines, _ = raw_echo.shape
     devices = lax.axis_size("lines")
     phases = phase_tables(azimuth_phase, devices)
     tables = focus_tables(devices, lines)
     far = compress(raw_echo, range_filter, devices, 1)
+    far = exchange(far, devices, devices // 2)
     near = compress(raw_echo, range_filter, devices, 0, far[0])
-    columns = []
-    for index, block in enumerate(near + far):
-        if index:
-            pairs = [(i, i ^ index) for i in range(devices)]
-            block = lax.ppermute(block, "lines", pairs)
-        columns.append(block)
-    sent = focus(columns, pair_offset, phases, tables)
-    looks = lax.all_to_all(sent, "lines", split_axis=0, concat_axis=0, tiled=True)
-    return goldstein([looks], dates, lines // ML_AZ)
+    near = exchange(near, devices, 0)
+    looks = exchange(focus(near + far, pair_offset, phases, tables), devices, 0)
+    return goldstein(looks, dates, lines // ML_AZ)
 
 
 def solution(mesh):

time: 58.8 us -> 70.8 us (1.20)
  starting transfers between devices: 22.7 us -> 45.9 us
  blocking collectives: 14.9 us -> 0 us
  waiting for transfers between devices: 5.28 us -> 7.21 us
  local copies, waits for them, and re-layouts: 5.28 us -> 7 us
    ppermute x15 -> x30, starting transfers between devices: 22.7 us -> 45.9 us  [exchange(): lax.ppermute(block, 'lines', [(i, i ^ index) for i in range(devices)])]
    all_to_all x1 -> x0, blocking collectives: 14.9 us -> none  [body(): lax.all_to_all(sent, 'lines', split_axis=0, concat_axis=0, tiled=True)]
    ppermute x15 -> x30, waiting for transfers between devices: 5.28 us -> 7.21 us  [exchange(): lax.ppermute(block, 'lines', [(i, i ^ index) for i in range(devices)])]
    sin x1, local copies, waits for them, and re-layouts: 0.94 us -> 1.85 us  [phase_tables(): return (jnp.cos(phase), jnp.sin(phase))]
    another operation x1, local copies, waits for them, and re-layouts: 2.21 us -> 3.01 us  [phase_tables(): phase = phase.transpose(0, 2, 1, 3).reshape(tiles, blocks * SUB, lines)]
  transfers between devices with their start and end apart: 15 -> 30, of which waited for: 2 -> 5; matrix products, arithmetic and copies ran while one was open for 9% -> 10% of each run, Pallas kernels for 0% -> 3%
where the time goes in v3:
time: 70.8 us; the launch traced here: 70.6 us
  starting transfers between devices  45.9 us (65%)
  Pallas kernels  10.3 us (15%)
  waiting for transfers between devices  7.21 us (10%)
  local copies, waits for them, and re-layouts  7 us (10%)
    ppermute x30, starting transfers between devices, exchange(): lax.ppermute(block, 'lines', [(i, i ^ index) for i in range(devices)])  45.9 us
    ppermute x30, waiting for transfers between devices, exchange(): lax.ppermute(block, 'lines', [(i, i ^ index) for i in range(devices)])  7.21 us
    pallas_call x2, Pallas kernels, compress(): pl.pallas_call(kernel, out_shape=[jax.ShapeDtypeStruct(block, jnp.bfloat1...  4.81 us
    another operation x1, local copies, waits for them, and re-layouts, phase_tables(): phase = phase.transpose(0, 2, 1, 3).reshape(tiles, blocks * SUB, lines)  3.01 us
    pallas_call x1, Pallas kernels, focus(): pl.pallas_call(lambda *refs: focus_kernel(shape, *refs), out_shape=[jax.S...  2.86 us
    pallas_call x1, Pallas kernels, goldstein(): pl.pallas_call(lambda *refs: goldstein_kernel(shape, *refs), out_shape=ja...  2.63 us
    reshape x1, local copies, waits for them, and re-layouts, phase_tables(): phase = azimuth_phase.reshape(looks_rows, ML_RG, lines, blocks)  2.08 us
    sin x1, local copies, waits for them, and re-layouts, phase_tables(): return (jnp.cos(phase), jnp.sin(phase))  1.85 us
  transfers between devices with their start and end apart: 30, of which 5 were waited for; matrix products, arithmetic and copies ran while one was open for 10% of the time, Pallas kernels for 3%

profile of v3, /device:TPU:0, one launch (start us, length us, event | category | flops | bytes accessed | tf_op | source)
XLA Modules:
  0.0 70.6 jit_solution(14932121007298912303)
XLA Ops:
  0.0 2.4 %compress.2 = (bf16[4,4,16,128]{3,2,1,0:T(8,128)(2,1)S(1)}, bf16[4,4,16,128]{3,2,1,0:T(8,128)(2,1)S(1)}, bf16[4,4,16,128]{3,2,1,0:T(8,128)(2,1)S(1)}, bf16[4,4,1...) custom-call(bf16[4,2,128,512]{3,2,1,0:T(8,128)(2,1)} %raw_hbm.3, ...), custom_call_target="tpu_custom_call" | custom-call | flops 536870912 | bytes 2621440 | tf_op jit(solution)/shard_map/compress/pallas_call | solution.py:148
  2.4 4.1 %collective-permute-start = (bf16[4,4,16,128]{3,2,1,0:T(8,128)(2,1)S(1)}, bf16[4,4,16,128]{3,2,1,0:T(8,128)(2,1)S(1)}, u32[]{:S(2)}, u32[]{:S(2)}) collective-permute-start(bf16[4,4,16,128]{3,2,1,0:T(8,128)(2,1)S(1)} %get-tuple-element.37), channel_id=1, source_target_pairs={{0,8},{1,9},{2,10},{3,11},{4,12},{5,13},{6,14},{7,15},{8,0},{9,1},... | collective-permute-start | bytes 196616 | tf_op jit(solution)/shard_map/ppermute | solution.py:475
  6.5 3.0 %collective-permute-start.9 = (bf16[4,4,16,128]{3,2,1,0:T(8,128)(2,1)S(1)}, bf16[4,4,16,128]{3,2,1,0:T(8,128)(2,1)S(1)}, u32[]{:S(2)}, u32[]{:S(2)}) collective-permute-start(bf16[4,4,16,128]{3,2,1,0:T(8,128)(2,1)S(1)} %get-tuple-element.47), channel_id=1, source_target_pairs={{0,10},{1,11},{2,8},{3,9},{4,14},{5,15},{6,12},{7,13},{8,2},{9,3},... | collective-permute-start | bytes 196616 | tf_op jit(solution)/shard_map/ppermute | solution.py:475
  10.2 3.6 %collective-permute-start.11 = (bf16[4,4,16,128]{3,2,1,0:T(8,128)(2,1)S(1)}, bf16[4,4,16,128]{3,2,1,0:T(8,128)(2,1)S(1)}, u32[]{:S(2)}, u32[]{:S(2)}) collective-permute-start(bf16[4,4,16,128]{3,2,1,0:T(8,128)(2,1)S(1)} %get-tuple-element.49), channel_id=1, source_target_pairs={{0,12},{1,13},{2,14},{3,15},{4,8},{5,9},{6,10},{7,11},{8,4},{9,5},... | collective-permute-start | bytes 196616 | tf_op jit(solution)/shard_map/ppermute | solution.py:475
  14.6 2.4 %compress.3 = (bf16[4,4,16,128]{3,2,1,0:T(8,128)(2,1)S(1)}, bf16[4,4,16,128]{3,2,1,0:T(8,128)(2,1)S(1)}, bf16[4,4,16,128]{3,2,1,0:T(8,128)(2,1)S(1)}, bf16[4,4,1...) custom-call(bf16[4,2,128,512]{3,2,1,0:T(8,128)(2,1)} %raw_hbm.3, ...), custom_call_target="tpu_custom_call" | custom-call | flops 536870912 | bytes 2621440 | tf_op jit(solution)/shard_map/compress/pallas_call | solution.py:148
  17.5 3.9 %collective-permute-start.13 = (bf16[4,4,16,128]{3,2,1,0:T(8,128)(2,1)S(1)}, bf16[4,4,16,128]{3,2,1,0:T(8,128)(2,1)S(1)}, u32[]{:S(2)}, u32[]{:S(2)}) collective-permute-start(bf16[4,4,16,128]{3,2,1,0:T(8,128)(2,1)S(1)} %get-tuple-element.51), channel_id=1, source_target_pairs={{0,14},{1,15},{2,12},{3,13},{4,10},{5,11},{6,8},{7,9},{8,6},{9,7},... | collective-permute-start | bytes 196616 | tf_op jit(solution)/shard_map/ppermute | solution.py:475
  21.4 3.1 %collective-permute-start.14 = (bf16[4,4,16,128]{3,2,1,0:T(8,128)(2,1)S(1)}, bf16[4,4,16,128]{3,2,1,0:T(8,128)(2,1)S(1)}, u32[]{:S(2)}, u32[]{:S(2)}) collective-permute-start(bf16[4,4,16,128]{3,2,1,0:T(8,128)(2,1)S(1)} %get-tuple-element.52), channel_id=1, source_target_pairs={{0,15},{1,14},{2,13},{3,12},{4,11},{5,10},{6,9},{7,8},{8,7},{9,6},... | collective-permute-start | bytes 196616 | tf_op jit(solution)/shard_map/ppermute | solution.py:475
  24.5 1.7 %collective-permute-start.2 = (bf16[4,4,16,128]{3,2,1,0:T(8,128)(2,1)S(1)}, bf16[4,4,16,128]{3,2,1,0:T(8,128)(2,1)S(1)}, u32[]{:S(2)}, u32[]{:S(2)}) collective-permute-start(bf16[4,4,16,128]{3,2,1,0:T(8,128)(2,1)S(1)} %get-tuple-element.40), channel_id=1, source_target_pairs={{0,2},{1,3},{2,0},{3,1},{4,6},{5,7},{6,4},{7,5},{8,10},{9,11},{10,... | collective-permute-start | bytes 196616 | tf_op jit(solution)/shard_map/ppermute | solution.py:475
  26.2 2.1 %reshape.6 = f32[8,4,128,16]{3,2,1,0:T(8,128)} reshape(f32[32,2048]{1,0:T(8,128)S(1)} %copy-done.10) | data formatting | bytes 524288 | tf_op jit(solution)/shard_map/reshape | solution.py:263
  28.4 3.0 %copy.15 = f32[4,16,8,128]{3,2,1,0:T(8,128)} copy(f32[4,16,8,128]{1,3,0,2:T(8,128)} %bitcast.3) | data formatting | bytes 524288 | tf_op jit(solution)/shard_map/transpose;transpose | solution.py:265
  31.6 1.6 %collective-permute-start.5 = (bf16[4,4,16,128]{3,2,1,0:T(8,128)(2,1)S(1)}, bf16[4,4,16,128]{3,2,1,0:T(8,128)(2,1)S(1)}, u32[]{:S(2)}, u32[]{:S(2)}) collective-permute-start(bf16[4,4,16,128]{3,2,1,0:T(8,128)(2,1)S(1)} %get-tuple-element.43), channel_id=1, source_target_pairs={{0,5},{1,4},{2,7},{3,6},{4,1},{5,0},{6,3},{7,2},{8,13},{9,12},{10,... | collective-permute-start | bytes 196616 | tf_op jit(solution)/shard_map/ppermute | solution.py:475
  36.0 1.9 %fusion = (f32[4,128,128]{2,1,0:T(8,128)S(1)}, f32[4,128,128]{2,1,0:T(8,128)S(1)}) fusion(f32[4,128,128]{2,1,0:T(8,128)} %bitcast.4), kind=kLoop, calls=%fused_computation | loop fusion | bytes 786432 | tf_op jit(solution)/shard_map/sin | solution.py:267
  37.9 2.5 %collective-permute-done.6.refs_12_ = bf16[4,4,16,128]{3,2,1,0:T(8,128)(2,1)S(1)} collective-permute-done((bf16[4,4,16,128]{3,2,1,0:T(8,128)(2,1)S(1)}, bf16[4,4,16,128]{3,2,1,0:T(8,128)(2,1)S(1)}, u32[]{:S(2)}, u32[]{:S(2)}) %collective-permute-start.6) | collective-permute-done | bytes 65568 | tf_op jit(solution)/shard_map/ppermute | solution.py:475
  40.6 2.9 %focus.1 = (bf16[48,128]{1,0:T(8,128)(2,1)S(1)}, bf16[48,128]{1,0:T(8,128)(2,1)S(1)}, bf16[48,128]{1,0:T(8,128)(2,1)S(1)}, bf16[48,128]{1,0:T(8,128)(2,1)S(1)}, ...) custom-call(s32[4]{0:T(128)S(1)} %copy-done.6, ...), custom_call_target="tpu_custom_call" | custom-call | flops 536870912 | bytes 2097152 | tf_op jit(solution)/shard_map/focus/pallas_call | solution.py:289
  48.1 1.7 %collective-permute-start.21 = (bf16[48,128]{1,0:T(8,128)(2,1)S(1)}, bf16[48,128]{1,0:T(8,128)(2,1)S(1)}, u32[]{:S(2)}, u32[]{:S(2)}) collective-permute-start(bf16[48,128]{1,0:T(8,128)(2,1)S(1)} %get-tuple-element.60), channel_id=1, source_target_pairs={{0,7},{1,6},{2,5},{3,4},{4,3},{5,2},{6,1},{7,0},{8,15},{9,14},{10,... | collective-permute-start | bytes 36872 | tf_op jit(solution)/shard_map/ppermute | solution.py:475
  49.9 2.7 %collective-permute-start.22 = (bf16[48,128]{1,0:T(8,128)(2,1)S(1)}, bf16[48,128]{1,0:T(8,128)(2,1)S(1)}, u32[]{:S(2)}, u32[]{:S(2)}) collective-permute-start(bf16[48,128]{1,0:T(8,128)(2,1)S(1)} %get-tuple-element.61), channel_id=1, source_target_pairs={{0,8},{1,9},{2,10},{3,11},{4,12},{5,13},{6,14},{7,15},{8,0},{9,1},... | collective-permute-start | bytes 36872 | tf_op jit(solution)/shard_map/ppermute | solution.py:475
  52.8 2.1 %collective-permute-start.24 = (bf16[48,128]{1,0:T(8,128)(2,1)S(1)}, bf16[48,128]{1,0:T(8,128)(2,1)S(1)}, u32[]{:S(2)}, u32[]{:S(2)}) collective-permute-start(bf16[48,128]{1,0:T(8,128)(2,1)S(1)} %get-tuple-element.63), channel_id=1, source_target_pairs={{0,10},{1,11},{2,8},{3,9},{4,14},{5,15},{6,12},{7,13},{8,2},{9,3},... | collective-permute-start | bytes 36872 | tf_op jit(solution)/shard_map/ppermute | solution.py:475
  56.1 2.3 %collective-permute-start.26 = (bf16[48,128]{1,0:T(8,128)(2,1)S(1)}, bf16[48,128]{1,0:T(8,128)(2,1)S(1)}, u32[]{:S(2)}, u32[]{:S(2)}) collective-permute-start(bf16[48,128]{1,0:T(8,128)(2,1)S(1)} %get-tuple-element.65), channel_id=1, source_target_pairs={{0,12},{1,13},{2,14},{3,15},{4,8},{5,9},{6,10},{7,11},{8,4},{9,5},... | collective-permute-start | bytes 36872 | tf_op jit(solution)/shard_map/ppermute | solution.py:475
  58.4 1.5 %collective-permute-start.27 = (bf16[48,128]{1,0:T(8,128)(2,1)S(1)}, bf16[48,128]{1,0:T(8,128)(2,1)S(1)}, u32[]{:S(2)}, u32[]{:S(2)}) collective-permute-start(bf16[48,128]{1,0:T(8,128)(2,1)S(1)} %get-tuple-element.66), channel_id=1, source_target_pairs={{0,13},{1,12},{2,15},{3,14},{4,9},{5,8},{6,11},{7,10},{8,5},{9,4},... | collective-permute-start | bytes 36872 | tf_op jit(solution)/shard_map/ppermute | solution.py:475
  59.9 2.3 %collective-permute-start.28 = (bf16[48,128]{1,0:T(8,128)(2,1)S(1)}, bf16[48,128]{1,0:T(8,128)(2,1)S(1)}, u32[]{:S(2)}, u32[]{:S(2)}) collective-permute-start(bf16[48,128]{1,0:T(8,128)(2,1)S(1)} %get-tuple-element.67), channel_id=1, source_target_pairs={{0,14},{1,15},{2,12},{3,13},{4,10},{5,11},{6,8},{7,9},{8,6},{9,7},... | collective-permute-start | bytes 36872 | tf_op jit(solution)/shard_map/ppermute | solution.py:475
  62.2 1.9 %collective-permute-start.29 = (bf16[48,128]{1,0:T(8,128)(2,1)S(1)}, bf16[48,128]{1,0:T(8,128)(2,1)S(1)}, u32[]{:S(2)}, u32[]{:S(2)}) collective-permute-start(bf16[48,128]{1,0:T(8,128)(2,1)S(1)} %get-tuple-element.68), channel_id=1, source_target_pairs={{0,15},{1,14},{2,13},{3,12},{4,11},{5,10},{6,9},{7,8},{8,7},{9,6},... | collective-permute-start | bytes 36872 | tf_op jit(solution)/shard_map/ppermute | solution.py:475
  64.1 2.2 %collective-permute-done.28.refs_14_ = bf16[48,128]{1,0:T(8,128)(2,1)S(1)} collective-permute-done((bf16[48,128]{1,0:T(8,128)(2,1)S(1)}, bf16[48,128]{1,0:T(8,128)(2,1)S(1)}, u32[]{:S(2)}, u32[]{:S(2)}) %collective-permute-start.28) | collective-permute-done | bytes 12320 | tf_op jit(solution)/shard_map/ppermute | solution.py:475
  66.3 1.7 %collective-permute-done.29.refs_15_ = bf16[48,128]{1,0:T(8,128)(2,1)S(1)} collective-permute-done((bf16[48,128]{1,0:T(8,128)(2,1)S(1)}, bf16[48,128]{1,0:T(8,128)(2,1)S(1)}, u32[]{:S(2)}, u32[]{:S(2)}) %collective-permute-start.29) | collective-permute-done | bytes 12320 | tf_op jit(solution)/shard_map/ppermute | solution.py:475
  68.0 2.6 %goldstein.1 = f32[4,2,64,128]{3,2,1,0:T(8,128)} custom-call(bf16[48,128]{1,0:T(8,128)(2,1)S(1)} %get-tuple-element.53.refs_0_, bf16[48,128]{1,0:T(8,128)(2,1)S(1)} %collective-permute-done.15.refs_1_, bf16[48,128]{1,0:T(8,128)(2,1)S(1)} %collective-permute-done.16.refs_2_, bf16[48,128]{1,0:T(8,128)(2,1)S(1)} %collective-permute-done.17.refs_3_, ...), custom_call_target="tpu_custom_call" | custom-call | tf_op jit(solution)/shard_map/goldstein/pallas_call | solution.py:454
  (65 shorter events, 11.3 us)
Async XLA Ops:
  2.4 11.3 %collective-permute-start = (bf16[4,4,16,128]{3,2,1,0:T(8,128)(2,1)S(1)}, bf16[4,4,16,128]{3,2,1,0:T(8,128)(2,1)S(1)}, u32[]{:S(2)}, u32[]{:S(2)}) collective-permute-start(bf16[4,4,16,128]{3,2,1,0:T(8,128)(2,1)S(1)} %get-tuple-element.37), channel_id=1, source_target_pairs={{0,8},{1,9},{2,10},{3,11},{4,12},{5,13},{6,14},{7,15},{8,0},{9,1},... | collective-permute-start | bytes 196616 | tf_op jit(solution)/shard_map/ppermute | solution.py:475
  6.5 11.0 %collective-permute-start.8 = (bf16[4,4,16,128]{3,2,1,0:T(8,128)(2,1)S(1)}, bf16[4,4,16,128]{3,2,1,0:T(8,128)(2,1)S(1)}, u32[]{:S(2)}, u32[]{:S(2)}) collective-permute-start(bf16[4,4,16,128]{3,2,1,0:T(8,128)(2,1)S(1)} %get-tuple-element.46), channel_id=1, source_target_pairs={{0,9},{1,8},{2,11},{3,10},{4,13},{5,12},{6,15},{7,14},{8,1},{9,0},... | collective-permute-start | bytes 196616 | tf_op jit(solution)/shard_map/ppermute | solution.py:475
  6.5 14.9 %collective-permute-start.9 = (bf16[4,4,16,128]{3,2,1,0:T(8,128)(2,1)S(1)}, bf16[4,4,16,128]{3,2,1,0:T(8,128)(2,1)S(1)}, u32[]{:S(2)}, u32[]{:S(2)}) collective-permute-start(bf16[4,4,16,128]{3,2,1,0:T(8,128)(2,1)S(1)} %get-tuple-element.47), channel_id=1, source_target_pairs={{0,10},{1,11},{2,8},{3,9},{4,14},{5,15},{6,12},{7,13},{8,2},{9,3},... | collective-permute-start | bytes 196616 | tf_op jit(solution)/shard_map/ppermute | solution.py:475
  9.6 14.9 %collective-permute-start.10 = (bf16[4,4,16,128]{3,2,1,0:T(8,128)(2,1)S(1)}, bf16[4,4,16,128]{3,2,1,0:T(8,128)(2,1)S(1)}, u32[]{:S(2)}, u32[]{:S(2)}) collective-permute-start(bf16[4,4,16,128]{3,2,1,0:T(8,128)(2,1)S(1)} %get-tuple-element.48), channel_id=1, source_target_pairs={{0,11},{1,10},{2,9},{3,8},{4,15},{5,14},{6,13},{7,12},{8,3},{9,2},... | collective-permute-start | bytes 196616 | tf_op jit(solution)/shard_map/ppermute | solution.py:475
  10.2 14.3 %collective-permute-start.11 = (bf16[4,4,16,128]{3,2,1,0:T(8,128)(2,1)S(1)}, bf16[4,4,16,128]{3,2,1,0:T(8,128)(2,1)S(1)}, u32[]{:S(2)}, u32[]{:S(2)}) collective-permute-start(bf16[4,4,16,128]{3,2,1,0:T(8,128)(2,1)S(1)} %get-tuple-element.49), channel_id=1, source_target_pairs={{0,12},{1,13},{2,14},{3,15},{4,8},{5,9},{6,10},{7,11},{8,4},{9,5},... | collective-permute-start | bytes 196616 | tf_op jit(solution)/shard_map/ppermute | solution.py:475
  13.7 17.6 %collective-permute-start.12 = (bf16[4,4,16,128]{3,2,1,0:T(8,128)(2,1)S(1)}, bf16[4,4,16,128]{3,2,1,0:T(8,128)(2,1)S(1)}, u32[]{:S(2)}, u32[]{:S(2)}) collective-permute-start(bf16[4,4,16,128]{3,2,1,0:T(8,128)(2,1)S(1)} %get-tuple-element.50), channel_id=1, source_target_pairs={{0,13},{1,12},{2,15},{3,14},{4,9},{5,8},{6,11},{7,10},{8,5},{9,4},... | collective-permute-start | bytes 196616 | tf_op jit(solution)/shard_map/ppermute | solution.py:475
  17.5 14.1 %collective-permute-start.13 = (bf16[4,4,16,128]{3,2,1,0:T(8,128)(2,1)S(1)}, bf16[4,4,16,128]{3,2,1,0:T(8,128)(2,1)S(1)}, u32[]{:S(2)}, u32[]{:S(2)}) collective-permute-start(bf16[4,4,16,128]{3,2,1,0:T(8,128)(2,1)S(1)} %get-tuple-element.51), channel_id=1, source_target_pairs={{0,14},{1,15},{2,12},{3,13},{4,10},{5,11},{6,8},{7,9},{8,6},{9,7},... | collective-permute-start | bytes 196616 | tf_op jit(solution)/shard_map/ppermute | solution.py:475
  21.4 10.2 %collective-permute-start.14 = (bf16[4,4,16,128]{3,2,1,0:T(8,128)(2,1)S(1)}, bf16[4,4,16,128]{3,2,1,0:T(8,128)(2,1)S(1)}, u32[]{:S(2)}, u32[]{:S(2)}) collective-permute-start(bf16[4,4,16,128]{3,2,1,0:T(8,128)(2,1)S(1)} %get-tuple-element.52), channel_id=1, source_target_pairs={{0,15},{1,14},{2,13},{3,12},{4,11},{5,10},{6,9},{7,8},{8,7},{9,6},... | collective-permute-start | bytes 196616 | tf_op jit(solution)/shard_map/ppermute | solution.py:475
  24.5 8.8 %collective-permute-start.1 = (bf16[4,4,16,128]{3,2,1,0:T(8,128)(2,1)S(1)}, bf16[4,4,16,128]{3,2,1,0:T(8,128)(2,1)S(1)}, u32[]{:S(2)}, u32[]{:S(2)}) collective-permute-start(bf16[4,4,16,128]{3,2,1,0:T(8,128)(2,1)S(1)} %get-tuple-element.39), channel_id=1, source_target_pairs={{0,1},{1,0},{2,3},{3,2},{4,5},{5,4},{6,7},{7,6},{8,9},{9,8},{10,11... | collective-permute-start | bytes 196616 | tf_op jit(solution)/shard_map/ppermute | solution.py:475
  24.5 10.2 %collective-permute-start.2 = (bf16[4,4,16,128]{3,2,1,0:T(8,128)(2,1)S(1)}, bf16[4,4,16,128]{3,2,1,0:T(8,128)(2,1)S(1)}, u32[]{:S(2)}, u32[]{:S(2)}) collective-permute-start(bf16[4,4,16,128]{3,2,1,0:T(8,128)(2,1)S(1)} %get-tuple-element.40), channel_id=1, source_target_pairs={{0,2},{1,3},{2,0},{3,1},{4,6},{5,7},{6,4},{7,5},{8,10},{9,11},{10,... | collective-permute-start | bytes 196616 | tf_op jit(solution)/shard_map/ppermute | solution.py:475
  31.4 6.4 %collective-permute-start.3 = (bf16[4,4,16,128]{3,2,1,0:T(8,128)(2,1)S(1)}, bf16[4,4,16,128]{3,2,1,0:T(8,128)(2,1)S(1)}, u32[]{:S(2)}, u32[]{:S(2)}) collective-permute-start(bf16[4,4,16,128]{3,2,1,0:T(8,128)(2,1)S(1)} %get-tuple-element.41), channel_id=1, source_target_pairs={{0,3},{1,2},{2,1},{3,0},{4,7},{5,6},{6,5},{7,4},{8,11},{9,10},{10,... | collective-permute-start | bytes 196616 | tf_op jit(solution)/shard_map/ppermute | solution.py:475
  31.6 6.3 %collective-permute-start.4 = (bf16[4,4,16,128]{3,2,1,0:T(8,128)(2,1)S(1)}, bf16[4,4,16,128]{3,2,1,0:T(8,128)(2,1)S(1)}, u32[]{:S(2)}, u32[]{:S(2)}) collective-permute-start(bf16[4,4,16,128]{3,2,1,0:T(8,128)(2,1)S(1)} %get-tuple-element.42), channel_id=1, source_target_pairs={{0,4},{1,5},{2,6},{3,7},{4,0},{5,1},{6,2},{7,3},{8,12},{9,13},{10,... | collective-permute-start | bytes 196616 | tf_op jit(solution)/shard_map/ppermute | solution.py:475
  31.6 6.2 %collective-permute-start.5 = (bf16[4,4,16,128]{3,2,1,0:T(8,128)(2,1)S(1)}, bf16[4,4,16,128]{3,2,1,0:T(8,128)(2,1)S(1)}, u32[]{:S(2)}, u32[]{:S(2)}) collective-permute-start(bf16[4,4,16,128]{3,2,1,0:T(8,128)(2,1)S(1)} %get-tuple-element.43), channel_id=1, source_target_pairs={{0,5},{1,4},{2,7},{3,6},{4,1},{5,0},{6,3},{7,2},{8,13},{9,12},{10,... | collective-permute-start | bytes 196616 | tf_op jit(solution)/shard_map/ppermute | solution.py:475
  33.3 7.1 %collective-permute-start.6 = (bf16[4,4,16,128]{3,2,1,0:T(8,128)(2,1)S(1)}, bf16[4,4,16,128]{3,2,1,0:T(8,128)(2,1)S(1)}, u32[]{:S(2)}, u32[]{:S(2)}) collective-permute-start(bf16[4,4,16,128]{3,2,1,0:T(8,128)(2,1)S(1)} %get-tuple-element.44), channel_id=1, source_target_pairs={{0,6},{1,7},{2,4},{3,5},{4,2},{5,3},{6,0},{7,1},{8,14},{9,15},{10,... | collective-permute-start | bytes 196616 | tf_op jit(solution)/shard_map/ppermute | solution.py:475
  45.4 7.1 %collective-permute-start.18 = (bf16[48,128]{1,0:T(8,128)(2,1)S(1)}, bf16[48,128]{1,0:T(8,128)(2,1)S(1)}, u32[]{:S(2)}, u32[]{:S(2)}) collective-permute-start(bf16[48,128]{1,0:T(8,128)(2,1)S(1)} %get-tuple-element.57), channel_id=1, source_target_pairs={{0,4},{1,5},{2,6},{3,7},{4,0},{5,1},{6,2},{7,3},{8,12},{9,13},{10,... | collective-permute-start | bytes 36872 | tf_op jit(solution)/shard_map/ppermute | solution.py:475
  46.6 6.2 %collective-permute-start.19 = (bf16[48,128]{1,0:T(8,128)(2,1)S(1)}, bf16[48,128]{1,0:T(8,128)(2,1)S(1)}, u32[]{:S(2)}, u32[]{:S(2)}) collective-permute-start(bf16[48,128]{1,0:T(8,128)(2,1)S(1)} %get-tuple-element.58), channel_id=1, source_target_pairs={{0,5},{1,4},{2,7},{3,6},{4,1},{5,0},{6,3},{7,2},{8,13},{9,12},{10,... | collective-permute-start | bytes 36872 | tf_op jit(solution)/shard_map/ppermute | solution.py:475
  47.5 7.4 %collective-permute-start.20 = (bf16[48,128]{1,0:T(8,128)(2,1)S(1)}, bf16[48,128]{1,0:T(8,128)(2,1)S(1)}, u32[]{:S(2)}, u32[]{:S(2)}) collective-permute-start(bf16[48,128]{1,0:T(8,128)(2,1)S(1)} %get-tuple-element.59), channel_id=1, source_target_pairs={{0,6},{1,7},{2,4},{3,5},{4,2},{5,3},{6,0},{7,1},{8,14},{9,15},{10,... | collective-permute-start | bytes 36872 | tf_op jit(solution)/shard_map/ppermute | solution.py:475
  48.1 8.0 %collective-permute-start.21 = (bf16[48,128]{1,0:T(8,128)(2,1)S(1)}, bf16[48,128]{1,0:T(8,128)(2,1)S(1)}, u32[]{:S(2)}, u32[]{:S(2)}) collective-permute-start(bf16[48,128]{1,0:T(8,128)(2,1)S(1)} %get-tuple-element.60), channel_id=1, source_target_pairs={{0,7},{1,6},{2,5},{3,4},{4,3},{5,2},{6,1},{7,0},{8,15},{9,14},{10,... | collective-permute-start | bytes 36872 | tf_op jit(solution)/shard_map/ppermute | solution.py:475
  49.9 8.5 %collective-permute-start.22 = (bf16[48,128]{1,0:T(8,128)(2,1)S(1)}, bf16[48,128]{1,0:T(8,128)(2,1)S(1)}, u32[]{:S(2)}, u32[]{:S(2)}) collective-permute-start(bf16[48,128]{1,0:T(8,128)(2,1)S(1)} %get-tuple-element.61), channel_id=1, source_target_pairs={{0,8},{1,9},{2,10},{3,11},{4,12},{5,13},{6,14},{7,15},{8,0},{9,1},... | collective-permute-start | bytes 36872 | tf_op jit(solution)/shard_map/ppermute | solution.py:475
  52.6 7.3 %collective-permute-start.23 = (bf16[48,128]{1,0:T(8,128)(2,1)S(1)}, bf16[48,128]{1,0:T(8,128)(2,1)S(1)}, u32[]{:S(2)}, u32[]{:S(2)}) collective-permute-start(bf16[48,128]{1,0:T(8,128)(2,1)S(1)} %get-tuple-element.62), channel_id=1, source_target_pairs={{0,9},{1,8},{2,11},{3,10},{4,13},{5,12},{6,15},{7,14},{8,1},{9,0},... | collective-permute-start | bytes 36872 | tf_op jit(solution)/shard_map/ppermute | solution.py:475
  52.8 9.4 %collective-permute-start.24 = (bf16[48,128]{1,0:T(8,128)(2,1)S(1)}, bf16[48,128]{1,0:T(8,128)(2,1)S(1)}, u32[]{:S(2)}, u32[]{:S(2)}) collective-permute-start(bf16[48,128]{1,0:T(8,128)(2,1)S(1)} %get-tuple-element.63), channel_id=1, source_target_pairs={{0,10},{1,11},{2,8},{3,9},{4,14},{5,15},{6,12},{7,13},{8,2},{9,3},... | collective-permute-start | bytes 36872 | tf_op jit(solution)/shard_map/ppermute | solution.py:475
  54.8 9.3 %collective-permute-start.25 = (bf16[48,128]{1,0:T(8,128)(2,1)S(1)}, bf16[48,128]{1,0:T(8,128)(2,1)S(1)}, u32[]{:S(2)}, u32[]{:S(2)}) collective-permute-start(bf16[48,128]{1,0:T(8,128)(2,1)S(1)} %get-tuple-element.64), channel_id=1, source_target_pairs={{0,11},{1,10},{2,9},{3,8},{4,15},{5,14},{6,13},{7,12},{8,3},{9,2},... | collective-permute-start | bytes 36872 | tf_op jit(solution)/shard_map/ppermute | solution.py:475
  56.1 8.0 %collective-permute-start.26 = (bf16[48,128]{1,0:T(8,128)(2,1)S(1)}, bf16[48,128]{1,0:T(8,128)(2,1)S(1)}, u32[]{:S(2)}, u32[]{:S(2)}) collective-permute-start(bf16[48,128]{1,0:T(8,128)(2,1)S(1)} %get-tuple-element.65), channel_id=1, source_target_pairs={{0,12},{1,13},{2,14},{3,15},{4,8},{5,9},{6,10},{7,11},{8,4},{9,5},... | collective-permute-start | bytes 36872 | tf_op jit(solution)/shard_map/ppermute | solution.py:475
  59.9 6.4 %collective-permute-start.28 = (bf16[48,128]{1,0:T(8,128)(2,1)S(1)}, bf16[48,128]{1,0:T(8,128)(2,1)S(1)}, u32[]{:S(2)}, u32[]{:S(2)}) collective-permute-start(bf16[48,128]{1,0:T(8,128)(2,1)S(1)} %get-tuple-element.67), channel_id=1, source_target_pairs={{0,14},{1,15},{2,12},{3,13},{4,10},{5,11},{6,8},{7,9},{8,6},{9,7},... | collective-permute-start | bytes 36872 | tf_op jit(solution)/shard_map/ppermute | solution.py:475
  (17 other events, 344.5 us)

commit v4 on v1

--- a/solution.py
+++ b/solution.py
@@ -16,7 +16,7 @@
 LEVEL_FLOOR = 1e-06
 SUB = 8
 LANES = 128
-VMEM_BYTES = 48 * 1024 * 1024
+VMEM_BYTES = 32 * 1024 * 1024
 
 
 def real_block(table):
@@ -74,7 +74,7 @@
 
 
 def compress_kernel(
-    shape, raw_hbm, filter_hbm, out_ref, raw_ref, filter_ref, wide_ref, raw_sems, filter_sem
+    shape, raw_hbm, filter_hbm, out_ref, raw_ref, filter_ref, wide_ref, raw_sems, filter_sems
 ):
     chunk, dates, step, targets, tiles, gates, lines = shape
     looks_rows = gates // ML_RG
@@ -85,12 +85,18 @@
         )
         for first in range(0, dates, step)
     ]
-    filter_copy = pltpu.make_async_copy(filter_hbm.at[:, :, chunk], filter_ref, filter_sem)
-    filter_copy.start()
-    for copy in copies:
+    parts = 2
+    held = targets // parts
+    filter_copies = [
+        pltpu.make_async_copy(
+            filter_hbm.at[:, pl.ds(part * held, held), chunk],
+            filter_ref.at[:, pl.ds(part * held, held)],
+            filter_sems.at[part],
+        )
+        for part in range(parts)
+    ]
+    for copy in [filter_copies[0], *copies[:1], *filter_copies[1:], *copies[1:]]:
         copy.start()
-    filter_copy.wait()
-    weight = [filter_ref[part].reshape(targets * gates, gates_in) for part in (0, 1)]
 
     def product(w, x):
         return lax.dot_general(
@@ -102,11 +108,19 @@
         raw = [
             raw_ref[first : first + step, part].reshape(step * lines, gates_in) for part in (0, 1)
         ]
-        real = product(weight[0], raw[0]) - product(weight[1], raw[1])
-        imag = product(weight[1], raw[0]) + product(weight[0], raw[1])
-        for at in range(step):
-            wide_ref[first + at, 0] = real[:, at * lines : (at + 1) * lines]
-            wide_ref[first + at, 1] = imag[:, at * lines : (at + 1) * lines]
+        for group in range(parts):
+            if first == 0:
+                filter_copies[group].wait()
+            weight = [
+                filter_ref[part, group * held : (group + 1) * held].reshape(held * gates, gates_in)
+                for part in (0, 1)
+            ]
+            real = product(weight[0], raw[0]) - product(weight[1], raw[1])
+            imag = product(weight[1], raw[0]) + product(weight[0], raw[1])
+            rows = slice(group * held * gates, (group + 1) * held * gates)
+            for at in range(step):
+                wide_ref[first + at, 0, rows] = real[:, at * lines : (at + 1) * lines]
+                wide_ref[first + at, 1, rows] = imag[:, at * lines : (at + 1) * lines]
         for target in range(targets):
             for date in range(first, first + step):
                 for tile in range(tiles):
@@ -138,7 +152,7 @@
             pltpu.VMEM((2, targets, gates, gates_in), jnp.bfloat16),
             pltpu.VMEM((dates, 2, targets * gates, lines), jnp.float32),
             pltpu.SemaphoreType.DMA((dates // step,)),
-            pltpu.SemaphoreType.DMA,
+            pltpu.SemaphoreType.DMA((2,)),
         ],
         compiler_params=pltpu.CompilerParams(vmem_limit_bytes=VMEM_BYTES),
         cost_estimate=pl.CostEstimate(
@@ -147,7 +161,7 @@
             transcendentals=0,
         ),
         name="compress",
-    )(raw_echo, filter_chunks)
+    )(*[pltpu.with_memory_space_constraint(x, pltpu.HBM) for x in (raw_echo, filter_chunks)])
 
 
 def focus_kernel(
@@ -475,7 +489,7 @@
     dates, _, lines, gates_in = raw_echo.shape
     devices = lax.axis_size("lines")
     gates = azimuth_phase.shape[0]
-    chunks = 2 if gates % (4 * SUB) == 0 else 1
+    chunks = 1
     filter_chunks = range_filter.reshape(2, devices, chunks, gates // chunks, gates_in)
     phases = phase_tables(azimuth_phase, chunks, devices)
     tables = focus_tables(devices, lines)

time: 71.6 us -> 56.7 us (0.79)
  starting transfers between devices: 15.6 us -> 7.39 us
  waiting for transfers between devices: 25 us -> 18.9 us
  blocking collectives: 9.98 us -> 15.7 us
  local copies, waits for them, and re-layouts: 9.36 us -> 4.92 us
  Pallas kernels: 10.8 us -> 9.41 us
    all_to_all x3 -> x1, starting transfers between devices: 15.6 us -> 7.39 us  [exchange(): lax.all_to_all(blocks, 'lines', split_axis=0, concat_axis=0, tiled=True)]
    all_to_all x3 -> x1, waiting for transfers between devices: 25 us -> 18.9 us  [exchange(): lax.all_to_all(blocks, 'lines', split_axis=0, concat_axis=0, tiled=True)]
    all_to_all x1, blocking collectives: 9.98 us -> 15.7 us  [exchange(): lax.all_to_all(blocks, 'lines', split_axis=0, concat_axis=0, tiled=True)]
    unnamed x28 -> x22, local copies, waits for them, and re-layouts: 4.42 us -> 0.95 us
    transpose x2 -> x0, local copies, waits for them, and re-layouts: 2.31 us -> none  [the longest x1 1.28 us: phase_tables(): phase.transpose(0, 2, 1, 4, 3).reshape(chunks, tiles, SUB, blocks, lines)]
    pallas_call x2 -> x1, Pallas kernels: 4.13 us -> 2.74 us  [focus(): pl.pallas_call(lambda *refs: focus_kernel(shape, *refs), out_shape=jax.Sh...]
    another operation x0 -> x1, local copies, waits for them, and re-layouts: none -> 1.28 us  [phase_tables(): phase.transpose(0, 1, 3, 2, 4).reshape(chunks, tiles, blocks * SUB, lines)]
    sin x1, local copies, waits for them, and re-layouts: 0.97 us -> 1.99 us  [phase_tables(): return (jnp.cos(phase), jnp.sin(phase))]
  transfers between devices with their start and end apart: 3 -> 1, of which waited for: 3 -> 1; matrix products, arithmetic and copies ran while one was open for 7% -> 7% of each run, Pallas kernels for 9% -> 0%
where the time goes in v4:
time: 56.7 us; the launch traced here: 56.4 us
  waiting for transfers between devices  18.9 us (33%)
  blocking collectives  15.7 us (28%)
  Pallas kernels  9.41 us (17%)
  starting transfers between devices  7.39 us (13%)
  local copies, waits for them, and re-layouts  4.92 us (9%)
    all_to_all x1, waiting for transfers between devices, exchange(): lax.all_to_all(blocks, 'lines', split_axis=0, concat_axis=0, tiled=True)  18.9 us
    all_to_all x1, blocking collectives, exchange(): lax.all_to_all(blocks, 'lines', split_axis=0, concat_axis=0, tiled=True)  15.7 us
    all_to_all x1, starting transfers between devices, exchange(): lax.all_to_all(blocks, 'lines', split_axis=0, concat_axis=0, tiled=True)  7.39 us
    pallas_call x1, Pallas kernels, compress(): pl.pallas_call(lambda *refs: compress_kernel(shape, *refs), out_shape=jax...  4.07 us
    pallas_call x1, Pallas kernels, focus(): pl.pallas_call(lambda *refs: focus_kernel(shape, *refs), out_shape=jax.Sh...  2.74 us
    pallas_call x1, Pallas kernels, goldstein(): pl.pallas_call(lambda *refs: goldstein_kernel(shape, *refs), out_shape=ja...  2.6 us
    sin x1, local copies, waits for them, and re-layouts, phase_tables(): return (jnp.cos(phase), jnp.sin(phase))  1.99 us
    another operation x1, local copies, waits for them, and re-layouts, phase_tables(): phase.transpose(0, 1, 3, 2, 4).reshape(chunks, tiles, blocks * SUB, lines)  1.28 us
  transfers between devices with their start and end apart: 1, of which 1 were waited for; matrix products, arithmetic and copies ran while one was open for 7% of the time, Pallas kernels for 0%

profile of v4, /device:TPU:0, one launch (start us, length us, event | category | flops | bytes accessed | tf_op | source)
XLA Modules:
  0.0 56.4 jit_solution(9217798924368814224)
XLA Ops:
  0.0 4.1 %compress.1 = bf16[16,4,4,16,128]{4,3,2,1,0:T(8,128)(2,1)} custom-call(bf16[4,2,128,512]{3,2,1,0:T(8,128)(2,1)} %refs_0_.2, bf16[2,16,1,32,512]{4,3,2,1,0:T(8,128)(2,1)} %bitcast.6), custom_call_target="tpu_custom_call" | custom-call | flops 1073741824 | bytes 3145728 | tf_op jit(solution)/shard_map/compress/pallas_call | solution.py:145
  4.1 7.4 %all-to-all-start = ((bf16[16,4,4,16,128]{4,3,2,1,0:T(8,128)(2,1)}), bf16[16,4,4,16,128]{4,3,2,1,0:T(8,128)(2,1)S(1)}, u32[]{:S(2)}, u32[]{:S(2)}) async-start(bf16[16,4,4,16,128]{4,3,2,1,0:T(8,128)(2,1)} %compress.1), calls=%async_computation | async-start | bytes 2097152 | tf_op jit(solution)/shard_map/all_to_all | solution.py:498
  11.5 0.0 copy-done.10
  11.5 0.7 %reshape.10 = f32[1,8,4,128,16]{4,3,2,1,0:T(8,128)S(1)} reshape(f32[32,2048]{1,0:T(8,128)S(1)} %copy-done.10) | data formatting | bytes 524288 | tf_op jit(solution)/shard_map/reshape | solution.py:257
  12.2 0.0 copy-start.5
  12.2 0.0 copy-start.8
  12.2 0.0 copy-start.9
  12.2 1.3 %copy.15 = f32[1,4,16,8,128]{4,3,2,1,0:T(8,128)} copy(f32[1,4,16,8,128]{2,4,1,3,0:T(8,128)S(1)} %bitcast.4) | data formatting | bytes 524288 | tf_op jit(solution)/shard_map/transpose;transpose | solution.py:259
  13.5 0.0 copy-start.4
  13.6 2.0 %fusion = (f32[1,4,128,128]{3,2,1,0:T(8,128)S(1)}, f32[1,4,128,128]{3,2,1,0:T(8,128)S(1)}) fusion(f32[1,4,128,128]{3,2,1,0:T(8,128)} %bitcast.5), kind=kLoop, calls=%fused_computation | loop fusion | bytes 786432 | tf_op jit(solution)/shard_map/sin | solution.py:261
  15.5 18.9 %all-to-all-done.refs_1_ = bf16[16,4,4,16,128]{4,3,2,1,0:T(8,128)(2,1)S(1)} async-done(((bf16[16,4,4,16,128]{4,3,2,1,0:T(8,128)(2,1)}), bf16[16,4,4,16,128]{4,3,2,1,0:T(8,128)(2,1)S(1)}, u32[]{:S(2)}, u32[]{:S(2)}) %all-to-all-start) | async-done | bytes 1048608 | tf_op jit(solution)/shard_map/all_to_all | solution.py:498
  34.4 0.0 copy-done.5
  34.4 0.0 copy-done.8
  34.4 0.0 copy-done.9
  34.4 0.0 copy-start.6
  34.4 0.9 %copy-done.6 = bf16[256,256]{1,0:T(8,128)(2,1)S(1)} copy-done((bf16[256,256]{1,0:T(8,128)(2,1)S(1)}, bf16[256,256]{1,0:T(8,128)(2,1)}, u32[]{:S(2)}) %copy-start.6) | copy-done | bytes 131096
  35.3 2.7 %focus.1 = bf16[16,48,128]{2,1,0:T(8,128)(2,1)S(1)} custom-call(s32[4]{0:T(128)S(1)} %copy-done.9, bf16[16,4,4,16,128]{4,3,2,1,0:T(8,128)(2,1)S(1)} %all-to-all-done.refs_1_, f32[1,4,128,128]{3,2,1,0:T(8,128)S(1)} %get-tuple-element.6.refs_2_, f32[1,4,128,128]{3,2,1,0:T(8,128)S(1)} %get-tuple-element.5.refs_3_, f32[4,16,128]{2,1,0:T(8,128)S(1)} %copy-done.8, ...), custom_call_target="tpu_custom_call" | custom-call | flops 536870912 | bytes 2097152 | tf_op jit(solution)/shard_map/focus/pallas_call | solution.py:282
  38.1 15.7 %all_to_all.10.refs_0_ = bf16[16,48,128]{2,1,0:T(8,128)(2,1)S(1)} all-to-all(bf16[16,48,128]{2,1,0:T(8,128)(2,1)S(1)} %focus.1), channel_id=1, replica_groups=mesh['groups'=2,'lines'=16] {'lines'}, dimensions={0} | all-to-all | bytes 393216 | tf_op jit(solution)/shard_map/all_to_all | solution.py:498
  53.7 0.0 copy-done
  53.8 0.0 copy-done.1
  53.8 0.0 copy-done.3
  53.8 0.0 copy-done.4
  53.8 0.0 copy-done.7
  53.8 2.6 %goldstein.1 = f32[4,2,64,128]{3,2,1,0:T(8,128)} custom-call(bf16[16,48,128]{2,1,0:T(8,128)(2,1)S(1)} %all_to_all.10.refs_0_, bf16[2,256,256]{2,1,0:T(8,128)(2,1)S(1)} %copy-done.4, bf16[768,256]{1,0:T(8,128)(2,1)S(1)} %copy-done.1, bf16[576,256]{1,0:T(8,128)(2,1)S(1)} %copy-done.3, bf16[128,256]{1,0:T(8,128)(2,1)S(1)} %copy-done.7, ...), custom_call_target="tpu_custom_call" | custom-call | tf_op jit(solution)/shard_map/goldstein/pallas_call | solution.py:472
  (7 shorter events, 0.0 us)
Async XLA Ops:
  0.0 11.5 %copy-start.10 = (f32[32,2048]{1,0:T(8,128)S(1)}, f32[32,2048]{1,0:T(8,128)}, u32[]{:S(2)}) copy-start(f32[32,2048]{1,0:T(8,128)} %param.15) | copy-start | bytes 786436
  4.1 30.3 %all-to-all-start = ((bf16[16,4,4,16,128]{4,3,2,1,0:T(8,128)(2,1)}), bf16[16,4,4,16,128]{4,3,2,1,0:T(8,128)(2,1)S(1)}, u32[]{:S(2)}, u32[]{:S(2)}) async-start(bf16[16,4,4,16,128]{4,3,2,1,0:T(8,128)(2,1)} %compress.1), calls=%async_computation | async-start | bytes 2097152 | tf_op jit(solution)/shard_map/all_to_all | solution.py:498
  12.2 22.2 %copy-start.5 = (bf16[256,256]{1,0:T(8,128)(2,1)S(1)}, bf16[256,256]{1,0:T(8,128)(2,1)}, u32[]{:S(2)}) copy-start(bf16[256,256]{1,0:T(8,128)(2,1)} %constant.18.clone.refs_5_) | copy-start | bytes 393220
  12.2 22.2 %copy-start.8 = (f32[4,16,128]{2,1,0:T(8,128)S(1)}, f32[4,16,128]{2,1,0:T(8,128)}, u32[]{:S(2)}) copy-start(f32[4,16,128]{2,1,0:T(8,128)} %constant.20.clone.refs_4_) | copy-start | bytes 98308
  12.2 22.2 %copy-start.9 = (s32[4]{0:T(128)S(1)}, s32[4]{0:T(128)}, u32[]{:S(2)}) copy-start(s32[4]{0:T(128)} %refs_0_.3) | copy-start | bytes 52
  13.5 40.2 %copy-start = (bf16[4,128,512]{2,1,0:T(8,128)(2,1)S(1)}, bf16[4,128,512]{2,1,0:T(8,128)(2,1)}, u32[]{:S(2)}) copy-start(bf16[4,128,512]{2,1,0:T(8,128)(2,1)} %constant.26.clone.refs_6_) | copy-start | bytes 1572868
  13.5 40.2 %copy-start.1 = (bf16[768,256]{1,0:T(8,128)(2,1)S(1)}, bf16[768,256]{1,0:T(8,128)(2,1)}, u32[]{:S(2)}) copy-start(bf16[768,256]{1,0:T(8,128)(2,1)} %constant.22.clone.refs_2_) | copy-start | bytes 1179652
  13.5 40.2 %copy-start.2 = (bf16[256,576]{1,0:T(8,128)(2,1)S(1)}, bf16[256,576]{1,0:T(8,128)(2,1)}, u32[]{:S(2)}) copy-start(bf16[256,576]{1,0:T(8,128)(2,1)} %constant.25.clone.refs_5_) | copy-start | bytes 884740
  13.5 40.2 %copy-start.3 = (bf16[576,256]{1,0:T(8,128)(2,1)S(1)}, bf16[576,256]{1,0:T(8,128)(2,1)}, u32[]{:S(2)}) copy-start(bf16[576,256]{1,0:T(8,128)(2,1)} %constant.23.clone.refs_3_) | copy-start | bytes 884740
  13.5 40.2 %copy-start.4 = (bf16[2,256,256]{2,1,0:T(8,128)(2,1)S(1)}, bf16[2,256,256]{2,1,0:T(8,128)(2,1)}, u32[]{:S(2)}) copy-start(bf16[2,256,256]{2,1,0:T(8,128)(2,1)} %constant.21.clone.refs_1_) | copy-start | bytes 786436
  34.4 0.9 %copy-start.6 = (bf16[256,256]{1,0:T(8,128)(2,1)S(1)}, bf16[256,256]{1,0:T(8,128)(2,1)}, u32[]{:S(2)}) copy-start(bf16[256,256]{1,0:T(8,128)(2,1)} %constant.19.clone.refs_6_) | copy-start | bytes 393220
  35.3 18.4 %copy-start.7 = (bf16[128,256]{1,0:T(8,128)(2,1)S(1)}, bf16[128,256]{1,0:T(8,128)(2,1)}, u32[]{:S(2)}) copy-start(bf16[128,256]{1,0:T(8,128)(2,1)} %constant.24.clone.refs_4_) | copy-start | bytes 196612

commit v5 on v4

--- a/solution.py
+++ b/solution.py
@@ -74,7 +74,8 @@
 
 
 def compress_kernel(
-    shape, raw_hbm, filter_hbm, out_ref, raw_ref, filter_ref, wide_ref, raw_sems, filter_sems
+    shape, raw_hbm, filter_hbm, out_hbm, raw_ref, filter_ref, wide_ref, out_ref, raw_sems,
+    filter_sems, out_sems,
 ):
     chunk, dates, step, targets, tiles, gates, lines = shape
     looks_rows = gates // ML_RG
@@ -84,6 +85,10 @@
             raw_hbm.at[pl.ds(first, step)], raw_ref.at[pl.ds(first, step)], raw_sems.at[first // step]
         )
         for first in range(0, dates, step)
+    ]
+    out_copies = [
+        pltpu.make_async_copy(out_ref.at[:, date], out_hbm.at[:, date], out_sems.at[date])
+        for date in range(dates)
     ]
     parts = 2
     held = targets // parts
@@ -121,8 +126,8 @@
             for at in range(step):
                 wide_ref[first + at, 0, rows] = real[:, at * lines : (at + 1) * lines]
                 wide_ref[first + at, 1, rows] = imag[:, at * lines : (at + 1) * lines]
-        for target in range(targets):
-            for date in range(first, first + step):
+        for date in range(first, first + step):
+            for target in range(targets):
                 for tile in range(tiles):
                     rows = []
                     for part in (0, 1):
@@ -133,6 +138,9 @@
                     out_ref[target, date, tile] = jnp.concatenate(rows, axis=0).astype(
                         jnp.bfloat16
                     )
+            out_copies[date].start()
+    for copy in out_copies:
+        copy.wait()
 
 
 def compress(raw_echo, filter_chunks, chunk):
@@ -146,13 +154,15 @@
         lambda *refs: compress_kernel(shape, *refs),
         out_shape=jax.ShapeDtypeStruct((targets, dates, tiles, 2 * SUB, lines), jnp.bfloat16),
         in_specs=[hbm, hbm],
-        out_specs=pl.BlockSpec(memory_space=pltpu.VMEM),
+        out_specs=pl.BlockSpec(memory_space=pl.ANY),
         scratch_shapes=[
             pltpu.VMEM(raw_echo.shape, jnp.bfloat16),
             pltpu.VMEM((2, targets, gates, gates_in), jnp.bfloat16),
             pltpu.VMEM((dates, 2, targets * gates, lines), jnp.float32),
+            pltpu.VMEM((targets, dates, tiles, 2 * SUB, lines), jnp.bfloat16),
             pltpu.SemaphoreType.DMA((dates // step,)),
             pltpu.SemaphoreType.DMA((2,)),
+            pltpu.SemaphoreType.DMA((dates,)),
         ],
         compiler_params=pltpu.CompilerParams(vmem_limit_bytes=VMEM_BYTES),
         cost_estimate=pl.CostEstimate(
@@ -272,6 +282,35 @@
     return jnp.asarray(turn), fwd, back
 
 
+def staged(tables, after):
+    count = len(tables)
+
+    def kernel(*refs):
+        sems = refs[-1]
+        copies = [
+            pltpu.make_async_copy(source, target, sems.at[index])
+            for index, (source, target) in enumerate(zip(refs[:count], refs[count + 1 : -1]))
+        ]
+        for copy in copies:
+            copy.start()
+        for copy in copies:
+            copy.wait()
+
+    return pl.pallas_call(
+        kernel,
+        out_shape=[jax.ShapeDtypeStruct(table.shape, table.dtype) for table in tables],
+        in_specs=[pl.BlockSpec(memory_space=pltpu.HBM)] * count
+        + [pl.BlockSpec(memory_space=pl.ANY)],
+        out_specs=[pl.BlockSpec(memory_space=pltpu.VMEM)] * count,
+        scratch_shapes=[pltpu.SemaphoreType.DMA((count,))],
+        compiler_params=pltpu.CompilerParams(vmem_limit_bytes=VMEM_BYTES),
+        cost_estimate=pl.CostEstimate(
+            flops=0, bytes_accessed=4 * sum(table.size for table in tables), transcendentals=0
+        ),
+        name="staged",
+    )(*[pltpu.with_memory_space_constraint(table, pltpu.HBM) for table in tables], after)
+
+
 def focus(columns, pair_offset, phases, tables, chunk):
     blocks, dates, tiles, _, lines = columns.shape
     gates = tiles * SUB
@@ -492,16 +531,13 @@
     chunks = 1
     filter_chunks = range_filter.reshape(2, devices, chunks, gates // chunks, gates_in)
     phases = phase_tables(azimuth_phase, chunks, devices)
-    tables = focus_tables(devices, lines)
 
     def exchange(blocks):
         return lax.all_to_all(blocks, "lines", split_axis=0, concat_axis=0, tiled=True)
 
-    columns = [exchange(compress(raw_echo, filter_chunks, chunk)) for chunk in range(chunks)]
-    looks = [
-        exchange(focus(columns[chunk], pair_offset, phases, tables, chunk))
-        for chunk in range(chunks)
-    ]
+    sent = compress(raw_echo, filter_chunks, 0)
+    tables = staged(focus_tables(devices, lines), sent)
+    looks = [exchange(focus(exchange(sent), pair_offset, phases, tables, 0))]
     return goldstein(looks, dates, lines // ML_AZ)
 
 

time: 56.7 us -> 56.5 us (level)
  waiting for transfers between devices: 18.9 us -> 17.2 us
  Pallas kernels: 9.41 us -> 10.4 us
    all_to_all x1, waiting for transfers between devices: 18.9 us -> 17.2 us  [exchange(): lax.all_to_all(blocks, 'lines', split_axis=0, concat_axis=0, tiled=True)]
    pallas_call x0 -> x1, Pallas kernels: none -> 1.14 us  [staged(): pl.pallas_call(kernel, out_shape=[jax.ShapeDtypeStruct(table.shape, table...]
    unnamed x22 -> x20, local copies, waits for them, and re-layouts: 0.95 us -> 1.58 us
  transfers between devices with their start and end apart: 1 -> 1, of which waited for: 1 -> 1; matrix products, arithmetic and copies ran while one was open for 7% -> 7% of each run, Pallas kernels for 0% -> 2%
where the time goes in v5:
time: 56.5 us; the launch traced here: 56.2 us
  waiting for transfers between devices  17.2 us (30%)
  blocking collectives  15.7 us (28%)
  Pallas kernels  10.4 us (18%)
  starting transfers between devices  7.39 us (13%)
  local copies, waits for them, and re-layouts  5.42 us (10%)
    all_to_all x1, waiting for transfers between devices, exchange(): lax.all_to_all(blocks, 'lines', split_axis=0, concat_axis=0, tiled=True)  17.2 us
    all_to_all x1, blocking collectives, exchange(): lax.all_to_all(blocks, 'lines', split_axis=0, concat_axis=0, tiled=True)  15.7 us
    all_to_all x1, starting transfers between devices, exchange(): lax.all_to_all(blocks, 'lines', split_axis=0, concat_axis=0, tiled=True)  7.39 us
    pallas_call x1, Pallas kernels, compress(): pl.pallas_call(lambda *refs: compress_kernel(shape, *refs), out_shape=jax...  3.93 us
    pallas_call x1, Pallas kernels, focus(): pl.pallas_call(lambda *refs: focus_kernel(shape, *refs), out_shape=jax.Sh...  2.68 us
    pallas_call x1, Pallas kernels, goldstein(): pl.pallas_call(lambda *refs: goldstein_kernel(shape, *refs), out_shape=ja...  2.61 us
    sin x1, local copies, waits for them, and re-layouts, phase_tables(): return (jnp.cos(phase), jnp.sin(phase))  1.85 us
    unnamed x20, local copies, waits for them, and re-layouts  1.58 us
  transfers between devices with their start and end apart: 1, of which 1 were waited for; matrix products, arithmetic and copies ran while one was open for 7% of the time, Pallas kernels for 2%

profile of v5, /device:TPU:0, one launch (start us, length us, event | category | flops | bytes accessed | tf_op | source)
XLA Modules:
  0.0 56.2 jit_solution(5471887412440569695)
XLA Ops:
  0.0 0.0 copy-start.9
  0.0 3.9 %compress.1.refs_3_ = bf16[16,4,4,16,128]{4,3,2,1,0:T(8,128)(2,1)} custom-call(bf16[4,2,128,512]{3,2,1,0:T(8,128)(2,1)} %refs_0_.3, bf16[2,16,1,32,512]{4,3,2,1,0:T(8,128)(2,1)} %bitcast.6), custom_call_target="tpu_custom_call" | custom-call | flops 1073741824 | bytes 3145728 | tf_op jit(solution)/shard_map/compress/pallas_call | solution.py:153
  3.9 7.4 %all-to-all-start = ((bf16[16,4,4,16,128]{4,3,2,1,0:T(8,128)(2,1)}), bf16[16,4,4,16,128]{4,3,2,1,0:T(8,128)(2,1)S(1)}, u32[]{:S(2)}, u32[]{:S(2)}) async-start(bf16[16,4,4,16,128]{4,3,2,1,0:T(8,128)(2,1)} %compress.1.refs_3_), calls=%async_computation | async-start | bytes 2097152 | tf_op jit(solution)/shard_map/all_to_all | solution.py:536
  11.3 0.0 copy-done.9
  11.3 0.7 %reshape.10 = f32[1,8,4,128,16]{4,3,2,1,0:T(8,128)S(1)} reshape(f32[32,2048]{1,0:T(8,128)S(1)} %copy-done.9) | data formatting | bytes 524288 | tf_op jit(solution)/shard_map/reshape | solution.py:267
  12.1 0.0 copy-start.8
  12.1 1.3 %copy.15 = f32[1,4,16,8,128]{4,3,2,1,0:T(8,128)} copy(f32[1,4,16,8,128]{2,4,1,3,0:T(8,128)S(1)} %bitcast.4) | data formatting | bytes 524288 | tf_op jit(solution)/shard_map/transpose;transpose | solution.py:269
  13.4 0.0 copy-start.4
  13.4 1.1 %staged.1 = (f32[4,16,128]{2,1,0:T(8,128)S(1)}, bf16[256,256]{1,0:T(8,128)(2,1)S(1)}, bf16[256,256]{1,0:T(8,128)(2,1)S(1)}) custom-call(f32[4,16,128]{2,1,0:T(8,128)} %constant.20.clone.refs_0_, bf16[256,256]{1,0:T(8,128)(2,1)} %constant.18.clone.refs_1_, bf16[256,256]{1,0:T(8,128)(2,1)} %constant.19.clone.refs_2_, bf16[16,4,4,16,128]{4,3,2,1,0:T(8,128)(2,1)} %compress.1.refs_3_), custom_call_target="tpu_custom_call" | custom-call | bytes 557056 | tf_op jit(solution)/shard_map/staged/pallas_call | solution.py:299
  14.5 0.0 copy-start.5
  14.5 0.6 %copy-done.5 = bf16[256,256]{1,0:T(8,128)(2,1)} copy-done((bf16[256,256]{1,0:T(8,128)(2,1)}, bf16[256,256]{1,0:T(8,128)(2,1)S(1)}, u32[]{:S(2)}) %copy-start.5) | copy-done | bytes 131096
  15.2 1.9 %fusion = (f32[1,4,128,128]{3,2,1,0:T(8,128)S(1)}, f32[1,4,128,128]{3,2,1,0:T(8,128)S(1)}) fusion(f32[1,4,128,128]{3,2,1,0:T(8,128)} %bitcast.5), kind=kLoop, calls=%fused_computation | loop fusion | bytes 786432 | tf_op jit(solution)/shard_map/sin | solution.py:271
  17.0 17.2 %all-to-all-done.refs_1_ = bf16[16,4,4,16,128]{4,3,2,1,0:T(8,128)(2,1)S(1)} async-done(((bf16[16,4,4,16,128]{4,3,2,1,0:T(8,128)(2,1)}), bf16[16,4,4,16,128]{4,3,2,1,0:T(8,128)(2,1)S(1)}, u32[]{:S(2)}, u32[]{:S(2)}) %all-to-all-start) | async-done | bytes 1048608 | tf_op jit(solution)/shard_map/all_to_all | solution.py:536
  34.3 0.0 copy-done.8
  34.3 0.9 %copy-done.6 = bf16[256,256]{1,0:T(8,128)(2,1)S(1)} copy-done((bf16[256,256]{1,0:T(8,128)(2,1)S(1)}, bf16[256,256]{1,0:T(8,128)(2,1)}, u32[]{:S(2)}) %copy-start.6) | copy-done | bytes 131096
  35.2 2.7 %focus.1 = bf16[16,48,128]{2,1,0:T(8,128)(2,1)S(1)} custom-call(s32[4]{0:T(128)S(1)} %copy-done.8, bf16[16,4,4,16,128]{4,3,2,1,0:T(8,128)(2,1)S(1)} %all-to-all-done.refs_1_, f32[1,4,128,128]{3,2,1,0:T(8,128)S(1)} %get-tuple-element.12.refs_2_, f32[1,4,128,128]{3,2,1,0:T(8,128)S(1)} %get-tuple-element.11.refs_3_, ...), custom_call_target="tpu_custom_call" | custom-call | flops 536870912 | bytes 2097152 | tf_op jit(solution)/shard_map/focus/pallas_call | solution.py:321
  37.9 15.7 %all_to_all.10.refs_0_ = bf16[16,48,128]{2,1,0:T(8,128)(2,1)S(1)} all-to-all(bf16[16,48,128]{2,1,0:T(8,128)(2,1)S(1)} %focus.1), channel_id=1, replica_groups=mesh['groups'=2,'lines'=16] {'lines'}, dimensions={0} | all-to-all | bytes 393216 | tf_op jit(solution)/shard_map/all_to_all | solution.py:536
  53.5 0.0 copy-done
  53.5 0.0 copy-done.1
  53.5 0.0 copy-done.2
  53.6 0.0 copy-done.3
  53.6 0.0 copy-done.4
  53.6 0.0 copy-done.7
  53.6 2.6 %goldstein.1 = f32[4,2,64,128]{3,2,1,0:T(8,128)} custom-call(bf16[16,48,128]{2,1,0:T(8,128)(2,1)S(1)} %all_to_all.10.refs_0_, bf16[2,256,256]{2,1,0:T(8,128)(2,1)S(1)} %copy-done.4, bf16[768,256]{1,0:T(8,128)(2,1)S(1)} %copy-done.1, bf16[576,256]{1,0:T(8,128)(2,1)S(1)} %copy-done.3, bf16[128,256]{1,0:T(8,128)(2,1)S(1)} %copy-done.7, ...), custom_call_target="tpu_custom_call" | custom-call | tf_op jit(solution)/shard_map/goldstein/pallas_call | solution.py:511
  (6 shorter events, 0.0 us)
Async XLA Ops:
  0.0 11.3 %copy-start.9 = (f32[32,2048]{1,0:T(8,128)S(1)}, f32[32,2048]{1,0:T(8,128)}, u32[]{:S(2)}) copy-start(f32[32,2048]{1,0:T(8,128)} %param.15) | copy-start | bytes 786436
  3.9 30.3 %all-to-all-start = ((bf16[16,4,4,16,128]{4,3,2,1,0:T(8,128)(2,1)}), bf16[16,4,4,16,128]{4,3,2,1,0:T(8,128)(2,1)S(1)}, u32[]{:S(2)}, u32[]{:S(2)}) async-start(bf16[16,4,4,16,128]{4,3,2,1,0:T(8,128)(2,1)} %compress.1.refs_3_), calls=%async_computation | async-start | bytes 2097152 | tf_op jit(solution)/shard_map/all_to_all | solution.py:536
  12.1 22.2 %copy-start.8 = (s32[4]{0:T(128)S(1)}, s32[4]{0:T(128)}, u32[]{:S(2)}) copy-start(s32[4]{0:T(128)} %refs_0_.4) | copy-start | bytes 52
  13.4 40.2 %copy-start = (bf16[4,128,512]{2,1,0:T(8,128)(2,1)S(1)}, bf16[4,128,512]{2,1,0:T(8,128)(2,1)}, u32[]{:S(2)}) copy-start(bf16[4,128,512]{2,1,0:T(8,128)(2,1)} %constant.26.clone.refs_6_) | copy-start | bytes 1572868
  13.4 40.2 %copy-start.1 = (bf16[768,256]{1,0:T(8,128)(2,1)S(1)}, bf16[768,256]{1,0:T(8,128)(2,1)}, u32[]{:S(2)}) copy-start(bf16[768,256]{1,0:T(8,128)(2,1)} %constant.22.clone.refs_2_) | copy-start | bytes 1179652
  13.4 40.2 %copy-start.2 = (bf16[256,576]{1,0:T(8,128)(2,1)S(1)}, bf16[256,576]{1,0:T(8,128)(2,1)}, u32[]{:S(2)}) copy-start(bf16[256,576]{1,0:T(8,128)(2,1)} %constant.25.clone.refs_5_) | copy-start | bytes 884740
  13.4 40.2 %copy-start.3 = (bf16[576,256]{1,0:T(8,128)(2,1)S(1)}, bf16[576,256]{1,0:T(8,128)(2,1)}, u32[]{:S(2)}) copy-start(bf16[576,256]{1,0:T(8,128)(2,1)} %constant.23.clone.refs_3_) | copy-start | bytes 884740
  13.4 40.2 %copy-start.4 = (bf16[2,256,256]{2,1,0:T(8,128)(2,1)S(1)}, bf16[2,256,256]{2,1,0:T(8,128)(2,1)}, u32[]{:S(2)}) copy-start(bf16[2,256,256]{2,1,0:T(8,128)(2,1)} %constant.21.clone.refs_1_) | copy-start | bytes 786436
  14.5 0.6 %copy-start.5 = (bf16[256,256]{1,0:T(8,128)(2,1)}, bf16[256,256]{1,0:T(8,128)(2,1)S(1)}, u32[]{:S(2)}) copy-start(bf16[256,256]{1,0:T(8,128)(2,1)S(1)} %get-tuple-element.10.refs_6_) | copy-start | bytes 393220
  34.3 0.9 %copy-start.6 = (bf16[256,256]{1,0:T(8,128)(2,1)S(1)}, bf16[256,256]{1,0:T(8,128)(2,1)}, u32[]{:S(2)}) copy-start(bf16[256,256]{1,0:T(8,128)(2,1)} %copy-done.5) | copy-start | bytes 393220
  35.2 18.4 %copy-start.7 = (bf16[128,256]{1,0:T(8,128)(2,1)S(1)}, bf16[128,256]{1,0:T(8,128)(2,1)}, u32[]{:S(2)}) copy-start(bf16[128,256]{1,0:T(8,128)(2,1)} %constant.24.clone.refs_4_) | copy-start | bytes 196612

commit v6 on v5

--- a/solution.py
+++ b/solution.py
@@ -16,7 +16,7 @@
 LEVEL_FLOOR = 1e-06
 SUB = 8
 LANES = 128
-VMEM_BYTES = 32 * 1024 * 1024
+VMEM_BYTES = 20 * 1024 * 1024
 
 
 def real_block(table):
@@ -82,9 +82,10 @@
     gates_in = raw_ref.shape[3]
     copies = [
         pltpu.make_async_copy(
-            raw_hbm.at[pl.ds(first, step)], raw_ref.at[pl.ds(first, step)], raw_sems.at[first // step]
+            raw_hbm.at[date, part], raw_ref.at[date, part], raw_sems.at[date, part]
         )
-        for first in range(0, dates, step)
+        for date in range(dates)
+        for part in (0, 1)
     ]
     out_copies = [
         pltpu.make_async_copy(out_ref.at[:, date], out_hbm.at[:, date], out_sems.at[date])
@@ -94,13 +95,15 @@
     held = targets // parts
     filter_copies = [
         pltpu.make_async_copy(
-            filter_hbm.at[:, pl.ds(part * held, held), chunk],
-            filter_ref.at[:, pl.ds(part * held, held)],
-            filter_sems.at[part],
+            filter_hbm.at[side, pl.ds(part * held, held), chunk],
+            filter_ref.at[side, pl.ds(part * held, held)],
+            filter_sems.at[part, side],
         )
         for part in range(parts)
+        for side in (0, 1)
     ]
-    for copy in [filter_copies[0], *copies[:1], *filter_copies[1:], *copies[1:]]:
+    early = 2 * step
+    for copy in filter_copies[:2] + copies[:early] + filter_copies[2:] + copies[early:]:
         copy.start()
 
     def product(w, x):
@@ -109,13 +112,15 @@
         )
 
     for first in range(0, dates, step):
-        copies[first // step].wait()
+        for copy in copies[2 * first : 2 * (first + step)]:
+            copy.wait()
         raw = [
             raw_ref[first : first + step, part].reshape(step * lines, gates_in) for part in (0, 1)
         ]
         for group in range(parts):
             if first == 0:
-                filter_copies[group].wait()
+                filter_copies[2 * group].wait()
+                filter_copies[2 * group + 1].wait()
             weight = [
                 filter_ref[part, group * held : (group + 1) * held].reshape(held * gates, gates_in)
                 for part in (0, 1)
@@ -160,8 +165,8 @@
             pltpu.VMEM((2, targets, gates, gates_in), jnp.bfloat16),
             pltpu.VMEM((dates, 2, targets * gates, lines), jnp.float32),
             pltpu.VMEM((targets, dates, tiles, 2 * SUB, lines), jnp.bfloat16),
-            pltpu.SemaphoreType.DMA((dates // step,)),
-            pltpu.SemaphoreType.DMA((2,)),
+            pltpu.SemaphoreType.DMA((dates, 2)),
+            pltpu.SemaphoreType.DMA((2, 2)),
             pltpu.SemaphoreType.DMA((dates,)),
         ],
         compiler_params=pltpu.CompilerParams(vmem_limit_bytes=VMEM_BYTES),
@@ -175,41 +180,40 @@
 
 
 def focus_kernel(
-    shape, offset_ref, data_ref, cos_ref, sin_ref, turn_ref, fwd_ref, back_ref, out_ref, image_ref,
-    look_ref,
+    shape, offset_ref, data_ref, cos_ref, sin_ref, turn_ref, table_ref, out_ref, image_ref, look_ref,
 ):
     chunk, dates, blocks, tiles, gates, lines = shape
     looks_rows = gates // ML_RG
     look_lines = lines // ML_AZ
+    count = blocks * SUB
     for date in range(dates):
+        rows = []
         for tile in range(tiles):
             parts = []
             for a in range(blocks):
                 both = data_ref[a, date, tile].astype(jnp.float32)
                 parts.append((both[:SUB], both[SUB:]))
-            parts = small_dft(parts, -1)
-            turned = []
-            for a, (re, im) in enumerate(parts):
+            for a, (re, im) in enumerate(small_dft(parts, -1)):
                 tr, ti = turn_ref[0, a : a + 1], turn_ref[1, a : a + 1]
-                turned.append((re * tr - im * ti, re * ti + im * tr))
-            rows = jnp.concatenate(
-                [jnp.concatenate([re, im], axis=1) for re, im in turned], axis=0
-            ).astype(jnp.bfloat16)
-            spectrum = jnp.dot(rows, fwd_ref[...], preferred_element_type=jnp.float32)
-            re, im = spectrum[:, :lines], spectrum[:, lines:]
+                rows.append(jnp.concatenate([re * tr - im * ti, re * ti + im * tr], axis=1))
+        rows = jnp.concatenate(rows, axis=0).astype(jnp.bfloat16)
+        spectrum = jnp.dot(rows, table_ref[0], preferred_element_type=jnp.float32)
+        rows = []
+        for tile in range(tiles):
+            re = spectrum[tile * count : (tile + 1) * count, :lines]
+            im = spectrum[tile * count : (tile + 1) * count, lines:]
             pr, pi = cos_ref[chunk, tile], sin_ref[chunk, tile]
-            rows = jnp.concatenate([re * pr - im * pi, re * pi + im * pr], axis=1).astype(
-                jnp.bfloat16
-            )
-            back = jnp.dot(rows, back_ref[...], preferred_element_type=jnp.float32)
+            rows.append(jnp.concatenate([re * pr - im * pi, re * pi + im * pr], axis=1))
+        rows = jnp.concatenate(rows, axis=0).astype(jnp.bfloat16)
+        back = jnp.dot(rows, table_ref[1], preferred_element_type=jnp.float32)
+        for tile in range(tiles):
             parts = []
             for a in range(blocks):
-                re = back[a * SUB : (a + 1) * SUB, :lines]
-                im = back[a * SUB : (a + 1) * SUB, lines:]
+                row = tile * count + a * SUB
+                re, im = back[row : row + SUB, :lines], back[row : row + SUB, lines:]
                 tr, ti = turn_ref[2, a : a + 1], turn_ref[3, a : a + 1]
                 parts.append((re * tr - im * ti, re * ti + im * tr))
-            parts = small_dft(parts, 1)
-            for a, (re, im) in enumerate(parts):
+            for a, (re, im) in enumerate(small_dft(parts, 1)):
                 image_ref[date, tile, a, 0] = re
                 image_ref[date, tile, a, 1] = im
 
@@ -277,38 +281,9 @@
     ahead = wave(np.arange(blocks), np.arange(lines), total, -1)
     behind = wave(np.arange(blocks), order, total, 1)
     turn = np.stack([ahead.real, ahead.imag, behind.real, behind.imag]).astype(np.float32)
-    fwd = as_bf16(real_block(wave(np.arange(lines), np.arange(lines), lines, -1)))
-    back = as_bf16(real_block(wave(np.arange(lines), order, lines, 1) / total))
-    return jnp.asarray(turn), fwd, back
-
-
-def staged(tables, after):
-    count = len(tables)
-
-    def kernel(*refs):
-        sems = refs[-1]
-        copies = [
-            pltpu.make_async_copy(source, target, sems.at[index])
-            for index, (source, target) in enumerate(zip(refs[:count], refs[count + 1 : -1]))
-        ]
-        for copy in copies:
-            copy.start()
-        for copy in copies:
-            copy.wait()
-
-    return pl.pallas_call(
-        kernel,
-        out_shape=[jax.ShapeDtypeStruct(table.shape, table.dtype) for table in tables],
-        in_specs=[pl.BlockSpec(memory_space=pltpu.HBM)] * count
-        + [pl.BlockSpec(memory_space=pl.ANY)],
-        out_specs=[pl.BlockSpec(memory_space=pltpu.VMEM)] * count,
-        scratch_shapes=[pltpu.SemaphoreType.DMA((count,))],
-        compiler_params=pltpu.CompilerParams(vmem_limit_bytes=VMEM_BYTES),
-        cost_estimate=pl.CostEstimate(
-            flops=0, bytes_accessed=4 * sum(table.size for table in tables), transcendentals=0
-        ),
-        name="staged",
-    )(*[pltpu.with_memory_space_constraint(table, pltpu.HBM) for table in tables], after)
+    fwd = real_block(wave(np.arange(lines), np.arange(lines), lines, -1))
+    back = real_block(wave(np.arange(lines), order, lines, 1) / total)
+    return jnp.asarray(turn), as_bf16(np.stack([fwd, back]))
 
 
 def focus(columns, pair_offset, phases, tables, chunk):
@@ -321,7 +296,7 @@
     return pl.pallas_call(
         lambda *refs: focus_kernel(shape, *refs),
         out_shape=jax.ShapeDtypeStruct((blocks, slots * looks_rows, lines), jnp.bfloat16),
-        in_specs=[pl.BlockSpec(memory_space=pltpu.SMEM)] + [whole] * 6,
+        in_specs=[pl.BlockSpec(memory_space=pltpu.SMEM)] + [whole] * 5,
         out_specs=whole,
         scratch_shapes=[
             pltpu.VMEM((dates, tiles, blocks, 2, SUB, lines), jnp.float32),
@@ -471,7 +446,8 @@
             total = jnp.sum(sums[rows, LANES:], axis=0, keepdims=True)
             smooth = line + pltpu.roll(line, 1, 0) + pltpu.roll(line, PATCH - 1, 0)
             level = total * (1.0 / (PATCH * PATCH)) + LEVEL_FLOOR
-            weight = jnp.sqrt(smooth * (1.0 / (9.0 * level)) + BOX_FLOOR)
+            square = smooth * (1.0 / (9.0 * level)) + BOX_FLOOR
+            weight = square * lax.rsqrt(square)
             weighted_ref[rows, lanes] = (re[rows] * weight).astype(jnp.bfloat16)
             weighted_ref[start + bins : start + bins + PATCH, lanes] = (im[rows] * weight).astype(
                 jnp.bfloat16
@@ -536,7 +512,7 @@
         return lax.all_to_all(blocks, "lines", split_axis=0, concat_axis=0, tiled=True)
 
     sent = compress(raw_echo, filter_chunks, 0)
-    tables = staged(focus_tables(devices, lines), sent)
+    tables = focus_tables(devices, lines)
     looks = [exchange(focus(exchange(sent), pair_offset, phases, tables, 0))]
     return goldstein(looks, dates, lines // ML_AZ)
 

time: 56.5 us -> 56.5 us (level)
  waiting for transfers between devices: 17.2 us -> 18.9 us
  Pallas kernels: 10.4 us -> 9.16 us
    all_to_all x1, waiting for transfers between devices: 17.2 us -> 18.9 us  [exchange(): lax.all_to_all(blocks, 'lines', split_axis=0, concat_axis=0, tiled=True)]
    pallas_call x1 -> x0, Pallas kernels: 1.14 us -> none  [staged(): pl.pallas_call(kernel, out_shape=[jax.ShapeDtypeStruct(table.shape, table...]
    unnamed x20, local copies, waits for them, and re-layouts: 1.58 us -> 1 us
  transfers between devices with their start and end apart: 1 -> 1, of which waited for: 1 -> 1; matrix products, arithmetic and copies ran while one was open for 7% -> 7% of each run, Pallas kernels for 2% -> 0%
where the time goes in v6:
time: 56.5 us; the launch traced here: 56.2 us
  waiting for transfers between devices  18.9 us (33%)
  blocking collectives  15.7 us (28%)
  Pallas kernels  9.16 us (16%)
  starting transfers between devices  7.4 us (13%)
  local copies, waits for them, and re-layouts  4.97 us (9%)
    all_to_all x1, waiting for transfers between devices, exchange(): lax.all_to_all(blocks, 'lines', split_axis=0, concat_axis=0, tiled=True)  18.9 us
    all_to_all x1, blocking collectives, exchange(): lax.all_to_all(blocks, 'lines', split_axis=0, concat_axis=0, tiled=True)  15.7 us
    all_to_all x1, starting transfers between devices, exchange(): lax.all_to_all(blocks, 'lines', split_axis=0, concat_axis=0, tiled=True)  7.4 us
    pallas_call x1, Pallas kernels, compress(): pl.pallas_call(lambda *refs: compress_kernel(shape, *refs), out_shape=jax...  4.1 us
    pallas_call x1, Pallas kernels, focus(): pl.pallas_call(lambda *refs: focus_kernel(shape, *refs), out_shape=jax.Sh...  2.64 us
    pallas_call x1, Pallas kernels, goldstein(): pl.pallas_call(lambda *refs: goldstein_kernel(shape, *refs), out_shape=ja...  2.41 us
    sin x1, local copies, waits for them, and re-layouts, phase_tables(): return (jnp.cos(phase), jnp.sin(phase))  1.99 us
    another operation x1, local copies, waits for them, and re-layouts, phase_tables(): phase.transpose(0, 1, 3, 2, 4).reshape(chunks, tiles, blocks * SUB, lines)  1.28 us
  transfers between devices with their start and end apart: 1, of which 1 were waited for; matrix products, arithmetic and copies ran while one was open for 7% of the time, Pallas kernels for 0%

profile of v6, /device:TPU:0, one launch (start us, length us, event | category | flops | bytes accessed | tf_op | source)
XLA Modules:
  0.0 56.2 jit_solution(2664150594444289423)
XLA Ops:
  0.0 0.0 copy-start.9
  0.0 4.1 %compress.1 = bf16[16,4,4,16,128]{4,3,2,1,0:T(8,128)(2,1)} custom-call(bf16[4,2,128,512]{3,2,1,0:T(8,128)(2,1)} %refs_0_.2, bf16[2,16,1,32,512]{4,3,2,1,0:T(8,128)(2,1)} %bitcast.6), custom_call_target="tpu_custom_call" | custom-call | flops 1073741824 | bytes 3145728 | tf_op jit(solution)/shard_map/compress/pallas_call | solution.py:158
  4.1 7.4 %all-to-all-start = ((bf16[16,4,4,16,128]{4,3,2,1,0:T(8,128)(2,1)}), bf16[16,4,4,16,128]{4,3,2,1,0:T(8,128)(2,1)S(1)}, u32[]{:S(2)}, u32[]{:S(2)}) async-start(bf16[16,4,4,16,128]{4,3,2,1,0:T(8,128)(2,1)} %compress.1), calls=%async_computation | async-start | bytes 2097152 | tf_op jit(solution)/shard_map/all_to_all | solution.py:512
  11.5 0.0 copy-done.9
  11.5 0.7 %reshape.10 = f32[1,8,4,128,16]{4,3,2,1,0:T(8,128)S(1)} reshape(f32[32,2048]{1,0:T(8,128)S(1)} %copy-done.9) | data formatting | bytes 524288 | tf_op jit(solution)/shard_map/reshape | solution.py:271
  12.2 0.0 copy-start.7
  12.3 0.0 copy-start.8
  12.3 0.0 copy-start.6
  12.3 1.3 %copy.14 = f32[1,4,16,8,128]{4,3,2,1,0:T(8,128)} copy(f32[1,4,16,8,128]{2,4,1,3,0:T(8,128)S(1)} %bitcast.4) | data formatting | bytes 524288 | tf_op jit(solution)/shard_map/transpose;transpose | solution.py:273
  13.6 0.0 copy-start.4
  13.6 2.0 %fusion = (f32[1,4,128,128]{3,2,1,0:T(8,128)S(1)}, f32[1,4,128,128]{3,2,1,0:T(8,128)S(1)}) fusion(f32[1,4,128,128]{3,2,1,0:T(8,128)} %bitcast.5), kind=kLoop, calls=%fused_computation | loop fusion | bytes 786432 | tf_op jit(solution)/shard_map/sin | solution.py:275
  15.6 18.9 %all-to-all-done.refs_1_ = bf16[16,4,4,16,128]{4,3,2,1,0:T(8,128)(2,1)S(1)} async-done(((bf16[16,4,4,16,128]{4,3,2,1,0:T(8,128)(2,1)}), bf16[16,4,4,16,128]{4,3,2,1,0:T(8,128)(2,1)S(1)}, u32[]{:S(2)}, u32[]{:S(2)}) %all-to-all-start) | async-done | bytes 1048608 | tf_op jit(solution)/shard_map/all_to_all | solution.py:512
  34.5 0.0 copy-done.7
  34.5 0.0 copy-done.8
  34.5 0.9 %copy-done.5 = bf16[2,256,256]{2,1,0:T(8,128)(2,1)S(1)} copy-done((bf16[2,256,256]{2,1,0:T(8,128)(2,1)S(1)}, bf16[2,256,256]{2,1,0:T(8,128)(2,1)}, u32[]{:S(2)}) %copy-start.5) | copy-done | bytes 262168
  35.4 2.6 %focus.1 = bf16[16,48,128]{2,1,0:T(8,128)(2,1)S(1)} custom-call(s32[4]{0:T(128)S(1)} %copy-done.8, bf16[16,4,4,16,128]{4,3,2,1,0:T(8,128)(2,1)S(1)} %all-to-all-done.refs_1_, f32[1,4,128,128]{3,2,1,0:T(8,128)S(1)} %get-tuple-element.6.refs_2_, f32[1,4,128,128]{3,2,1,0:T(8,128)S(1)} %get-tuple-element.5.refs_3_, f32[4,16,128]{2,1,0:T(8,128)S(1)} %copy-done.7, ...), custom_call_target="tpu_custom_call" | custom-call | flops 536870912 | bytes 2097152 | tf_op jit(solution)/shard_map/focus/pallas_call | solution.py:296
  38.1 15.7 %all_to_all.10.refs_0_ = bf16[16,48,128]{2,1,0:T(8,128)(2,1)S(1)} all-to-all(bf16[16,48,128]{2,1,0:T(8,128)(2,1)S(1)} %focus.1), channel_id=1, replica_groups=mesh['groups'=2,'lines'=16] {'lines'}, dimensions={0} | all-to-all | bytes 393216 | tf_op jit(solution)/shard_map/all_to_all | solution.py:512
  53.7 0.0 copy-done.6
  53.7 0.0 copy-done
  53.7 0.0 copy-done.1
  53.7 0.0 copy-done.2
  53.8 0.0 copy-done.3
  53.8 0.0 copy-done.4
  53.8 2.4 %goldstein.1 = f32[4,2,64,128]{3,2,1,0:T(8,128)} custom-call(bf16[16,48,128]{2,1,0:T(8,128)(2,1)S(1)} %all_to_all.10.refs_0_, bf16[2,256,256]{2,1,0:T(8,128)(2,1)S(1)} %copy-done.4, bf16[768,256]{1,0:T(8,128)(2,1)S(1)} %copy-done.1, bf16[576,256]{1,0:T(8,128)(2,1)S(1)} %copy-done.3, bf16[128,256]{1,0:T(8,128)(2,1)S(1)} %copy-done.6, ...), custom_call_target="tpu_custom_call" | custom-call | tf_op jit(solution)/shard_map/goldstein/pallas_call | solution.py:487
  (5 shorter events, 0.0 us)
Async XLA Ops:
  0.0 11.5 %copy-start.9 = (f32[32,2048]{1,0:T(8,128)S(1)}, f32[32,2048]{1,0:T(8,128)}, u32[]{:S(2)}) copy-start(f32[32,2048]{1,0:T(8,128)} %param.14) | copy-start | bytes 786436
  4.1 30.4 %all-to-all-start = ((bf16[16,4,4,16,128]{4,3,2,1,0:T(8,128)(2,1)}), bf16[16,4,4,16,128]{4,3,2,1,0:T(8,128)(2,1)S(1)}, u32[]{:S(2)}, u32[]{:S(2)}) async-start(bf16[16,4,4,16,128]{4,3,2,1,0:T(8,128)(2,1)} %compress.1), calls=%async_computation | async-start | bytes 2097152 | tf_op jit(solution)/shard_map/all_to_all | solution.py:512
  12.2 22.2 %copy-start.7 = (f32[4,16,128]{2,1,0:T(8,128)S(1)}, f32[4,16,128]{2,1,0:T(8,128)}, u32[]{:S(2)}) copy-start(f32[4,16,128]{2,1,0:T(8,128)} %constant.16.clone.refs_4_) | copy-start | bytes 98308
  12.3 22.2 %copy-start.8 = (s32[4]{0:T(128)S(1)}, s32[4]{0:T(128)}, u32[]{:S(2)}) copy-start(s32[4]{0:T(128)} %refs_0_.3) | copy-start | bytes 52
  12.3 41.5 %copy-start.6 = (bf16[128,256]{1,0:T(8,128)(2,1)S(1)}, bf16[128,256]{1,0:T(8,128)(2,1)}, u32[]{:S(2)}) copy-start(bf16[128,256]{1,0:T(8,128)(2,1)} %constant.21.clone.refs_4_) | copy-start | bytes 196612
  13.6 40.2 %copy-start = (bf16[4,128,512]{2,1,0:T(8,128)(2,1)S(1)}, bf16[4,128,512]{2,1,0:T(8,128)(2,1)}, u32[]{:S(2)}) copy-start(bf16[4,128,512]{2,1,0:T(8,128)(2,1)} %constant.23.clone.refs_6_) | copy-start | bytes 1572868
  13.6 40.2 %copy-start.1 = (bf16[768,256]{1,0:T(8,128)(2,1)S(1)}, bf16[768,256]{1,0:T(8,128)(2,1)}, u32[]{:S(2)}) copy-start(bf16[768,256]{1,0:T(8,128)(2,1)} %constant.19.clone.refs_2_) | copy-start | bytes 1179652
  13.6 40.2 %copy-start.2 = (bf16[256,576]{1,0:T(8,128)(2,1)S(1)}, bf16[256,576]{1,0:T(8,128)(2,1)}, u32[]{:S(2)}) copy-start(bf16[256,576]{1,0:T(8,128)(2,1)} %constant.22.clone.refs_5_) | copy-start | bytes 884740
  13.6 40.2 %copy-start.3 = (bf16[576,256]{1,0:T(8,128)(2,1)S(1)}, bf16[576,256]{1,0:T(8,128)(2,1)}, u32[]{:S(2)}) copy-start(bf16[576,256]{1,0:T(8,128)(2,1)} %constant.20.clone.refs_3_) | copy-start | bytes 884740
  13.6 40.2 %copy-start.4 = (bf16[2,256,256]{2,1,0:T(8,128)(2,1)S(1)}, bf16[2,256,256]{2,1,0:T(8,128)(2,1)}, u32[]{:S(2)}) copy-start(bf16[2,256,256]{2,1,0:T(8,128)(2,1)} %constant.18.clone.refs_1_) | copy-start | bytes 786436
  34.5 1.0 %copy-start.5 = (bf16[2,256,256]{2,1,0:T(8,128)(2,1)S(1)}, bf16[2,256,256]{2,1,0:T(8,128)(2,1)}, u32[]{:S(2)}) copy-start(bf16[2,256,256]{2,1,0:T(8,128)(2,1)} %constant.17.clone.refs_5_) | copy-start | bytes 786436

commit v7 on v6

--- a/solution.py
+++ b/solution.py
@@ -74,7 +74,7 @@
 
 
 def compress_kernel(
-    shape, raw_hbm, filter_hbm, out_hbm, raw_ref, filter_ref, wide_ref, out_ref, raw_sems,
+    shape, raw_hbm, filter_hbm, out_hbm, raw_ref, filter_ref, out_ref, raw_sems,
     filter_sems, out_sems,
 ):
     chunk, dates, step, targets, tiles, gates, lines = shape
@@ -111,6 +111,14 @@
             w, x, (((1,), (1,)), ((), ())), preferred_element_type=jnp.float32
         )
 
+    run = held * gates
+    row = lax.broadcasted_iota(jnp.int32, (run, run), 0)
+    col = lax.broadcasted_iota(jnp.int32, (run, run), 1)
+    within = row & (gates - 1)
+    q, r = within & (looks_rows - 1), within >> (looks_rows.bit_length() - 1)
+    order = jnp.where(col == row - within + ML_RG * q + r, 1.0, 0.0).astype(jnp.bfloat16)
+    weights = {}
+
     for first in range(0, dates, step):
         for copy in copies[2 * first : 2 * (first + step)]:
             copy.wait()
@@ -121,28 +129,26 @@
             if first == 0:
                 filter_copies[2 * group].wait()
                 filter_copies[2 * group + 1].wait()
-            weight = [
-                filter_ref[part, group * held : (group + 1) * held].reshape(held * gates, gates_in)
-                for part in (0, 1)
-            ]
+                weights[group] = [
+                    jnp.dot(
+                        order,
+                        filter_ref[part, group * held : (group + 1) * held].reshape(run, gates_in),
+                        preferred_element_type=jnp.float32,
+                    ).astype(jnp.bfloat16)
+                    for part in (0, 1)
+                ]
+            weight = weights[group]
             real = product(weight[0], raw[0]) - product(weight[1], raw[1])
             imag = product(weight[1], raw[0]) + product(weight[0], raw[1])
-            rows = slice(group * held * gates, (group + 1) * held * gates)
             for at in range(step):
-                wide_ref[first + at, 0, rows] = real[:, at * lines : (at + 1) * lines]
-                wide_ref[first + at, 1, rows] = imag[:, at * lines : (at + 1) * lines]
+                lanes = slice(at * lines, (at + 1) * lines)
+                for target in range(held):
+                    for tile in range(tiles):
+                        rows = slice(target * gates + tile * SUB, target * gates + (tile + 1) * SUB)
+                        out_ref[group * held + target, first + at, tile] = jnp.concatenate(
+                            [real[rows, lanes], imag[rows, lanes]], axis=0
+                        ).astype(jnp.bfloat16)
         for date in range(first, first + step):
-            for target in range(targets):
-                for tile in range(tiles):
-                    rows = []
-                    for part in (0, 1):
-                        begin, count = tile * SUB, min(looks_rows, SUB)
-                        for at in range(begin, begin + SUB, count):
-                            gate = target * gates + at // looks_rows + ML_RG * (at % looks_rows)
-                            rows.append(wide_ref[date, part, pl.ds(gate, count, stride=ML_RG), :])
-                    out_ref[target, date, tile] = jnp.concatenate(rows, axis=0).astype(
-                        jnp.bfloat16
-                    )
             out_copies[date].start()
     for copy in out_copies:
         copy.wait()
@@ -163,7 +169,6 @@
         scratch_shapes=[
             pltpu.VMEM(raw_echo.shape, jnp.bfloat16),
             pltpu.VMEM((2, targets, gates, gates_in), jnp.bfloat16),
-            pltpu.VMEM((dates, 2, targets * gates, lines), jnp.float32),
             pltpu.VMEM((targets, dates, tiles, 2 * SUB, lines), jnp.bfloat16),
             pltpu.SemaphoreType.DMA((dates, 2)),
             pltpu.SemaphoreType.DMA((2, 2)),
@@ -180,12 +185,15 @@
 
 
 def focus_kernel(
-    shape, offset_ref, data_ref, cos_ref, sin_ref, turn_ref, table_ref, out_ref, image_ref, look_ref,
+    shape, offset_ref, data_ref, cos_ref, sin_ref, turn_ref, table_hbm, out_ref, image_ref, look_ref,
+    row_ref, table_ref, table_sem,
 ):
     chunk, dates, blocks, tiles, gates, lines = shape
     looks_rows = gates // ML_RG
     look_lines = lines // ML_AZ
     count = blocks * SUB
+    table_copy = pltpu.make_async_copy(table_hbm, table_ref, table_sem)
+    table_copy.start()
     for date in range(dates):
         rows = []
         for tile in range(tiles):
@@ -196,8 +204,10 @@
             for a, (re, im) in enumerate(small_dft(parts, -1)):
                 tr, ti = turn_ref[0, a : a + 1], turn_ref[1, a : a + 1]
                 rows.append(jnp.concatenate([re * tr - im * ti, re * ti + im * tr], axis=1))
-        rows = jnp.concatenate(rows, axis=0).astype(jnp.bfloat16)
-        spectrum = jnp.dot(rows, table_ref[0], preferred_element_type=jnp.float32)
+        row_ref[date] = jnp.concatenate(rows, axis=0).astype(jnp.bfloat16)
+    table_copy.wait()
+    for date in range(dates):
+        spectrum = jnp.dot(row_ref[date], table_ref[0], preferred_element_type=jnp.float32)
         rows = []
         for tile in range(tiles):
             re = spectrum[tile * count : (tile + 1) * count, :lines]
@@ -296,11 +306,16 @@
     return pl.pallas_call(
         lambda *refs: focus_kernel(shape, *refs),
         out_shape=jax.ShapeDtypeStruct((blocks, slots * looks_rows, lines), jnp.bfloat16),
-        in_specs=[pl.BlockSpec(memory_space=pltpu.SMEM)] + [whole] * 5,
+        in_specs=[pl.BlockSpec(memory_space=pltpu.SMEM)]
+        + [whole] * 4
+        + [pl.BlockSpec(memory_space=pltpu.HBM)],
         out_specs=whole,
         scratch_shapes=[
             pltpu.VMEM((dates, tiles, blocks, 2, SUB, lines), jnp.float32),
             pltpu.VMEM((blocks, slots * looks_rows, lines), jnp.float32),
+            pltpu.VMEM((dates, tiles * blocks * SUB, 2 * lines), jnp.bfloat16),
+            pltpu.VMEM(tables[1].shape, jnp.bfloat16),
+            pltpu.SemaphoreType.DMA,
         ],
         compiler_params=pltpu.CompilerParams(vmem_limit_bytes=VMEM_BYTES),
         cost_estimate=pl.CostEstimate(
@@ -309,7 +324,13 @@
             transcendentals=0,
         ),
         name="focus",
-    )(pair_offset, columns, *phases, *tables)
+    )(
+        pair_offset,
+        columns,
+        *phases,
+        tables[0],
+        pltpu.with_memory_space_constraint(tables[1], pltpu.HBM),
+    )
 
 
 def tri_window(offset):

time: 56.5 us -> 56.4 us (level)
  local copies, waits for them, and re-layouts: 4.97 us -> 4.02 us
  Pallas kernels: 9.16 us -> 10 us
    unnamed x20 -> x18, local copies, waits for them, and re-layouts: 1 us -> 0.05 us
where the time goes in v7:
time: 56.4 us; the launch traced here: 56.1 us
  waiting for transfers between devices  18.9 us (34%)
  blocking collectives  15.7 us (28%)
  Pallas kernels  10 us (18%)
  starting transfers between devices  7.39 us (13%)
  local copies, waits for them, and re-layouts  4.02 us (7%)
    all_to_all x1, waiting for transfers between devices, exchange(): lax.all_to_all(blocks, 'lines', split_axis=0, concat_axis=0, tiled=True)  18.9 us
    all_to_all x1, blocking collectives, exchange(): lax.all_to_all(blocks, 'lines', split_axis=0, concat_axis=0, tiled=True)  15.7 us
    all_to_all x1, starting transfers between devices, exchange(): lax.all_to_all(blocks, 'lines', split_axis=0, concat_axis=0, tiled=True)  7.39 us
    pallas_call x1, Pallas kernels, compress(): pl.pallas_call(lambda *refs: compress_kernel(shape, *refs), out_shape=jax...  4.43 us
    pallas_call x1, Pallas kernels, focus(): pl.pallas_call(lambda *refs: focus_kernel(shape, *refs), out_shape=jax.Sh...  3.16 us
    pallas_call x1, Pallas kernels, goldstein(): pl.pallas_call(lambda *refs: goldstein_kernel(shape, *refs), out_shape=ja...  2.41 us
    sin x1, local copies, waits for them, and re-layouts, phase_tables(): return (jnp.cos(phase), jnp.sin(phase))  1.99 us
    another operation x1, local copies, waits for them, and re-layouts, phase_tables(): phase.transpose(0, 1, 3, 2, 4).reshape(chunks, tiles, blocks * SUB, lines)  1.28 us
  transfers between devices with their start and end apart: 1, of which 1 were waited for; matrix products, arithmetic and copies ran while one was open for 7% of the time, Pallas kernels for 0%

profile of v7, /device:TPU:0, one launch (start us, length us, event | category | flops | bytes accessed | tf_op | source)
XLA Modules:
  0.0 56.1 jit_solution(14922299655968708311)
XLA Ops:
  0.0 0.0 copy-start.8
  0.0 4.4 %compress.1 = bf16[16,4,4,16,128]{4,3,2,1,0:T(8,128)(2,1)} custom-call(bf16[4,2,128,512]{3,2,1,0:T(8,128)(2,1)} %refs_0_.2, bf16[2,16,1,32,512]{4,3,2,1,0:T(8,128)(2,1)} %bitcast.6), custom_call_target="tpu_custom_call" | custom-call | flops 1073741824 | bytes 3145728 | tf_op jit(solution)/shard_map/compress/pallas_call | solution.py:164
  4.4 7.4 %all-to-all-start = ((bf16[16,4,4,16,128]{4,3,2,1,0:T(8,128)(2,1)}), bf16[16,4,4,16,128]{4,3,2,1,0:T(8,128)(2,1)S(1)}, u32[]{:S(2)}, u32[]{:S(2)}) async-start(bf16[16,4,4,16,128]{4,3,2,1,0:T(8,128)(2,1)} %compress.1), calls=%async_computation | async-start | bytes 2097152 | tf_op jit(solution)/shard_map/all_to_all | solution.py:533
  11.8 0.0 copy-done.8
  11.8 0.7 %reshape.10 = f32[1,8,4,128,16]{4,3,2,1,0:T(8,128)S(1)} reshape(f32[32,2048]{1,0:T(8,128)S(1)} %copy-done.8) | data formatting | bytes 524288 | tf_op jit(solution)/shard_map/reshape | solution.py:281
  12.6 0.0 copy-start.6
  12.6 0.0 copy-start.7
  12.6 1.3 %copy.14 = f32[1,4,16,8,128]{4,3,2,1,0:T(8,128)} copy(f32[1,4,16,8,128]{2,4,1,3,0:T(8,128)S(1)} %bitcast.4) | data formatting | bytes 524288 | tf_op jit(solution)/shard_map/transpose;transpose | solution.py:283
  13.9 0.0 copy-start.1
  13.9 0.0 copy-start.4
  13.9 0.0 copy-start.5
  13.9 2.0 %fusion = (f32[1,4,128,128]{3,2,1,0:T(8,128)S(1)}, f32[1,4,128,128]{3,2,1,0:T(8,128)S(1)}) fusion(f32[1,4,128,128]{3,2,1,0:T(8,128)} %bitcast.5), kind=kLoop, calls=%fused_computation | loop fusion | bytes 786432 | tf_op jit(solution)/shard_map/sin | solution.py:285
  15.9 18.9 %all-to-all-done.refs_1_ = bf16[16,4,4,16,128]{4,3,2,1,0:T(8,128)(2,1)S(1)} async-done(((bf16[16,4,4,16,128]{4,3,2,1,0:T(8,128)(2,1)}), bf16[16,4,4,16,128]{4,3,2,1,0:T(8,128)(2,1)S(1)}, u32[]{:S(2)}, u32[]{:S(2)}) %all-to-all-start) | async-done | bytes 1048608 | tf_op jit(solution)/shard_map/all_to_all | solution.py:533
  34.8 0.0 copy-done.6
  34.8 0.0 copy-done.7
  34.8 3.2 %focus.1 = bf16[16,48,128]{2,1,0:T(8,128)(2,1)S(1)} custom-call(s32[4]{0:T(128)S(1)} %copy-done.7, bf16[16,4,4,16,128]{4,3,2,1,0:T(8,128)(2,1)S(1)} %all-to-all-done.refs_1_, f32[1,4,128,128]{3,2,1,0:T(8,128)S(1)} %get-tuple-element.6.refs_2_, f32[1,4,128,128]{3,2,1,0:T(8,128)S(1)} %get-tuple-element.5.refs_3_, f32[4,16,128]{2,1,0:T(8,128)S(1)} %copy-done.6, ...), custom_call_target="tpu_custom_call" | custom-call | flops 536870912 | bytes 2097152 | tf_op jit(solution)/shard_map/focus/pallas_call | solution.py:306
  38.0 15.7 %all_to_all.10.refs_0_ = bf16[16,48,128]{2,1,0:T(8,128)(2,1)S(1)} all-to-all(bf16[16,48,128]{2,1,0:T(8,128)(2,1)S(1)} %focus.1), channel_id=1, replica_groups=mesh['groups'=2,'lines'=16] {'lines'}, dimensions={0} | all-to-all | bytes 393216 | tf_op jit(solution)/shard_map/all_to_all | solution.py:533
  53.6 0.0 copy-done
  53.6 0.0 copy-done.1
  53.6 0.0 copy-done.2
  53.6 0.0 copy-done.3
  53.6 0.0 copy-done.4
  53.7 0.0 copy-done.5
  53.7 2.4 %goldstein.1 = f32[4,2,64,128]{3,2,1,0:T(8,128)} custom-call(bf16[16,48,128]{2,1,0:T(8,128)(2,1)S(1)} %all_to_all.10.refs_0_, bf16[2,256,256]{2,1,0:T(8,128)(2,1)S(1)} %copy-done.4, bf16[768,256]{1,0:T(8,128)(2,1)S(1)} %copy-done.1, bf16[576,256]{1,0:T(8,128)(2,1)S(1)} %copy-done.3, bf16[128,256]{1,0:T(8,128)(2,1)S(1)} %copy-done.5, ...), custom_call_target="tpu_custom_call" | custom-call | tf_op jit(solution)/shard_map/goldstein/pallas_call | solution.py:508
  (3 shorter events, 0.0 us)
Async XLA Ops:
  0.0 11.8 %copy-start.8 = (f32[32,2048]{1,0:T(8,128)S(1)}, f32[32,2048]{1,0:T(8,128)}, u32[]{:S(2)}) copy-start(f32[32,2048]{1,0:T(8,128)} %param.14) | copy-start | bytes 786436
  4.4 30.3 %all-to-all-start = ((bf16[16,4,4,16,128]{4,3,2,1,0:T(8,128)(2,1)}), bf16[16,4,4,16,128]{4,3,2,1,0:T(8,128)(2,1)S(1)}, u32[]{:S(2)}, u32[]{:S(2)}) async-start(bf16[16,4,4,16,128]{4,3,2,1,0:T(8,128)(2,1)} %compress.1), calls=%async_computation | async-start | bytes 2097152 | tf_op jit(solution)/shard_map/all_to_all | solution.py:533
  12.6 22.2 %copy-start.6 = (f32[4,16,128]{2,1,0:T(8,128)S(1)}, f32[4,16,128]{2,1,0:T(8,128)}, u32[]{:S(2)}) copy-start(f32[4,16,128]{2,1,0:T(8,128)} %constant.16.clone.refs_4_) | copy-start | bytes 98308
  12.6 22.2 %copy-start.7 = (s32[4]{0:T(128)S(1)}, s32[4]{0:T(128)}, u32[]{:S(2)}) copy-start(s32[4]{0:T(128)} %refs_0_.3) | copy-start | bytes 52
  13.9 39.8 %copy-start = (bf16[4,128,512]{2,1,0:T(8,128)(2,1)S(1)}, bf16[4,128,512]{2,1,0:T(8,128)(2,1)}, u32[]{:S(2)}) copy-start(bf16[4,128,512]{2,1,0:T(8,128)(2,1)} %constant.23.clone.refs_6_) | copy-start | bytes 1572868
  13.9 39.8 %copy-start.1 = (bf16[768,256]{1,0:T(8,128)(2,1)S(1)}, bf16[768,256]{1,0:T(8,128)(2,1)}, u32[]{:S(2)}) copy-start(bf16[768,256]{1,0:T(8,128)(2,1)} %constant.19.clone.refs_2_) | copy-start | bytes 1179652
  13.9 39.8 %copy-start.2 = (bf16[256,576]{1,0:T(8,128)(2,1)S(1)}, bf16[256,576]{1,0:T(8,128)(2,1)}, u32[]{:S(2)}) copy-start(bf16[256,576]{1,0:T(8,128)(2,1)} %constant.22.clone.refs_5_) | copy-start | bytes 884740
  13.9 39.8 %copy-start.3 = (bf16[576,256]{1,0:T(8,128)(2,1)S(1)}, bf16[576,256]{1,0:T(8,128)(2,1)}, u32[]{:S(2)}) copy-start(bf16[576,256]{1,0:T(8,128)(2,1)} %constant.20.clone.refs_3_) | copy-start | bytes 884740
  13.9 39.8 %copy-start.4 = (bf16[2,256,256]{2,1,0:T(8,128)(2,1)S(1)}, bf16[2,256,256]{2,1,0:T(8,128)(2,1)}, u32[]{:S(2)}) copy-start(bf16[2,256,256]{2,1,0:T(8,128)(2,1)} %constant.18.clone.refs_1_) | copy-start | bytes 786436
  13.9 39.8 %copy-start.5 = (bf16[128,256]{1,0:T(8,128)(2,1)S(1)}, bf16[128,256]{1,0:T(8,128)(2,1)}, u32[]{:S(2)}) copy-start(bf16[128,256]{1,0:T(8,128)(2,1)} %constant.21.clone.refs_4_) | copy-start | bytes 196612

commit v8 on v6

--- a/solution.py
+++ b/solution.py
@@ -96,7 +96,7 @@
     filter_copies = [
         pltpu.make_async_copy(
             filter_hbm.at[side, pl.ds(part * held, held), chunk],
-            filter_ref.at[side, pl.ds(part * held, held)],
+            filter_ref.at[part, side],
             filter_sems.at[part, side],
         )
         for part in range(parts)
@@ -111,6 +111,7 @@
             w, x, (((1,), (1,)), ((), ())), preferred_element_type=jnp.float32
         )
 
+    run = held * gates
     for first in range(0, dates, step):
         for copy in copies[2 * first : 2 * (first + step)]:
             copy.wait()
@@ -121,13 +122,11 @@
             if first == 0:
                 filter_copies[2 * group].wait()
                 filter_copies[2 * group + 1].wait()
-            weight = [
-                filter_ref[part, group * held : (group + 1) * held].reshape(held * gates, gates_in)
-                for part in (0, 1)
-            ]
-            real = product(weight[0], raw[0]) - product(weight[1], raw[1])
-            imag = product(weight[1], raw[0]) + product(weight[0], raw[1])
-            rows = slice(group * held * gates, (group + 1) * held * gates)
+            both = filter_ref[group].reshape(2 * run, gates_in)
+            by_real, by_imag = product(both, raw[0]), product(both, raw[1])
+            real = by_real[:run] - by_imag[run:]
+            imag = by_real[run:] + by_imag[:run]
+            rows = slice(group * run, (group + 1) * run)
             for at in range(step):
                 wide_ref[first + at, 0, rows] = real[:, at * lines : (at + 1) * lines]
                 wide_ref[first + at, 1, rows] = imag[:, at * lines : (at + 1) * lines]
@@ -162,7 +161,7 @@
         out_specs=pl.BlockSpec(memory_space=pl.ANY),
         scratch_shapes=[
             pltpu.VMEM(raw_echo.shape, jnp.bfloat16),
-            pltpu.VMEM((2, targets, gates, gates_in), jnp.bfloat16),
+            pltpu.VMEM((2, 2, targets // 2, gates, gates_in), jnp.bfloat16),
             pltpu.VMEM((dates, 2, targets * gates, lines), jnp.float32),
             pltpu.VMEM((targets, dates, tiles, 2 * SUB, lines), jnp.bfloat16),
             pltpu.SemaphoreType.DMA((dates, 2)),
@@ -180,12 +179,15 @@
 
 
 def focus_kernel(
-    shape, offset_ref, data_ref, cos_ref, sin_ref, turn_ref, table_ref, out_ref, image_ref, look_ref,
+    shape, offset_ref, data_ref, cos_ref, sin_ref, turn_ref, table_hbm, out_ref, image_ref, look_ref,
+    row_ref, table_ref, table_sem,
 ):
     chunk, dates, blocks, tiles, gates, lines = shape
     looks_rows = gates // ML_RG
     look_lines = lines // ML_AZ
     count = blocks * SUB
+    table_copy = pltpu.make_async_copy(table_hbm, table_ref, table_sem)
+    table_copy.start()
     for date in range(dates):
         rows = []
         for tile in range(tiles):
@@ -196,8 +198,10 @@
             for a, (re, im) in enumerate(small_dft(parts, -1)):
                 tr, ti = turn_ref[0, a : a + 1], turn_ref[1, a : a + 1]
                 rows.append(jnp.concatenate([re * tr - im * ti, re * ti + im * tr], axis=1))
-        rows = jnp.concatenate(rows, axis=0).astype(jnp.bfloat16)
-        spectrum = jnp.dot(rows, table_ref[0], preferred_element_type=jnp.float32)
+        row_ref[date] = jnp.concatenate(rows, axis=0).astype(jnp.bfloat16)
+    table_copy.wait()
+    for date in range(dates):
+        spectrum = jnp.dot(row_ref[date], table_ref[0], preferred_element_type=jnp.float32)
         rows = []
         for tile in range(tiles):
             re = spectrum[tile * count : (tile + 1) * count, :lines]
@@ -296,11 +300,16 @@
     return pl.pallas_call(
         lambda *refs: focus_kernel(shape, *refs),
         out_shape=jax.ShapeDtypeStruct((blocks, slots * looks_rows, lines), jnp.bfloat16),
-        in_specs=[pl.BlockSpec(memory_space=pltpu.SMEM)] + [whole] * 5,
+        in_specs=[pl.BlockSpec(memory_space=pltpu.SMEM)]
+        + [whole] * 4
+        + [pl.BlockSpec(memory_space=pltpu.HBM)],
         out_specs=whole,
         scratch_shapes=[
             pltpu.VMEM((dates, tiles, blocks, 2, SUB, lines), jnp.float32),
             pltpu.VMEM((blocks, slots * looks_rows, lines), jnp.float32),
+            pltpu.VMEM((dates, tiles * blocks * SUB, 2 * lines), jnp.bfloat16),
+            pltpu.VMEM(tables[1].shape, jnp.bfloat16),
+            pltpu.SemaphoreType.DMA,
         ],
         compiler_params=pltpu.CompilerParams(vmem_limit_bytes=VMEM_BYTES),
         cost_estimate=pl.CostEstimate(
@@ -309,7 +318,13 @@
             transcendentals=0,
         ),
         name="focus",
-    )(pair_offset, columns, *phases, *tables)
+    )(
+        pair_offset,
+        columns,
+        *phases,
+        tables[0],
+        pltpu.with_memory_space_constraint(tables[1], pltpu.HBM),
+    )
 
 
 def tri_window(offset):

time: 56.5 us -> 56.5 us (level)
  Pallas kernels: 9.16 us -> 10.2 us
  local copies, waits for them, and re-layouts: 4.97 us -> 4.02 us
    unnamed x20 -> x18, local copies, waits for them, and re-layouts: 1 us -> 0.05 us
where the time goes in v8:
time: 56.5 us; the launch traced here: 56.2 us
  waiting for transfers between devices  18.9 us (33%)
  blocking collectives  15.7 us (28%)
  Pallas kernels  10.2 us (18%)
  starting transfers between devices  7.39 us (13%)
  local copies, waits for them, and re-layouts  4.02 us (7%)
    all_to_all x1, waiting for transfers between devices, exchange(): lax.all_to_all(blocks, 'lines', split_axis=0, concat_axis=0, tiled=True)  18.9 us
    all_to_all x1, blocking collectives, exchange(): lax.all_to_all(blocks, 'lines', split_axis=0, concat_axis=0, tiled=True)  15.7 us
    all_to_all x1, starting transfers between devices, exchange(): lax.all_to_all(blocks, 'lines', split_axis=0, concat_axis=0, tiled=True)  7.39 us
    pallas_call x1, Pallas kernels, compress(): pl.pallas_call(lambda *refs: compress_kernel(shape, *refs), out_shape=jax...  4.59 us
    pallas_call x1, Pallas kernels, focus(): pl.pallas_call(lambda *refs: focus_kernel(shape, *refs), out_shape=jax.Sh...  3.17 us
    pallas_call x1, Pallas kernels, goldstein(): pl.pallas_call(lambda *refs: goldstein_kernel(shape, *refs), out_shape=ja...  2.41 us
    sin x1, local copies, waits for them, and re-layouts, phase_tables(): return (jnp.cos(phase), jnp.sin(phase))  1.99 us
    another operation x1, local copies, waits for them, and re-layouts, phase_tables(): phase.transpose(0, 1, 3, 2, 4).reshape(chunks, tiles, blocks * SUB, lines)  1.28 us
  transfers between devices with their start and end apart: 1, of which 1 were waited for; matrix products, arithmetic and copies ran while one was open for 7% of the time, Pallas kernels for 0%

profile of v8, /device:TPU:0, one launch (start us, length us, event | category | flops | bytes accessed | tf_op | source)
XLA Modules:
  0.0 56.2 jit_solution(867327124646510916)
XLA Ops:
  0.0 0.0 copy-start.8
  0.0 4.6 %compress.1 = bf16[16,4,4,16,128]{4,3,2,1,0:T(8,128)(2,1)} custom-call(bf16[4,2,128,512]{3,2,1,0:T(8,128)(2,1)} %refs_0_.2, bf16[2,16,1,32,512]{4,3,2,1,0:T(8,128)(2,1)} %bitcast.6), custom_call_target="tpu_custom_call" | custom-call | flops 1073741824 | bytes 3145728 | tf_op jit(solution)/shard_map/compress/pallas_call | solution.py:157
  4.6 7.4 %all-to-all-start = ((bf16[16,4,4,16,128]{4,3,2,1,0:T(8,128)(2,1)}), bf16[16,4,4,16,128]{4,3,2,1,0:T(8,128)(2,1)S(1)}, u32[]{:S(2)}, u32[]{:S(2)}) async-start(bf16[16,4,4,16,128]{4,3,2,1,0:T(8,128)(2,1)} %compress.1), calls=%async_computation | async-start | bytes 2097152 | tf_op jit(solution)/shard_map/all_to_all | solution.py:527
  12.0 0.0 copy-done.8
  12.0 0.7 %reshape.10 = f32[1,8,4,128,16]{4,3,2,1,0:T(8,128)S(1)} reshape(f32[32,2048]{1,0:T(8,128)S(1)} %copy-done.8) | data formatting | bytes 524288 | tf_op jit(solution)/shard_map/reshape | solution.py:275
  12.7 0.0 copy-start.6
  12.7 0.0 copy-start.7
  12.7 1.3 %copy.14 = f32[1,4,16,8,128]{4,3,2,1,0:T(8,128)} copy(f32[1,4,16,8,128]{2,4,1,3,0:T(8,128)S(1)} %bitcast.4) | data formatting | bytes 524288 | tf_op jit(solution)/shard_map/transpose;transpose | solution.py:277
  14.0 0.0 copy-start
  14.0 0.0 copy-start.4
  14.1 0.0 copy-start.5
  14.1 2.0 %fusion = (f32[1,4,128,128]{3,2,1,0:T(8,128)S(1)}, f32[1,4,128,128]{3,2,1,0:T(8,128)S(1)}) fusion(f32[1,4,128,128]{3,2,1,0:T(8,128)} %bitcast.5), kind=kLoop, calls=%fused_computation | loop fusion | bytes 786432 | tf_op jit(solution)/shard_map/sin | solution.py:279
  16.1 18.9 %all-to-all-done.refs_1_ = bf16[16,4,4,16,128]{4,3,2,1,0:T(8,128)(2,1)S(1)} async-done(((bf16[16,4,4,16,128]{4,3,2,1,0:T(8,128)(2,1)}), bf16[16,4,4,16,128]{4,3,2,1,0:T(8,128)(2,1)S(1)}, u32[]{:S(2)}, u32[]{:S(2)}) %all-to-all-start) | async-done | bytes 1048608 | tf_op jit(solution)/shard_map/all_to_all | solution.py:527
  34.9 0.0 copy-done.6
  34.9 0.0 copy-done.7
  34.9 3.2 %focus.1 = bf16[16,48,128]{2,1,0:T(8,128)(2,1)S(1)} custom-call(s32[4]{0:T(128)S(1)} %copy-done.7, bf16[16,4,4,16,128]{4,3,2,1,0:T(8,128)(2,1)S(1)} %all-to-all-done.refs_1_, f32[1,4,128,128]{3,2,1,0:T(8,128)S(1)} %get-tuple-element.6.refs_2_, f32[1,4,128,128]{3,2,1,0:T(8,128)S(1)} %get-tuple-element.5.refs_3_, f32[4,16,128]{2,1,0:T(8,128)S(1)} %copy-done.6, ...), custom_call_target="tpu_custom_call" | custom-call | flops 536870912 | bytes 2097152 | tf_op jit(solution)/shard_map/focus/pallas_call | solution.py:300
  38.1 15.7 %all_to_all.10.refs_0_ = bf16[16,48,128]{2,1,0:T(8,128)(2,1)S(1)} all-to-all(bf16[16,48,128]{2,1,0:T(8,128)(2,1)S(1)} %focus.1), channel_id=1, replica_groups=mesh['groups'=2,'lines'=16] {'lines'}, dimensions={0} | all-to-all | bytes 393216 | tf_op jit(solution)/shard_map/all_to_all | solution.py:527
  53.8 0.0 copy-done
  53.8 0.0 copy-done.1
  53.8 0.0 copy-done.2
  53.8 0.0 copy-done.3
  53.8 0.0 copy-done.4
  53.8 0.0 copy-done.5
  53.8 2.4 %goldstein.1 = f32[4,2,64,128]{3,2,1,0:T(8,128)} custom-call(bf16[16,48,128]{2,1,0:T(8,128)(2,1)S(1)} %all_to_all.10.refs_0_, bf16[2,256,256]{2,1,0:T(8,128)(2,1)S(1)} %copy-done.4, bf16[768,256]{1,0:T(8,128)(2,1)S(1)} %copy-done.1, bf16[576,256]{1,0:T(8,128)(2,1)S(1)} %copy-done.3, bf16[128,256]{1,0:T(8,128)(2,1)S(1)} %copy-done.5, ...), custom_call_target="tpu_custom_call" | custom-call | tf_op jit(solution)/shard_map/goldstein/pallas_call | solution.py:502
  (3 shorter events, 0.0 us)
Async XLA Ops:
  0.0 12.0 %copy-start.8 = (f32[32,2048]{1,0:T(8,128)S(1)}, f32[32,2048]{1,0:T(8,128)}, u32[]{:S(2)}) copy-start(f32[32,2048]{1,0:T(8,128)} %param.14) | copy-start | bytes 786436
  4.6 30.3 %all-to-all-start = ((bf16[16,4,4,16,128]{4,3,2,1,0:T(8,128)(2,1)}), bf16[16,4,4,16,128]{4,3,2,1,0:T(8,128)(2,1)S(1)}, u32[]{:S(2)}, u32[]{:S(2)}) async-start(bf16[16,4,4,16,128]{4,3,2,1,0:T(8,128)(2,1)} %compress.1), calls=%async_computation | async-start | bytes 2097152 | tf_op jit(solution)/shard_map/all_to_all | solution.py:527
  12.7 22.2 %copy-start.6 = (f32[4,16,128]{2,1,0:T(8,128)S(1)}, f32[4,16,128]{2,1,0:T(8,128)}, u32[]{:S(2)}) copy-start(f32[4,16,128]{2,1,0:T(8,128)} %constant.16.clone.refs_4_) | copy-start | bytes 98308
  12.7 22.2 %copy-start.7 = (s32[4]{0:T(128)S(1)}, s32[4]{0:T(128)}, u32[]{:S(2)}) copy-start(s32[4]{0:T(128)} %refs_0_.3) | copy-start | bytes 52
  14.0 39.8 %copy-start = (bf16[4,128,512]{2,1,0:T(8,128)(2,1)S(1)}, bf16[4,128,512]{2,1,0:T(8,128)(2,1)}, u32[]{:S(2)}) copy-start(bf16[4,128,512]{2,1,0:T(8,128)(2,1)} %constant.23.clone.refs_6_) | copy-start | bytes 1572868
  14.0 39.8 %copy-start.1 = (bf16[768,256]{1,0:T(8,128)(2,1)S(1)}, bf16[768,256]{1,0:T(8,128)(2,1)}, u32[]{:S(2)}) copy-start(bf16[768,256]{1,0:T(8,128)(2,1)} %constant.19.clone.refs_2_) | copy-start | bytes 1179652
  14.0 39.8 %copy-start.2 = (bf16[256,576]{1,0:T(8,128)(2,1)S(1)}, bf16[256,576]{1,0:T(8,128)(2,1)}, u32[]{:S(2)}) copy-start(bf16[256,576]{1,0:T(8,128)(2,1)} %constant.22.clone.refs_5_) | copy-start | bytes 884740
  14.0 39.8 %copy-start.3 = (bf16[576,256]{1,0:T(8,128)(2,1)S(1)}, bf16[576,256]{1,0:T(8,128)(2,1)}, u32[]{:S(2)}) copy-start(bf16[576,256]{1,0:T(8,128)(2,1)} %constant.20.clone.refs_3_) | copy-start | bytes 884740
  14.0 39.8 %copy-start.4 = (bf16[2,256,256]{2,1,0:T(8,128)(2,1)S(1)}, bf16[2,256,256]{2,1,0:T(8,128)(2,1)}, u32[]{:S(2)}) copy-start(bf16[2,256,256]{2,1,0:T(8,128)(2,1)} %constant.18.clone.refs_1_) | copy-start | bytes 786436
  14.1 39.8 %copy-start.5 = (bf16[128,256]{1,0:T(8,128)(2,1)S(1)}, bf16[128,256]{1,0:T(8,128)(2,1)}, u32[]{:S(2)}) copy-start(bf16[128,256]{1,0:T(8,128)(2,1)} %constant.21.clone.refs_4_) | copy-start | bytes 196612

commit v9 on v8

--- a/solution.py
+++ b/solution.py
@@ -82,10 +82,9 @@
     gates_in = raw_ref.shape[3]
     copies = [
         pltpu.make_async_copy(
-            raw_hbm.at[date, part], raw_ref.at[date, part], raw_sems.at[date, part]
+            raw_hbm.at[pl.ds(first, step)], raw_ref.at[pl.ds(first, step)], raw_sems.at[first // step]
         )
-        for date in range(dates)
-        for part in (0, 1)
+        for first in range(0, dates, step)
     ]
     out_copies = [
         pltpu.make_async_copy(out_ref.at[:, date], out_hbm.at[:, date], out_sems.at[date])
@@ -95,15 +94,13 @@
     held = targets // parts
     filter_copies = [
         pltpu.make_async_copy(
-            filter_hbm.at[side, pl.ds(part * held, held), chunk],
-            filter_ref.at[part, side],
-            filter_sems.at[part, side],
+            filter_hbm.at[:, pl.ds(part * held, held), chunk],
+            filter_ref.at[:, pl.ds(part * held, held)],
+            filter_sems.at[part],
         )
         for part in range(parts)
-        for side in (0, 1)
     ]
-    early = 2 * step
-    for copy in filter_copies[:2] + copies[:early] + filter_copies[2:] + copies[early:]:
+    for copy in [filter_copies[0], *copies[:1], *filter_copies[1:], *copies[1:]]:
         copy.start()
 
     def product(w, x):
@@ -111,22 +108,21 @@
             w, x, (((1,), (1,)), ((), ())), preferred_element_type=jnp.float32
         )
 
-    run = held * gates
     for first in range(0, dates, step):
-        for copy in copies[2 * first : 2 * (first + step)]:
-            copy.wait()
+        copies[first // step].wait()
         raw = [
             raw_ref[first : first + step, part].reshape(step * lines, gates_in) for part in (0, 1)
         ]
         for group in range(parts):
             if first == 0:
-                filter_copies[2 * group].wait()
-                filter_copies[2 * group + 1].wait()
-            both = filter_ref[group].reshape(2 * run, gates_in)
-            by_real, by_imag = product(both, raw[0]), product(both, raw[1])
-            real = by_real[:run] - by_imag[run:]
-            imag = by_real[run:] + by_imag[:run]
-            rows = slice(group * run, (group + 1) * run)
+                filter_copies[group].wait()
+            weight = [
+                filter_ref[part, group * held : (group + 1) * held].reshape(held * gates, gates_in)
+                for part in (0, 1)
+            ]
+            real = product(weight[0], raw[0]) - product(weight[1], raw[1])
+            imag = product(weight[1], raw[0]) + product(weight[0], raw[1])
+            rows = slice(group * held * gates, (group + 1) * held * gates)
             for at in range(step):
                 wide_ref[first + at, 0, rows] = real[:, at * lines : (at + 1) * lines]
                 wide_ref[first + at, 1, rows] = imag[:, at * lines : (at + 1) * lines]
@@ -161,11 +157,11 @@
         out_specs=pl.BlockSpec(memory_space=pl.ANY),
         scratch_shapes=[
             pltpu.VMEM(raw_echo.shape, jnp.bfloat16),
-            pltpu.VMEM((2, 2, targets // 2, gates, gates_in), jnp.bfloat16),
+            pltpu.VMEM((2, targets, gates, gates_in), jnp.bfloat16),
             pltpu.VMEM((dates, 2, targets * gates, lines), jnp.float32),
             pltpu.VMEM((targets, dates, tiles, 2 * SUB, lines), jnp.bfloat16),
-            pltpu.SemaphoreType.DMA((dates, 2)),
-            pltpu.SemaphoreType.DMA((2, 2)),
+            pltpu.SemaphoreType.DMA((dates // step,)),
+            pltpu.SemaphoreType.DMA((2,)),
             pltpu.SemaphoreType.DMA((dates,)),
         ],
         compiler_params=pltpu.CompilerParams(vmem_limit_bytes=VMEM_BYTES),

time: 56.5 us -> 55.9 us (0.989)
  Pallas kernels: 10.2 us -> 9.51 us
    pallas_call x1, Pallas kernels: 4.59 us -> 3.93 us  [compress(): pl.pallas_call(lambda *refs: compress_kernel(shape, *refs), out_shape=jax...]
where the time goes in v9:
time: 55.9 us; the launch traced here: 55.6 us
  waiting for transfers between devices  18.9 us (34%)
  blocking collectives  15.7 us (28%)
  Pallas kernels  9.51 us (17%)
  starting transfers between devices  7.39 us (13%)
  local copies, waits for them, and re-layouts  4.02 us (7%)
    all_to_all x1, waiting for transfers between devices, exchange(): lax.all_to_all(blocks, 'lines', split_axis=0, concat_axis=0, tiled=True)  18.9 us
    all_to_all x1, blocking collectives, exchange(): lax.all_to_all(blocks, 'lines', split_axis=0, concat_axis=0, tiled=True)  15.7 us
    all_to_all x1, starting transfers between devices, exchange(): lax.all_to_all(blocks, 'lines', split_axis=0, concat_axis=0, tiled=True)  7.39 us
    pallas_call x1, Pallas kernels, compress(): pl.pallas_call(lambda *refs: compress_kernel(shape, *refs), out_shape=jax...  3.93 us
    pallas_call x1, Pallas kernels, focus(): pl.pallas_call(lambda *refs: focus_kernel(shape, *refs), out_shape=jax.Sh...  3.17 us
    pallas_call x1, Pallas kernels, goldstein(): pl.pallas_call(lambda *refs: goldstein_kernel(shape, *refs), out_shape=ja...  2.41 us
    sin x1, local copies, waits for them, and re-layouts, phase_tables(): return (jnp.cos(phase), jnp.sin(phase))  1.99 us
    another operation x1, local copies, waits for them, and re-layouts, phase_tables(): phase.transpose(0, 1, 3, 2, 4).reshape(chunks, tiles, blocks * SUB, lines)  1.28 us
  transfers between devices with their start and end apart: 1, of which 1 were waited for; matrix products, arithmetic and copies ran while one was open for 7% of the time, Pallas kernels for 0%

profile of v9, /device:TPU:0, one launch (start us, length us, event | category | flops | bytes accessed | tf_op | source)
XLA Modules:
  0.0 55.6 jit_solution(17025297267733065212)
XLA Ops:
  0.0 0.0 copy-start.8
  0.0 3.9 %compress.1 = bf16[16,4,4,16,128]{4,3,2,1,0:T(8,128)(2,1)} custom-call(bf16[4,2,128,512]{3,2,1,0:T(8,128)(2,1)} %refs_0_.2, bf16[2,16,1,32,512]{4,3,2,1,0:T(8,128)(2,1)} %bitcast.6), custom_call_target="tpu_custom_call" | custom-call | flops 1073741824 | bytes 3145728 | tf_op jit(solution)/shard_map/compress/pallas_call | solution.py:153
  3.9 7.4 %all-to-all-start = ((bf16[16,4,4,16,128]{4,3,2,1,0:T(8,128)(2,1)}), bf16[16,4,4,16,128]{4,3,2,1,0:T(8,128)(2,1)S(1)}, u32[]{:S(2)}, u32[]{:S(2)}) async-start(bf16[16,4,4,16,128]{4,3,2,1,0:T(8,128)(2,1)} %compress.1), calls=%async_computation | async-start | bytes 2097152 | tf_op jit(solution)/shard_map/all_to_all | solution.py:523
  11.3 0.0 copy-done.8
  11.4 0.7 %reshape.10 = f32[1,8,4,128,16]{4,3,2,1,0:T(8,128)S(1)} reshape(f32[32,2048]{1,0:T(8,128)S(1)} %copy-done.8) | data formatting | bytes 524288 | tf_op jit(solution)/shard_map/reshape | solution.py:271
  12.1 0.0 copy-start.6
  12.1 0.0 copy-start.7
  12.1 1.3 %copy.14 = f32[1,4,16,8,128]{4,3,2,1,0:T(8,128)} copy(f32[1,4,16,8,128]{2,4,1,3,0:T(8,128)S(1)} %bitcast.4) | data formatting | bytes 524288 | tf_op jit(solution)/shard_map/transpose;transpose | solution.py:273
  13.4 0.0 copy-start
  13.4 0.0 copy-start.4
  13.4 0.0 copy-start.5
  13.4 2.0 %fusion = (f32[1,4,128,128]{3,2,1,0:T(8,128)S(1)}, f32[1,4,128,128]{3,2,1,0:T(8,128)S(1)}) fusion(f32[1,4,128,128]{3,2,1,0:T(8,128)} %bitcast.5), kind=kLoop, calls=%fused_computation | loop fusion | bytes 786432 | tf_op jit(solution)/shard_map/sin | solution.py:275
  15.4 18.9 %all-to-all-done.refs_1_ = bf16[16,4,4,16,128]{4,3,2,1,0:T(8,128)(2,1)S(1)} async-done(((bf16[16,4,4,16,128]{4,3,2,1,0:T(8,128)(2,1)}), bf16[16,4,4,16,128]{4,3,2,1,0:T(8,128)(2,1)S(1)}, u32[]{:S(2)}, u32[]{:S(2)}) %all-to-all-start) | async-done | bytes 1048608 | tf_op jit(solution)/shard_map/all_to_all | solution.py:523
  34.3 0.0 copy-done.6
  34.3 0.0 copy-done.7
  34.3 3.2 %focus.1 = bf16[16,48,128]{2,1,0:T(8,128)(2,1)S(1)} custom-call(s32[4]{0:T(128)S(1)} %copy-done.7, bf16[16,4,4,16,128]{4,3,2,1,0:T(8,128)(2,1)S(1)} %all-to-all-done.refs_1_, f32[1,4,128,128]{3,2,1,0:T(8,128)S(1)} %get-tuple-element.6.refs_2_, f32[1,4,128,128]{3,2,1,0:T(8,128)S(1)} %get-tuple-element.5.refs_3_, f32[4,16,128]{2,1,0:T(8,128)S(1)} %copy-done.6, ...), custom_call_target="tpu_custom_call" | custom-call | flops 536870912 | bytes 2097152 | tf_op jit(solution)/shard_map/focus/pallas_call | solution.py:296
  37.5 15.7 %all_to_all.10.refs_0_ = bf16[16,48,128]{2,1,0:T(8,128)(2,1)S(1)} all-to-all(bf16[16,48,128]{2,1,0:T(8,128)(2,1)S(1)} %focus.1), channel_id=1, replica_groups=mesh['groups'=2,'lines'=16] {'lines'}, dimensions={0} | all-to-all | bytes 393216 | tf_op jit(solution)/shard_map/all_to_all | solution.py:523
  53.1 0.0 copy-done
  53.1 0.0 copy-done.1
  53.1 0.0 copy-done.2
  53.1 0.0 copy-done.3
  53.1 0.0 copy-done.4
  53.2 0.0 copy-done.5
  53.2 2.4 %goldstein.1 = f32[4,2,64,128]{3,2,1,0:T(8,128)} custom-call(bf16[16,48,128]{2,1,0:T(8,128)(2,1)S(1)} %all_to_all.10.refs_0_, bf16[2,256,256]{2,1,0:T(8,128)(2,1)S(1)} %copy-done.4, bf16[768,256]{1,0:T(8,128)(2,1)S(1)} %copy-done.1, bf16[576,256]{1,0:T(8,128)(2,1)S(1)} %copy-done.3, bf16[128,256]{1,0:T(8,128)(2,1)S(1)} %copy-done.5, ...), custom_call_target="tpu_custom_call" | custom-call | tf_op jit(solution)/shard_map/goldstein/pallas_call | solution.py:498
  (3 shorter events, 0.0 us)
Async XLA Ops:
  0.0 11.3 %copy-start.8 = (f32[32,2048]{1,0:T(8,128)S(1)}, f32[32,2048]{1,0:T(8,128)}, u32[]{:S(2)}) copy-start(f32[32,2048]{1,0:T(8,128)} %param.14) | copy-start | bytes 786436
  3.9 30.3 %all-to-all-start = ((bf16[16,4,4,16,128]{4,3,2,1,0:T(8,128)(2,1)}), bf16[16,4,4,16,128]{4,3,2,1,0:T(8,128)(2,1)S(1)}, u32[]{:S(2)}, u32[]{:S(2)}) async-start(bf16[16,4,4,16,128]{4,3,2,1,0:T(8,128)(2,1)} %compress.1), calls=%async_computation | async-start | bytes 2097152 | tf_op jit(solution)/shard_map/all_to_all | solution.py:523
  12.1 22.2 %copy-start.6 = (f32[4,16,128]{2,1,0:T(8,128)S(1)}, f32[4,16,128]{2,1,0:T(8,128)}, u32[]{:S(2)}) copy-start(f32[4,16,128]{2,1,0:T(8,128)} %constant.16.clone.refs_4_) | copy-start | bytes 98308
  12.1 22.2 %copy-start.7 = (s32[4]{0:T(128)S(1)}, s32[4]{0:T(128)}, u32[]{:S(2)}) copy-start(s32[4]{0:T(128)} %refs_0_.3) | copy-start | bytes 52
  13.4 39.7 %copy-start = (bf16[4,128,512]{2,1,0:T(8,128)(2,1)S(1)}, bf16[4,128,512]{2,1,0:T(8,128)(2,1)}, u32[]{:S(2)}) copy-start(bf16[4,128,512]{2,1,0:T(8,128)(2,1)} %constant.23.clone.refs_6_) | copy-start | bytes 1572868
  13.4 39.7 %copy-start.1 = (bf16[768,256]{1,0:T(8,128)(2,1)S(1)}, bf16[768,256]{1,0:T(8,128)(2,1)}, u32[]{:S(2)}) copy-start(bf16[768,256]{1,0:T(8,128)(2,1)} %constant.19.clone.refs_2_) | copy-start | bytes 1179652
  13.4 39.7 %copy-start.2 = (bf16[256,576]{1,0:T(8,128)(2,1)S(1)}, bf16[256,576]{1,0:T(8,128)(2,1)}, u32[]{:S(2)}) copy-start(bf16[256,576]{1,0:T(8,128)(2,1)} %constant.22.clone.refs_5_) | copy-start | bytes 884740
  13.4 39.8 %copy-start.3 = (bf16[576,256]{1,0:T(8,128)(2,1)S(1)}, bf16[576,256]{1,0:T(8,128)(2,1)}, u32[]{:S(2)}) copy-start(bf16[576,256]{1,0:T(8,128)(2,1)} %constant.20.clone.refs_3_) | copy-start | bytes 884740
  13.4 39.8 %copy-start.4 = (bf16[2,256,256]{2,1,0:T(8,128)(2,1)S(1)}, bf16[2,256,256]{2,1,0:T(8,128)(2,1)}, u32[]{:S(2)}) copy-start(bf16[2,256,256]{2,1,0:T(8,128)(2,1)} %constant.18.clone.refs_1_) | copy-start | bytes 786436
  13.4 39.8 %copy-start.5 = (bf16[128,256]{1,0:T(8,128)(2,1)S(1)}, bf16[128,256]{1,0:T(8,128)(2,1)}, u32[]{:S(2)}) copy-start(bf16[128,256]{1,0:T(8,128)(2,1)} %constant.21.clone.refs_4_) | copy-start | bytes 196612

commit v10 on v9

--- a/solution.py
+++ b/solution.py
@@ -184,7 +184,8 @@
     count = blocks * SUB
     table_copy = pltpu.make_async_copy(table_hbm, table_ref, table_sem)
     table_copy.start()
-    for date in range(dates):
+
+    def ahead(date):
         rows = []
         for tile in range(tiles):
             parts = []
@@ -195,8 +196,14 @@
                 tr, ti = turn_ref[0, a : a + 1], turn_ref[1, a : a + 1]
                 rows.append(jnp.concatenate([re * tr - im * ti, re * ti + im * tr], axis=1))
         row_ref[date] = jnp.concatenate(rows, axis=0).astype(jnp.bfloat16)
+
+    lead = min(2, dates)
+    for date in range(lead):
+        ahead(date)
     table_copy.wait()
     for date in range(dates):
+        if date + lead < dates:
+            ahead(date + lead)
         spectrum = jnp.dot(row_ref[date], table_ref[0], preferred_element_type=jnp.float32)
         rows = []
         for tile in range(tiles):

time: 55.9 us -> 56.1 us (level)
  no operation moved by 1% of the time
where the time goes in v10:
time: 56.1 us; the launch traced here: 55.8 us
  waiting for transfers between devices  18.9 us (34%)
  blocking collectives  15.7 us (28%)
  Pallas kernels  9.76 us (17%)
  starting transfers between devices  7.39 us (13%)
  local copies, waits for them, and re-layouts  4.02 us (7%)
    all_to_all x1, waiting for transfers between devices, exchange(): lax.all_to_all(blocks, 'lines', split_axis=0, concat_axis=0, tiled=True)  18.9 us
    all_to_all x1, blocking collectives, exchange(): lax.all_to_all(blocks, 'lines', split_axis=0, concat_axis=0, tiled=True)  15.7 us
    all_to_all x1, starting transfers between devices, exchange(): lax.all_to_all(blocks, 'lines', split_axis=0, concat_axis=0, tiled=True)  7.39 us
    pallas_call x1, Pallas kernels, compress(): pl.pallas_call(lambda *refs: compress_kernel(shape, *refs), out_shape=jax...  3.93 us
    pallas_call x1, Pallas kernels, focus(): pl.pallas_call(lambda *refs: focus_kernel(shape, *refs), out_shape=jax.Sh...  3.42 us
    pallas_call x1, Pallas kernels, goldstein(): pl.pallas_call(lambda *refs: goldstein_kernel(shape, *refs), out_shape=ja...  2.41 us
    sin x1, local copies, waits for them, and re-layouts, phase_tables(): return (jnp.cos(phase), jnp.sin(phase))  1.99 us
    another operation x1, local copies, waits for them, and re-layouts, phase_tables(): phase.transpose(0, 1, 3, 2, 4).reshape(chunks, tiles, blocks * SUB, lines)  1.28 us
  transfers between devices with their start and end apart: 1, of which 1 were waited for; matrix products, arithmetic and copies ran while one was open for 7% of the time, Pallas kernels for 0%

profile of v10, /device:TPU:0, one launch (start us, length us, event | category | flops | bytes accessed | tf_op | source)
XLA Modules:
  0.0 55.8 jit_solution(13169578006883708474)
XLA Ops:
  0.0 0.0 copy-start.8
  0.0 3.9 %compress.1 = bf16[16,4,4,16,128]{4,3,2,1,0:T(8,128)(2,1)} custom-call(bf16[4,2,128,512]{3,2,1,0:T(8,128)(2,1)} %refs_0_.2, bf16[2,16,1,32,512]{4,3,2,1,0:T(8,128)(2,1)} %bitcast.6), custom_call_target="tpu_custom_call" | custom-call | flops 1073741824 | bytes 3145728 | tf_op jit(solution)/shard_map/compress/pallas_call | solution.py:153
  3.9 7.4 %all-to-all-start = ((bf16[16,4,4,16,128]{4,3,2,1,0:T(8,128)(2,1)}), bf16[16,4,4,16,128]{4,3,2,1,0:T(8,128)(2,1)S(1)}, u32[]{:S(2)}, u32[]{:S(2)}) async-start(bf16[16,4,4,16,128]{4,3,2,1,0:T(8,128)(2,1)} %compress.1), calls=%async_computation | async-start | bytes 2097152 | tf_op jit(solution)/shard_map/all_to_all | solution.py:530
  11.3 0.0 copy-done.8
  11.4 0.7 %reshape.10 = f32[1,8,4,128,16]{4,3,2,1,0:T(8,128)S(1)} reshape(f32[32,2048]{1,0:T(8,128)S(1)} %copy-done.8) | data formatting | bytes 524288 | tf_op jit(solution)/shard_map/reshape | solution.py:278
  12.1 0.0 copy-start.6
  12.1 0.0 copy-start.7
  12.1 1.3 %copy.14 = f32[1,4,16,8,128]{4,3,2,1,0:T(8,128)} copy(f32[1,4,16,8,128]{2,4,1,3,0:T(8,128)S(1)} %bitcast.4) | data formatting | bytes 524288 | tf_op jit(solution)/shard_map/transpose;transpose | solution.py:280
  13.4 0.0 copy-start
  13.4 0.0 copy-start.4
  13.4 0.0 copy-start.5
  13.4 2.0 %fusion = (f32[1,4,128,128]{3,2,1,0:T(8,128)S(1)}, f32[1,4,128,128]{3,2,1,0:T(8,128)S(1)}) fusion(f32[1,4,128,128]{3,2,1,0:T(8,128)} %bitcast.5), kind=kLoop, calls=%fused_computation | loop fusion | bytes 786432 | tf_op jit(solution)/shard_map/sin | solution.py:282
  15.4 18.9 %all-to-all-done.refs_1_ = bf16[16,4,4,16,128]{4,3,2,1,0:T(8,128)(2,1)S(1)} async-done(((bf16[16,4,4,16,128]{4,3,2,1,0:T(8,128)(2,1)}), bf16[16,4,4,16,128]{4,3,2,1,0:T(8,128)(2,1)S(1)}, u32[]{:S(2)}, u32[]{:S(2)}) %all-to-all-start) | async-done | bytes 1048608 | tf_op jit(solution)/shard_map/all_to_all | solution.py:530
  34.3 0.0 copy-done.6
  34.3 0.0 copy-done.7
  34.3 3.4 %focus.1 = bf16[16,48,128]{2,1,0:T(8,128)(2,1)S(1)} custom-call(s32[4]{0:T(128)S(1)} %copy-done.7, bf16[16,4,4,16,128]{4,3,2,1,0:T(8,128)(2,1)S(1)} %all-to-all-done.refs_1_, f32[1,4,128,128]{3,2,1,0:T(8,128)S(1)} %get-tuple-element.6.refs_2_, f32[1,4,128,128]{3,2,1,0:T(8,128)S(1)} %get-tuple-element.5.refs_3_, f32[4,16,128]{2,1,0:T(8,128)S(1)} %copy-done.6, ...), custom_call_target="tpu_custom_call" | custom-call | flops 536870912 | bytes 2097152 | tf_op jit(solution)/shard_map/focus/pallas_call | solution.py:303
  37.7 15.7 %all_to_all.10.refs_0_ = bf16[16,48,128]{2,1,0:T(8,128)(2,1)S(1)} all-to-all(bf16[16,48,128]{2,1,0:T(8,128)(2,1)S(1)} %focus.1), channel_id=1, replica_groups=mesh['groups'=2,'lines'=16] {'lines'}, dimensions={0} | all-to-all | bytes 393216 | tf_op jit(solution)/shard_map/all_to_all | solution.py:530
  53.4 0.0 copy-done
  53.4 0.0 copy-done.1
  53.4 0.0 copy-done.2
  53.4 0.0 copy-done.3
  53.4 0.0 copy-done.4
  53.4 0.0 copy-done.5
  53.4 2.4 %goldstein.1 = f32[4,2,64,128]{3,2,1,0:T(8,128)} custom-call(bf16[16,48,128]{2,1,0:T(8,128)(2,1)S(1)} %all_to_all.10.refs_0_, bf16[2,256,256]{2,1,0:T(8,128)(2,1)S(1)} %copy-done.4, bf16[768,256]{1,0:T(8,128)(2,1)S(1)} %copy-done.1, bf16[576,256]{1,0:T(8,128)(2,1)S(1)} %copy-done.3, bf16[128,256]{1,0:T(8,128)(2,1)S(1)} %copy-done.5, ...), custom_call_target="tpu_custom_call" | custom-call | tf_op jit(solution)/shard_map/goldstein/pallas_call | solution.py:505
  (3 shorter events, 0.0 us)
Async XLA Ops:
  0.0 11.3 %copy-start.8 = (f32[32,2048]{1,0:T(8,128)S(1)}, f32[32,2048]{1,0:T(8,128)}, u32[]{:S(2)}) copy-start(f32[32,2048]{1,0:T(8,128)} %param.14) | copy-start | bytes 786436
  3.9 30.3 %all-to-all-start = ((bf16[16,4,4,16,128]{4,3,2,1,0:T(8,128)(2,1)}), bf16[16,4,4,16,128]{4,3,2,1,0:T(8,128)(2,1)S(1)}, u32[]{:S(2)}, u32[]{:S(2)}) async-start(bf16[16,4,4,16,128]{4,3,2,1,0:T(8,128)(2,1)} %compress.1), calls=%async_computation | async-start | bytes 2097152 | tf_op jit(solution)/shard_map/all_to_all | solution.py:530
  12.1 22.2 %copy-start.6 = (f32[4,16,128]{2,1,0:T(8,128)S(1)}, f32[4,16,128]{2,1,0:T(8,128)}, u32[]{:S(2)}) copy-start(f32[4,16,128]{2,1,0:T(8,128)} %constant.16.clone.refs_4_) | copy-start | bytes 98308
  12.1 22.2 %copy-start.7 = (s32[4]{0:T(128)S(1)}, s32[4]{0:T(128)}, u32[]{:S(2)}) copy-start(s32[4]{0:T(128)} %refs_0_.3) | copy-start | bytes 52
  13.4 40.0 %copy-start = (bf16[4,128,512]{2,1,0:T(8,128)(2,1)S(1)}, bf16[4,128,512]{2,1,0:T(8,128)(2,1)}, u32[]{:S(2)}) copy-start(bf16[4,128,512]{2,1,0:T(8,128)(2,1)} %constant.23.clone.refs_6_) | copy-start | bytes 1572868
  13.4 40.0 %copy-start.1 = (bf16[768,256]{1,0:T(8,128)(2,1)S(1)}, bf16[768,256]{1,0:T(8,128)(2,1)}, u32[]{:S(2)}) copy-start(bf16[768,256]{1,0:T(8,128)(2,1)} %constant.19.clone.refs_2_) | copy-start | bytes 1179652
  13.4 40.0 %copy-start.2 = (bf16[256,576]{1,0:T(8,128)(2,1)S(1)}, bf16[256,576]{1,0:T(8,128)(2,1)}, u32[]{:S(2)}) copy-start(bf16[256,576]{1,0:T(8,128)(2,1)} %constant.22.clone.refs_5_) | copy-start | bytes 884740
  13.4 40.0 %copy-start.3 = (bf16[576,256]{1,0:T(8,128)(2,1)S(1)}, bf16[576,256]{1,0:T(8,128)(2,1)}, u32[]{:S(2)}) copy-start(bf16[576,256]{1,0:T(8,128)(2,1)} %constant.20.clone.refs_3_) | copy-start | bytes 884740
  13.4 40.0 %copy-start.4 = (bf16[2,256,256]{2,1,0:T(8,128)(2,1)S(1)}, bf16[2,256,256]{2,1,0:T(8,128)(2,1)}, u32[]{:S(2)}) copy-start(bf16[2,256,256]{2,1,0:T(8,128)(2,1)} %constant.18.clone.refs_1_) | copy-start | bytes 786436
  13.4 40.0 %copy-start.5 = (bf16[128,256]{1,0:T(8,128)(2,1)S(1)}, bf16[128,256]{1,0:T(8,128)(2,1)}, u32[]{:S(2)}) copy-start(bf16[128,256]{1,0:T(8,128)(2,1)} %constant.21.clone.refs_4_) | copy-start | bytes 196612
